TPU v7x, 32 devices: a whole 2x2x4 slice. The times are simulated.
32 devices in a mesh: parts: 2 (over x), row: 2 (over core), col: 8 (over z, y).
Axes of the slice: x: 2, y: 2, z: 4, core: 2. Of those that a mesh axis runs over, the one named last changes fastest.
Arguments:
- points: bfloat16 [16384, 128], P(('parts', 'row', 'col')), parts along dimension 0, may hold values from -4 to 4
- vectors: bfloat16 [16384, 64], P(('parts', 'row', 'col')), parts along dimension 0, may hold values from -18 to 18
Outputs:
- smoothed: float32 [16384, 64], P(('parts', 'row', 'col')), parts along dimension 0
- log_density: float32 [16384], P(('parts', 'row', 'col')), parts along dimension 0
There are 2 independent parts, one for each index of `parts`. A program takes and returns all parts, laid end to end along the dimension named above; each array names one. Nothing has to cross between parts.
All inputs are finite; a program needn't handle non-finite values.
Results may differ from a plain program's by a relative error of at most 0.0029.
Values may be sent and summed in bfloat16 or wider, within the bound.
No kernel may reach another device: no remote copies, remote signals or barrier semaphores. Data moves between devices by JAX's collectives and lax.ppermute only.
A program may use at most 64 MiB of HBM per device.

v0:
```python
import math

import jax
import jax.numpy as jnp
from jax import lax
from jax.sharding import PartitionSpec as P


def by_blocks(piece, tile_fn):
    count = piece.shape[0]
    size = 512
    groups = piece.reshape(count // size, size, piece.shape[1])
    firsts = jnp.arange(count // size, dtype=jnp.int32) * size
    return lax.map(lambda item: tile_fn(item[0], item[1]), (groups, firsts))


def on_device(points, vectors):
    rows_dev = points.shape[0]
    feats = points.shape[1]
    n_col = lax.axis_size("col")
    n_row = lax.axis_size("row")
    half = rows_dev * n_col
    total_pts = half * n_row
    row_pos = lax.axis_index("row")
    col_pos = lax.axis_index("col")
    width = 1.05 * math.sqrt(feats)
    col_points, col_vectors = (
        lax.all_gather(points, "row", axis=0, tiled=True),
        lax.all_gather(vectors, "row", axis=0, tiled=True),
    )
    local = jnp.arange(n_row * rows_dev, dtype=jnp.int32)
    col_ids = local // rows_dev * half + col_pos * rows_dev + local % rows_dev
    col_norms = jnp.sum(col_points.astype(jnp.float32) ** 2, axis=1)
    row_base = row_pos * half

    def kernel_tile(block, first):
        norms = jnp.sum(block.astype(jnp.float32) ** 2, axis=1)
        cross = lax.dot_general(
            block, col_points, (((1,), (1,)), ((), ())), preferred_element_type=jnp.float32
        )
        dist = norms[:, None] + col_norms[None, :] - 2.0 * cross
        values = jnp.exp((2.0 * feats - dist) / width)
        rows = row_base + first + jnp.arange(block.shape[0], dtype=jnp.int32)
        return jnp.where(rows[:, None] == col_ids[None, :], jnp.zeros_like(values), values)

    sums = by_blocks(
        lax.all_gather(points, "col", axis=0, tiled=True),
        lambda block, first: jnp.sum(kernel_tile(block, first), axis=1),
    )
    row_sums = sums.reshape(-1)
    own_sums = lax.psum_scatter(row_sums, "col", scatter_dimension=0, tiled=True)
    own_density = own_sums / total_pts
    col_density = lax.all_gather(own_density, "row", axis=0, tiled=True)
    vec_cols = vectors.shape[1]

    def product_tile(block, first):
        weight = kernel_tile(block, first) / col_density[None, :]
        degree = jnp.sum(weight, axis=1)
        numer = jnp.dot(
            weight.astype(jnp.bfloat16), col_vectors, preferred_element_type=jnp.float32
        )
        return (numer, degree)

    piece = lax.all_gather(points, "col", axis=0, tiled=True)
    numer, degree = by_blocks(piece, product_tile)
    numer = numer.reshape(piece.shape[0], vec_cols)
    degree = degree.reshape(piece.shape[0])
    numer_own, degree_own = (
        lax.psum_scatter(numer, "col", scatter_dimension=0, tiled=True),
        lax.psum_scatter(degree, "col", scatter_dimension=0, tiled=True),
    )
    smoothed = numer_own / degree_own[:, None]
    return (smoothed, jnp.log(own_density))


def solution(mesh):
    placed = (P(("parts", "row", "col"), None), P(("parts", "row", "col"), None))
    return jax.shard_map(
        on_device,
        mesh=mesh,
        in_specs=placed,
        out_specs=(P(("parts", "row", "col"), None), P(("parts", "row", "col"))),
        check_vma=False,
    )
```

profile of v0, /device:TPU:0, one launch (start us, length us, event | category | flops | bytes accessed | tf_op | source)
XLA Modules:
  0.0 244.1 jit_solution(8885208843070334365)
XLA Ops:
  8.9 1.3 dynamic-slice
  10.9 2.1 all_gather.16
  12.9 2.2 all_gather.14
  15.4 37.7 %all-gather.3.cloned.1.call-done = bf16[4096,128]{1,0:T(8,128)(2,1)} async-done(((bf16[512,128]{1,0:T(8,128)(2,1)}), bf16[4096,128]{1,0:T(8,128)(2,1)}) %all-gather.3.cloned.1.call-update) | async-done | bytes 1048592 | tf_op jit(solution)/shard_map/all_gather | solution.py:64
  53.1 34.0 %while.24 = (s32[]{:T(128)}, f32[8,512]{1,0:T(8,128)S(1)}, s32[8]{0:T(128)S(1)}, s32[]{:T(128)}, bf16[8,512,128]{2,1,0:T(8,128)(2,1)}, /*index=5*/f32[1024]{0:T(...) while((s32[]{:T(128)}, f32[8,512]{1,0:T(8,128)S(1)}, s32[8]{0:T(128)S(1)}, ...), condition=%wide.region_4.5_spmd.clone, body=%wide.region_1.4_spmd.clone.sunk | while | flops 138623488 | bytes 551565 | solution.py:14
  55.4 1.8 select_reduce_fusion.2
  59.7 1.8 select_reduce_fusion.2
  63.9 1.8 select_reduce_fusion.2
  68.2 1.8 select_reduce_fusion.2
  72.4 1.8 select_reduce_fusion.2
  76.7 1.8 select_reduce_fusion.2
  80.9 1.8 select_reduce_fusion.2
  85.2 1.8 select_reduce_fusion.2
  87.1 34.9 %all-reduce = f32[4096]{0:T(1024)S(1)} all-reduce(f32[4096]{0:T(1024)S(1)} %bitcast.63), channel_id=2, replica_groups=mesh['parts'=2,'row'=2,'col'=8] {'col'}, use_global_device_ids=true, to_apply=%region_5.6.clone | all-reduce | flops 4096 | bytes 32768
  122.7 1.8 all-gather
  124.5 48.7 %while.25 = (s32[]{:T(128)}, f32[8,512,64]{1,0,2:T(8,128)S(1)}, f32[8,512]{1,0:T(8,128)S(1)}, s32[8]{0:T(128)S(1)}, s32[]{:T(128)}, /*index=5*/bf16[8,512,128]{2...) while((s32[]{:T(128)}, f32[8,512,64]{1,0,2:T(8,128)S(1)}, ...), condition=%wide.region_9.10_spmd.clone, body=%wide.region_6.9_spmd.clone.sunk | while | flops 206780928 | bytes 3439273 | solution.py:14
  126.8 1.9 fusion.52
  129.3 1.1 dynamic_update_slice.18
  132.9 1.9 fusion.52
  135.4 1.1 dynamic_update_slice.18
  139.0 1.9 fusion.52
  141.5 1.1 dynamic_update_slice.18
  145.1 1.9 fusion.52
  147.6 1.1 dynamic_update_slice.18
  151.2 1.9 fusion.52
  157.2 1.9 fusion.52
  163.3 1.9 fusion.52
  169.4 1.9 fusion.52
  173.2 1.6 copy.12
  174.8 33.0 %all-reduce.1 = f32[4096]{0:T(1024)S(1)} all-reduce(f32[4096]{0:T(1024)S(1)} %bitcast.64), channel_id=4, replica_groups=mesh['parts'=2,'row'=2,'col'=8] {'col'}, use_global_device_ids=true, to_apply=%region_11.12.clone | all-reduce | flops 4096 | bytes 32768
  207.9 27.8 %reduce-scatter.2.cloned.1.call-done = f32[512,64]{0,1:T(8,128)} async-done(((f32[4096,64]{0,1:T(8,128)}), f32[512,64]{0,1:T(8,128)}) %reduce-scatter.2.cloned.1.call-update) | async-done | bytes 131088 | tf_op jit(solution)/shard_map/reduce_scatter | solution.py:69
  235.7 1.6 broadcast_divide_fusion
  (114 shorter events, 39.7 us)
Async XLA Ops:
  7.2 45.9 %all-gather.3.cloned.1.call-start = ((), (), s32[]{:S(2)}) async-start(), calls=%async_computation.1 | async-start | bytes 1179648 | tf_op jit(solution)/shard_map/all_gather | solution.py:64
  7.9 227.8 %reduce-scatter.2.cloned.1.call-start = ((), (), s32[]{:S(2)}) async-start(), calls=%async_computation.2 | async-start | bytes 1179648 | tf_op jit(solution)/shard_map/reduce_scatter | solution.py:69
Sparse Core Ops, SparseCore 0:
  10.1 42.9 all-gather.2
  174.9 60.7 reduce-scatter.1
where the time goes:
time: 245 us; the launch traced here: 244 us
  blocking collectives  74 us (30%)
  waiting for transfers between devices  66.2 us (27%)
  matrix products  33.8 us (14%)
  local copies, waits for them, and re-layouts  24.8 us (10%)
  other arithmetic  19.5 us (8%)
  between operations  14.8 us (6%)
  loops' own time  11 us (4%)
    unnamed x2, blocking collectives  68 us
    all_gather x1, waiting for transfers between devices, on_device(): piece = lax.all_gather(points, 'col', axis=0, tiled=True)  37.7 us
    dot_general x16, matrix products, kernel_tile(): lax.dot_general(block, col_points, (((1,), (1,)), ((), ())), preferred_el...  30.2 us
    reduce_scatter x1, waiting for transfers between devices, on_device(): lax.psum_scatter(numer, 'col', scatter_dimension=0, tiled=True)  27.8 us
    reduce_sum x16, other arithmetic, kernel_tile(): norms = jnp.sum(block.astype(jnp.float32) ** 2, axis=1)  16.9 us
    dynamic_update_slice x32, local copies, waits for them, and re-layouts, by_blocks(): return lax.map(lambda item: tile_fn(item[0], item[1]), (groups, firsts))  11.1 us
    another operation x2, loops' own time, by_blocks(): return lax.map(lambda item: tile_fn(item[0], item[1]), (groups, firsts))  11 us
    dynamic_slice x16, local copies, waits for them, and re-layouts, by_blocks(): return lax.map(lambda item: tile_fn(item[0], item[1]), (groups, firsts))  9.8 us
  transfers between devices with their start and end apart: 2, of which 2 were waited for; matrix products, arithmetic and copies ran while one was open for 1% of the time, Pallas kernels for 0%

commit v1 on v0

v1 whole, which is shorter than its diff:
```python
import functools
import math

import jax
import jax.numpy as jnp
from jax import lax
from jax.experimental import pallas as pl
from jax.experimental.pallas import tpu as pltpu
from jax.sharding import PartitionSpec as P

MIB = 2**20
NT = (((1,), (1,)), ((), ()))
VMEM_SPEC = pl.BlockSpec(memory_space=pltpu.VMEM)


def by_blocks(piece, tile_fn):
    count = piece.shape[0]
    size = 512
    groups = piece.reshape(count // size, size, piece.shape[1])
    firsts = jnp.arange(count // size, dtype=jnp.int32) * size
    return lax.map(lambda item: tile_fn(item[0], item[1]), (groups, firsts))


def plain_device(points, vectors):
    rows_dev = points.shape[0]
    feats = points.shape[1]
    n_col = lax.axis_size("col")
    n_row = lax.axis_size("row")
    half = rows_dev * n_col
    total_pts = half * n_row
    row_pos = lax.axis_index("row")
    col_pos = lax.axis_index("col")
    width = 1.05 * math.sqrt(feats)
    col_points = lax.all_gather(points, "row", axis=0, tiled=True)
    col_vectors = lax.all_gather(vectors, "row", axis=0, tiled=True)
    local = jnp.arange(n_row * rows_dev, dtype=jnp.int32)
    col_ids = local // rows_dev * half + col_pos * rows_dev + local % rows_dev
    col_norms = jnp.sum(col_points.astype(jnp.float32) ** 2, axis=1)
    row_base = row_pos * half
    piece = lax.all_gather(points, "col", axis=0, tiled=True)

    def kernel_tile(block, first):
        norms = jnp.sum(block.astype(jnp.float32) ** 2, axis=1)
        cross = lax.dot_general(block, col_points, NT, preferred_element_type=jnp.float32)
        dist = norms[:, None] + col_norms[None, :] - 2.0 * cross
        values = jnp.exp((2.0 * feats - dist) / width)
        rows = row_base + first + jnp.arange(block.shape[0], dtype=jnp.int32)
        return jnp.where(rows[:, None] == col_ids[None, :], jnp.zeros_like(values), values)

    sums = by_blocks(piece, lambda block, first: jnp.sum(kernel_tile(block, first), axis=1))
    own_sums = lax.psum_scatter(sums.reshape(-1), "col", scatter_dimension=0, tiled=True)
    own_density = own_sums / total_pts
    col_density = lax.all_gather(own_density, "row", axis=0, tiled=True)

    def product_tile(block, first):
        weight = kernel_tile(block, first) / col_density[None, :]
        degree = jnp.sum(weight, axis=1)
        numer = jnp.dot(
            weight.astype(jnp.bfloat16), col_vectors, preferred_element_type=jnp.float32
        )
        return (numer, degree)

    numer, degree = by_blocks(piece, product_tile)
    numer = numer.reshape(piece.shape[0], vectors.shape[1])
    numer_own = lax.psum_scatter(numer, "col", scatter_dimension=0, tiled=True)
    degree_own = lax.psum_scatter(
        degree.reshape(-1), "col", scatter_dimension=0, tiled=True
    )
    return (numer_own / degree_own[:, None], jnp.log(own_density))


def augment(dst, base, pts, first):
    count, feats = pts.shape
    square = pts.astype(jnp.float32)
    square = square * square
    high = square.astype(jnp.bfloat16)
    low = (square - high.astype(jnp.float32)).astype(jnp.bfloat16)
    pair = jnp.concatenate([high, low], axis=1)
    norm = jnp.dot(
        pair, jnp.ones((2 * feats, 128), jnp.bfloat16), preferred_element_type=jnp.float32
    )
    q = 0.5 * feats - 0.5 * norm
    q0 = q.astype(jnp.bfloat16).astype(jnp.float32)
    rest = q - q0
    q1 = rest.astype(jnp.bfloat16).astype(jnp.float32)
    q2 = rest - q1
    lane = lax.broadcasted_iota(jnp.int32, (count, 128), 1)
    other = 3 - first
    extra = jnp.where((lane >= other) & (lane < other + 3), 1.0, 0.0)
    extra = jnp.where(lane == first + 2, q2, extra)
    extra = jnp.where(lane == first + 1, q1, extra)
    extra = jnp.where(lane == first, q0, extra)
    dst[base : base + count, 0:feats] = pts
    dst[base : base + count, feats : feats + 128] = extra.astype(jnp.bfloat16)


def kernel_body(n_rows, n_cols, unit, scale, diagonal, bm, bn, *refs):
    rows = refs[:n_rows]
    cols = refs[n_rows : n_rows + n_cols]
    k_ref, sum_ref, lhs, rhs = refs[n_rows + n_cols :]
    for u in range(n_rows):
        augment(lhs, u * unit, rows[u][...], 0)
    for u in range(n_cols):
        augment(rhs, u * unit, cols[u][...], 3)
    for c0 in range(0, n_cols * unit, bn):
        total = jnp.zeros((8, bn), jnp.float32)
        for r0 in range(0, n_rows * unit, bm):
            half_log = lax.dot_general(
                lhs[r0 : r0 + bm, :],
                rhs[c0 : c0 + bn, :],
                NT,
                preferred_element_type=jnp.float32,
            )
            value = jnp.exp2(half_log * scale)
            if (r0 // unit, c0 // unit) == diagonal:
                i = lax.broadcasted_iota(jnp.int32, (bm, bn), 0) + r0 % unit
                j = lax.broadcasted_iota(jnp.int32, (bm, bn), 1) + c0 % unit
                value = jnp.where(i == j, 0.0, value)
            k_ref[r0 : r0 + bm, c0 : c0 + bn] = value
            total = total + jnp.sum(value.reshape(bm // 8, 8, bn), axis=0)
        sum_ref[0:1, c0 : c0 + bn] = jnp.sum(total, axis=0, keepdims=True)


def kernel_tile(rows, cols, diagonal):
    unit, feats = rows[0].shape
    n_rows, n_cols = len(rows), len(cols)
    scale = 2.0 * math.log2(math.e) / (1.05 * math.sqrt(feats))
    return pl.pallas_call(
        functools.partial(kernel_body, n_rows, n_cols, unit, scale, diagonal, 256, 512),
        out_shape=(
            pltpu.VMEM((n_rows * unit, n_cols * unit), jnp.float32),
            jax.ShapeDtypeStruct((1, n_cols * unit), jnp.float32),
        ),
        in_specs=[VMEM_SPEC] * (n_rows + n_cols),
        out_specs=(VMEM_SPEC, VMEM_SPEC),
        scratch_shapes=[
            pltpu.VMEM((n_rows * unit, feats + 128), jnp.bfloat16),
            pltpu.VMEM((n_cols * unit, feats + 128), jnp.bfloat16),
        ],
        compiler_params=pltpu.CompilerParams(vmem_limit_bytes=20 * MIB),
        name="kernel_tile",
    )(*rows, *cols)


def product_body(n_cols, unit, points_all, bm, k_ref, *refs):
    sums = refs[:n_cols]
    vecs = refs[n_cols : 2 * n_cols]
    keep_ref, give_ref, log_ref, vec_all = refs[2 * n_cols :]
    width = vecs[0].shape[0]
    inverse = []
    for v in range(n_cols):
        total = sums[0][:, v * unit : (v + 1) * unit]
        for u in range(1, n_cols):
            w = v ^ u
            total = total + sums[u][:, w * unit : (w + 1) * unit]
        density = total / points_all
        if v == 0:
            log_ref[...] = jnp.log(density)
        inverse.append(1.0 / density)
        vec_all[0:width, v * unit : (v + 1) * unit] = vecs[v][...]
    inverse = jnp.concatenate(inverse, axis=1)
    ones = lax.broadcasted_iota(jnp.int32, (128 - width, n_cols * unit), 0) == 0
    vec_all[width:128, :] = jnp.where(ones, 1.0, 0.0).astype(jnp.bfloat16)
    for r0 in range(0, k_ref.shape[0], bm):
        weight = (k_ref[r0 : r0 + bm, :] * inverse).astype(jnp.bfloat16)
        numer = lax.dot_general(weight, vec_all[...], NT, preferred_element_type=jnp.float32)
        owner, at = r0 // unit, r0 % unit + r0 // (2 * unit) * unit
        if owner % 2 == 0:
            keep_ref[at : at + bm, :] = numer
        else:
            give_ref[at : at + bm, :] = numer


def product_tile(k, sums, vecs, points_all):
    n_cols = len(sums)
    unit = vecs[0].shape[1]
    shape = jax.ShapeDtypeStruct((k.shape[0] // 2, 128), jnp.float32)
    return pl.pallas_call(
        functools.partial(product_body, n_cols, unit, points_all, 256),
        out_shape=(shape, shape, jax.ShapeDtypeStruct((1, unit), jnp.float32)),
        in_specs=[VMEM_SPEC] * (1 + 2 * n_cols),
        out_specs=(VMEM_SPEC,) * 3,
        scratch_shapes=[pltpu.VMEM((128, n_cols * unit), jnp.bfloat16)],
        compiler_params=pltpu.CompilerParams(vmem_limit_bytes=16 * MIB),
        name="product_tile",
    )(k, *sums, *vecs)


def halves_body(keep_ref, got_ref, own_ref, far_ref):
    unit, height = own_ref.shape[1], own_ref.shape[0]
    own = keep_ref[0:unit, :] + got_ref[0:unit, :]
    own_ref[...] = own.T[0:height, :]
    far = keep_ref[unit:, :] + got_ref[unit:, :]
    far_ref[...] = far.T[0:height, :]


def finish_body(own_ref, far_ref, out_ref):
    width = out_ref.shape[0]
    both = own_ref[...] + far_ref[...]
    out_ref[...] = both[0:width, :] / both[width : width + 1, :]


def small_call(body, shapes, name, *args):
    return pl.pallas_call(
        body,
        out_shape=shapes,
        in_specs=[VMEM_SPEC] * len(args),
        out_specs=jax.tree.map(lambda _: VMEM_SPEC, shapes),
        compiler_params=pltpu.CompilerParams(vmem_limit_bytes=8 * MIB),
        name=name,
    )(*args)


def grid_device(points, vectors):
    n_col = lax.axis_size("col")
    unit = points.shape[0]
    width = vectors.shape[1]
    points_all = float(unit * n_col * lax.axis_size("row"))
    n_units = n_col // 2

    def across(x, mask):
        return lax.ppermute(x, "col", [(i, i ^ mask) for i in range(n_col)])

    def sibling(x):
        return lax.ppermute(x, "row", [(0, 1), (1, 0)])

    def units(x):
        held = {0: x}
        bit = n_units // 2
        while bit:
            for u in list(held):
                held[u | bit] = across(held[u], bit)
            bit //= 2
        return [held[u] for u in range(n_units)]

    far = across(points, n_units)
    cols = units(points)
    rows = [points, sibling(points), far, sibling(far)]
    vecs = units(vectors.T)
    k, sums = kernel_tile(rows, cols, (0, 0))
    all_sums = [sums] + [across(sums, u) for u in range(1, n_units)]
    keep, give, log_density = product_tile(k, all_sums, vecs, points_all)
    got = sibling(give)
    shape = jax.ShapeDtypeStruct((width + 8, unit), jnp.float32)
    own, away = small_call(halves_body, (shape, shape), "halves", keep, got)
    back = across(away, n_units)
    smoothed = small_call(
        finish_body, jax.ShapeDtypeStruct((width, unit), jnp.float32), "finish", own, back
    )
    return (smoothed.T, log_density.reshape(unit))


def solution(mesh):
    n_col = mesh.shape["col"]
    n_row = mesh.shape["row"]
    placed = (P(("parts", "row", "col"), None), P(("parts", "row", "col"), None))

    def run(points, vectors):
        unit, feats = points.shape
        paired = n_row == 2 and n_col >= 2 and n_col & (n_col - 1) == 0
        tile_bytes = 4 * (4 * unit) * (n_col // 2 * unit)
        shaped = unit % 512 == 0 and feats == 128 and vectors.shape[1] <= 120
        if paired and shaped and tile_bytes <= 16 * MIB:
            return grid_device(points, vectors)
        return plain_device(points, vectors)

    return jax.shard_map(
        run,
        mesh=mesh,
        in_specs=placed,
        out_specs=(P(("parts", "row", "col"), None), P(("parts", "row", "col"))),
        check_vma=False,
    )
```

time: 245 us -> 46.5 us (0.19)
  blocking collectives: 74 us -> 0 us
  waiting for transfers between devices: 66.2 us -> 18.8 us
  matrix products: 33.8 us -> 0 us
  local copies, waits for them, and re-layouts: 24.8 us -> 1.74 us
  other arithmetic: 19.5 us -> 0 us
  starting transfers between devices: 0.08 us -> 17.8 us
  between operations: 14.8 us -> 0.67 us
  loops' own time: 11 us -> 0 us
  Pallas kernels: 0 us -> 7.38 us
    unnamed x2 -> x0, blocking collectives: 68 us -> none
    all_gather x1 -> x0, waiting for transfers between devices: 37.7 us -> none  [on_device(): piece = lax.all_gather(points, 'col', axis=0, tiled=True)]
    dot_general x24 -> x0, matrix products: 33.8 us -> none  [the longest x16 30.2 us: kernel_tile(): lax.dot_general(block, col_points, (((1,), (1,)), ((), ())), preferred_el...]
    reduce_scatter x1 -> x0, waiting for transfers between devices: 27.8 us -> none  [on_device(): lax.psum_scatter(numer, 'col', scatter_dimension=0, tiled=True)]
    ppermute x0 -> x14, waiting for transfers between devices: none -> 18.8 us  [the longest x11 16.8 us: across(): return lax.ppermute(x, 'col', [(i, i ^ mask) for i in range(n_col)])]
    ppermute x0 -> x14, starting transfers between devices: none -> 17.8 us  [the longest x11 17.8 us: across(): return lax.ppermute(x, 'col', [(i, i ^ mask) for i in range(n_col)])]
    reduce_sum x17 -> x0, other arithmetic: 17.1 us -> none  [the longest x16 16.9 us: kernel_tile(): norms = jnp.sum(block.astype(jnp.float32) ** 2, axis=1)]
    dynamic_update_slice x32 -> x0, local copies, waits for them, and re-layouts: 11.1 us -> none  [by_blocks(): return lax.map(lambda item: tile_fn(item[0], item[1]), (groups, firsts))]
  transfers between devices with their start and end apart: 2 -> 14, of which waited for: 2 -> 8; matrix products, arithmetic and copies ran while one was open for 1% -> 0% of each run, Pallas kernels for 0% -> 8%
where the time goes in v1:
time: 46.5 us; the launch traced here: 46.4 us
  waiting for transfers between devices  18.8 us (40%)
  starting transfers between devices  17.8 us (38%)
  Pallas kernels  7.38 us (16%)
  local copies, waits for them, and re-layouts  1.74 us (4%)
  between operations  0.67 us (1%)
    ppermute x11, starting transfers between devices, across(): return lax.ppermute(x, 'col', [(i, i ^ mask) for i in range(n_col)])  17.8 us
    ppermute x11, waiting for transfers between devices, across(): return lax.ppermute(x, 'col', [(i, i ^ mask) for i in range(n_col)])  16.8 us
    pallas_call x1, Pallas kernels, kernel_tile(): pl.pallas_call(functools.partial(kernel_body, n_rows, n_cols, unit, scale...  3.74 us
    pallas_call x1, Pallas kernels, product_tile(): pl.pallas_call(functools.partial(product_body, n_cols, unit, points_all,...  2.78 us
    ppermute x3, waiting for transfers between devices, sibling(): return lax.ppermute(x, 'row', [(0, 1), (1, 0)])  1.91 us
    unnamed x4, local copies, waits for them, and re-layouts  1.74 us
  transfers between devices with their start and end apart: 14, of which 8 were waited for; matrix products, arithmetic and copies ran while one was open for 0% of the time, Pallas kernels for 8%

profile of v1, /device:TPU:0, one launch (start us, length us, event | category | flops | bytes accessed | tf_op | source)
XLA Modules:
  0.0 46.4 jit_solution(10220732238285172065)
XLA Ops:
  0.6 4.1 %collective-permute-start.1 = (bf16[512,128]{1,0:T(8,128)(2,1)}, bf16[512,128]{1,0:T(8,128)(2,1)S(1)}, u32[]{:S(2)}, u32[]{:S(2)}) collective-permute-start(bf16[512,128]{1,0:T(8,128)(2,1)} %refs_4_.1), channel_id=1, source_target_pairs={{0,4},{1,5},{2,6},{3,7},{4,0},{5,1},{6,2},{7,3},{8,12},{9,13},{10,... | collective-permute-start | bytes 393224 | tf_op jit(solution)/shard_map/ppermute | solution.py:222
  4.7 1.6 %collective-permute-start.4 = (bf16[512,128]{1,0:T(8,128)(2,1)}, bf16[512,128]{1,0:T(8,128)(2,1)S(1)}, u32[]{:S(2)}, u32[]{:S(2)}) collective-permute-start(bf16[512,128]{1,0:T(8,128)(2,1)} %refs_4_.1), channel_id=1, source_target_pairs={{0,2},{1,3},{2,0},{3,1},{4,6},{5,7},{6,4},{7,5},{8,10},{9,11},{10,... | collective-permute-start | bytes 393224 | tf_op jit(solution)/shard_map/ppermute | solution.py:222
  6.3 1.5 %collective-permute-start.3 = (bf16[512,128]{1,0:T(8,128)(2,1)}, bf16[512,128]{1,0:T(8,128)(2,1)S(1)}, u32[]{:S(2)}, u32[]{:S(2)}) collective-permute-start(bf16[512,128]{1,0:T(8,128)(2,1)} %refs_4_.1), channel_id=1, source_target_pairs={{0,1},{1,0},{2,3},{3,2},{4,5},{5,4},{6,7},{7,6},{8,9},{9,8},{10,11... | collective-permute-start | bytes 393224 | tf_op jit(solution)/shard_map/ppermute | solution.py:222
  7.8 0.0 collective-permute-start
  7.8 3.5 %collective-permute-done.1.refs_2_ = bf16[512,128]{1,0:T(8,128)(2,1)S(1)} collective-permute-done((bf16[512,128]{1,0:T(8,128)(2,1)}, bf16[512,128]{1,0:T(8,128)(2,1)S(1)}, u32[]{:S(2)}, u32[]{:S(2)}) %collective-permute-start.1) | collective-permute-done | bytes 131104 | tf_op jit(solution)/shard_map/ppermute | solution.py:222
  11.4 0.0 collective-permute-start.2
  11.4 0.2 collective-permute-done.4.refs_6_
  11.6 1.6 %collective-permute-start.5 = (bf16[512,128]{1,0:T(8,128)(2,1)S(1)}, bf16[512,128]{1,0:T(8,128)(2,1)S(1)}, u32[]{:S(2)}, u32[]{:S(2)}) collective-permute-start(bf16[512,128]{1,0:T(8,128)(2,1)S(1)} %collective-permute-done.4.refs_6_), channel_id=1, source_target_pairs={{0,1},{1,0},{2,3},{3,2},{4,5},{5,4},{6,7},{7,6},{8,9},{9,8},{10,11... | collective-permute-start | bytes 393224 | tf_op jit(solution)/shard_map/ppermute | solution.py:222
  13.1 1.4 %collective-permute-start.10 = (bf16[64,512]{1,0:T(8,128)(2,1)}, bf16[64,512]{1,0:T(8,128)(2,1)S(1)}, u32[]{:S(2)}, u32[]{:S(2)}) collective-permute-start(bf16[64,512]{1,0:T(8,128)(2,1)} %bitcast.3), channel_id=1, source_target_pairs={{0,2},{1,3},{2,0},{3,1},{4,6},{5,7},{6,4},{7,5},{8,10},{9,11},{10,... | collective-permute-start | bytes 196616 | tf_op jit(solution)/shard_map/ppermute | solution.py:222
  14.5 3.1 %collective-permute-done.10.refs_6_ = bf16[64,512]{1,0:T(8,128)(2,1)S(1)} collective-permute-done((bf16[64,512]{1,0:T(8,128)(2,1)}, bf16[64,512]{1,0:T(8,128)(2,1)S(1)}, u32[]{:S(2)}, u32[]{:S(2)}) %collective-permute-start.10) | collective-permute-done | bytes 65568 | tf_op jit(solution)/shard_map/ppermute | solution.py:222
  17.6 0.5 collective-permute-start.9
  18.1 0.0 collective-permute-done.3.refs_5_
  18.1 1.6 %collective-permute-start.11 = (bf16[64,512]{1,0:T(8,128)(2,1)S(1)}, bf16[64,512]{1,0:T(8,128)(2,1)S(1)}, u32[]{:S(2)}, u32[]{:S(2)}) collective-permute-start(bf16[64,512]{1,0:T(8,128)(2,1)S(1)} %collective-permute-done.10.refs_6_), channel_id=1, source_target_pairs={{0,1},{1,0},{2,3},{3,2},{4,5},{5,4},{6,7},{7,6},{8,9},{9,8},{10,11... | collective-permute-start | bytes 196616 | tf_op jit(solution)/shard_map/ppermute | solution.py:222
  19.6 0.0 collective-permute-done.refs_1_
  19.6 0.0 collective-permute-done.2.refs_3_
  19.7 0.9 %copy-done = bf16[512,128]{1,0:T(8,128)(2,1)S(1)} copy-done((bf16[512,128]{1,0:T(8,128)(2,1)S(1)}, bf16[512,128]{1,0:T(8,128)(2,1)}, u32[]{:S(2)}) %copy-start) | copy-done | bytes 131096
  20.6 3.7 %kernel_tile.1 = (f32[2048,2048]{1,0:T(8,128)S(1)}, f32[1,2048]{1,0:T(1,128)S(1)}) custom-call(bf16[512,128]{1,0:T(8,128)(2,1)S(1)} %copy-done, bf16[512,128]{1,0:T(8,128)(2,1)S(1)} %collective-permute-done.refs_1_, bf16[512,128]{1,0:T(8,128)(2,1)S(1)} %collective-permute-done.1.refs_2_, bf16[512,128]{1,0:T(8,128)(2,1)S(1)} %collective-permute-done.2.refs_3_, ...), custom_call_target="tpu_custom_call" | custom-call | tf_op jit(solution)/shard_map/kernel_tile/pallas_call | solution.py:128
  24.3 1.4 %collective-permute-start.8 = (f32[1,2048]{1,0:T(1,128)S(1)}, f32[1,2048]{1,0:T(1,128)S(1)}, u32[]{:S(2)}, u32[]{:S(2)}) collective-permute-start(f32[1,2048]{1,0:T(1,128)S(1)} %get-tuple-element.10.refs_0_), channel_id=1, source_target_pairs={{0,3},{1,2},{2,1},{3,0},{4,7},{5,6},{6,5},{7,4},{8,11},{9,10},{10,... | collective-permute-start | bytes 24584 | tf_op jit(solution)/shard_map/ppermute | solution.py:222
  25.7 0.6 %collective-permute-start.7 = (f32[1,2048]{1,0:T(1,128)S(1)}, f32[1,2048]{1,0:T(1,128)S(1)}, u32[]{:S(2)}, u32[]{:S(2)}) collective-permute-start(f32[1,2048]{1,0:T(1,128)S(1)} %get-tuple-element.10.refs_0_), channel_id=1, source_target_pairs={{0,2},{1,3},{2,0},{3,1},{4,6},{5,7},{6,4},{7,5},{8,10},{9,11},{10,... | collective-permute-start | bytes 24584 | tf_op jit(solution)/shard_map/ppermute | solution.py:222
  26.3 1.6 %collective-permute-start.6 = (f32[1,2048]{1,0:T(1,128)S(1)}, f32[1,2048]{1,0:T(1,128)S(1)}, u32[]{:S(2)}, u32[]{:S(2)}) collective-permute-start(f32[1,2048]{1,0:T(1,128)S(1)} %get-tuple-element.10.refs_0_), channel_id=1, source_target_pairs={{0,1},{1,0},{2,3},{3,2},{4,5},{5,4},{6,7},{7,6},{8,9},{9,8},{10,11... | collective-permute-start | bytes 24584 | tf_op jit(solution)/shard_map/ppermute | solution.py:222
  27.9 0.0 collective-permute-done.9.refs_5_
  27.9 0.0 collective-permute-done.11.refs_7_
  27.9 1.1 %collective-permute-done.8.refs_3_ = f32[1,2048]{1,0:T(1,128)S(1)} collective-permute-done((f32[1,2048]{1,0:T(1,128)S(1)}, f32[1,2048]{1,0:T(1,128)S(1)}, u32[]{:S(2)}, u32[]{:S(2)}) %collective-permute-start.8) | collective-permute-done | bytes 8224 | tf_op jit(solution)/shard_map/ppermute | solution.py:222
  28.9 0.4 collective-permute-done.7.refs_2_
  29.3 0.6 %collective-permute-done.6.refs_1_ = f32[1,2048]{1,0:T(1,128)S(1)} collective-permute-done((f32[1,2048]{1,0:T(1,128)S(1)}, f32[1,2048]{1,0:T(1,128)S(1)}, u32[]{:S(2)}, u32[]{:S(2)}) %collective-permute-start.6) | collective-permute-done | bytes 8224 | tf_op jit(solution)/shard_map/ppermute | solution.py:222
  29.9 0.8 %copy-done.1 = bf16[512,64]{0,1:T(8,128)(2,1)S(1)} copy-done((bf16[512,64]{0,1:T(8,128)(2,1)S(1)}, bf16[512,64]{0,1:T(8,128)(2,1)}, u32[]{:S(2)}) %copy-start.1) | copy-done | bytes 65560
  30.8 2.8 %product_tile.1 = (f32[1024,128]{1,0:T(8,128)S(1)}, f32[1024,128]{1,0:T(8,128)S(1)}, f32[1,512]{1,0:T(1,128)}) custom-call(f32[2048,2048]{1,0:T(8,128)S(1)} %get-tuple-element.9.k_ref, f32[1,2048]{1,0:T(1,128)S(1)} %get-tuple-element.10.refs_0_, f32[1,2048]{1,0:T(1,128)S(1)} %collective-permute-done.6.refs_1_, f32[1,2048]{1,0:T(1,128)S(1)} %collective-permute-done.7.refs_2_, ...), custom_call_target="tpu_custom_call" | custom-call | tf_op jit(solution)/shard_map/product_tile/pallas_call | solution.py:178
  33.6 1.9 %collective-permute-done.12.got_ref = f32[1024,128]{1,0:T(8,128)S(1)} collective-permute-done((f32[1024,128]{1,0:T(8,128)S(1)}, f32[1024,128]{1,0:T(8,128)S(1)}, u32[]{:S(2)}, u32[]{:S(2)}) %collective-permute-start.12) | collective-permute-done | bytes 524320 | tf_op jit(solution)/shard_map/ppermute | solution.py:225
  35.5 0.2 halves.1
  35.7 2.1 %collective-permute-start.13 = (f32[72,512]{1,0:T(8,128)S(1)}, f32[72,512]{1,0:T(8,128)S(1)}, u32[]{:S(2)}, u32[]{:S(2)}) collective-permute-start(f32[72,512]{1,0:T(8,128)S(1)} %get-tuple-element.14), channel_id=1, source_target_pairs={{0,4},{1,5},{2,6},{3,7},{4,0},{5,1},{6,2},{7,3},{8,12},{9,13},{10,... | collective-permute-start | bytes 442376 | tf_op jit(solution)/shard_map/ppermute | solution.py:222
  37.7 7.9 %collective-permute-done.13.far_ref = f32[72,512]{1,0:T(8,128)S(1)} collective-permute-done((f32[72,512]{1,0:T(8,128)S(1)}, f32[72,512]{1,0:T(8,128)S(1)}, u32[]{:S(2)}, u32[]{:S(2)}) %collective-permute-start.13) | collective-permute-done | bytes 147488 | tf_op jit(solution)/shard_map/ppermute | solution.py:222
  45.7 0.7 %finish.1 = f32[64,512]{1,0:T(8,128)} custom-call(f32[72,512]{1,0:T(8,128)S(1)} %get-tuple-element.13.own_ref, f32[72,512]{1,0:T(8,128)S(1)} %collective-permute-done.13.far_ref), custom_call_target="tpu_custom_call" | custom-call | tf_op jit(solution)/shard_map/finish/pallas_call | solution.py:204
  (4 shorter events, 0.0 us)
Async XLA Ops:
  0.6 10.7 %collective-permute-start.1 = (bf16[512,128]{1,0:T(8,128)(2,1)}, bf16[512,128]{1,0:T(8,128)(2,1)S(1)}, u32[]{:S(2)}, u32[]{:S(2)}) collective-permute-start(bf16[512,128]{1,0:T(8,128)(2,1)} %refs_4_.1), channel_id=1, source_target_pairs={{0,4},{1,5},{2,6},{3,7},{4,0},{5,1},{6,2},{7,3},{8,12},{9,13},{10,... | collective-permute-start | bytes 393224 | tf_op jit(solution)/shard_map/ppermute | solution.py:222
  4.7 6.8 %collective-permute-start.4 = (bf16[512,128]{1,0:T(8,128)(2,1)}, bf16[512,128]{1,0:T(8,128)(2,1)S(1)}, u32[]{:S(2)}, u32[]{:S(2)}) collective-permute-start(bf16[512,128]{1,0:T(8,128)(2,1)} %refs_4_.1), channel_id=1, source_target_pairs={{0,2},{1,3},{2,0},{3,1},{4,6},{5,7},{6,4},{7,5},{8,10},{9,11},{10,... | collective-permute-start | bytes 393224 | tf_op jit(solution)/shard_map/ppermute | solution.py:222
  6.3 11.8 %collective-permute-start.3 = (bf16[512,128]{1,0:T(8,128)(2,1)}, bf16[512,128]{1,0:T(8,128)(2,1)S(1)}, u32[]{:S(2)}, u32[]{:S(2)}) collective-permute-start(bf16[512,128]{1,0:T(8,128)(2,1)} %refs_4_.1), channel_id=1, source_target_pairs={{0,1},{1,0},{2,3},{3,2},{4,5},{5,4},{6,7},{7,6},{8,9},{9,8},{10,11... | collective-permute-start | bytes 393224 | tf_op jit(solution)/shard_map/ppermute | solution.py:222
  7.8 11.8 %collective-permute-start = (bf16[512,128]{1,0:T(8,128)(2,1)}, bf16[512,128]{1,0:T(8,128)(2,1)S(1)}, u32[]{:S(2)}, u32[]{:S(2)}) collective-permute-start(bf16[512,128]{1,0:T(8,128)(2,1)} %refs_4_.1), channel_id=1, source_target_pairs={{0,8},{8,0},{1,9},{9,1},{2,10},{10,2},{3,11},{11,3},{4,12},{12,4},... | collective-permute-start | bytes 393224 | tf_op jit(solution)/shard_map/ppermute | solution.py:225
  11.4 8.3 %collective-permute-start.2 = (bf16[512,128]{1,0:T(8,128)(2,1)S(1)}, bf16[512,128]{1,0:T(8,128)(2,1)S(1)}, u32[]{:S(2)}, u32[]{:S(2)}) collective-permute-start(bf16[512,128]{1,0:T(8,128)(2,1)S(1)} %collective-permute-done.1.refs_2_), channel_id=1, source_target_pairs={{0,8},{8,0},{1,9},{9,1},{2,10},{10,2},{3,11},{11,3},{4,12},{12,4},... | collective-permute-start | bytes 393224 | tf_op jit(solution)/shard_map/ppermute | solution.py:225
  11.6 8.1 %collective-permute-start.5 = (bf16[512,128]{1,0:T(8,128)(2,1)S(1)}, bf16[512,128]{1,0:T(8,128)(2,1)S(1)}, u32[]{:S(2)}, u32[]{:S(2)}) collective-permute-start(bf16[512,128]{1,0:T(8,128)(2,1)S(1)} %collective-permute-done.4.refs_6_), channel_id=1, source_target_pairs={{0,1},{1,0},{2,3},{3,2},{4,5},{5,4},{6,7},{7,6},{8,9},{9,8},{10,11... | collective-permute-start | bytes 393224 | tf_op jit(solution)/shard_map/ppermute | solution.py:222
  13.1 4.5 %collective-permute-start.10 = (bf16[64,512]{1,0:T(8,128)(2,1)}, bf16[64,512]{1,0:T(8,128)(2,1)S(1)}, u32[]{:S(2)}, u32[]{:S(2)}) collective-permute-start(bf16[64,512]{1,0:T(8,128)(2,1)} %bitcast.3), channel_id=1, source_target_pairs={{0,2},{1,3},{2,0},{3,1},{4,6},{5,7},{6,4},{7,5},{8,10},{9,11},{10,... | collective-permute-start | bytes 196616 | tf_op jit(solution)/shard_map/ppermute | solution.py:222
  17.6 10.3 %collective-permute-start.9 = (bf16[64,512]{1,0:T(8,128)(2,1)}, bf16[64,512]{1,0:T(8,128)(2,1)S(1)}, u32[]{:S(2)}, u32[]{:S(2)}) collective-permute-start(bf16[64,512]{1,0:T(8,128)(2,1)} %bitcast.4), channel_id=1, source_target_pairs={{0,1},{1,0},{2,3},{3,2},{4,5},{5,4},{6,7},{7,6},{8,9},{9,8},{10,11... | collective-permute-start | bytes 196616 | tf_op jit(solution)/shard_map/ppermute | solution.py:222
  18.1 9.8 %collective-permute-start.11 = (bf16[64,512]{1,0:T(8,128)(2,1)S(1)}, bf16[64,512]{1,0:T(8,128)(2,1)S(1)}, u32[]{:S(2)}, u32[]{:S(2)}) collective-permute-start(bf16[64,512]{1,0:T(8,128)(2,1)S(1)} %collective-permute-done.10.refs_6_), channel_id=1, source_target_pairs={{0,1},{1,0},{2,3},{3,2},{4,5},{5,4},{6,7},{7,6},{8,9},{9,8},{10,11... | collective-permute-start | bytes 196616 | tf_op jit(solution)/shard_map/ppermute | solution.py:222
  19.6 0.9 %copy-start = (bf16[512,128]{1,0:T(8,128)(2,1)S(1)}, bf16[512,128]{1,0:T(8,128)(2,1)}, u32[]{:S(2)}) copy-start(bf16[512,128]{1,0:T(8,128)(2,1)} %refs_4_.1) | copy-start | bytes 393220
  24.3 4.6 %collective-permute-start.8 = (f32[1,2048]{1,0:T(1,128)S(1)}, f32[1,2048]{1,0:T(1,128)S(1)}, u32[]{:S(2)}, u32[]{:S(2)}) collective-permute-start(f32[1,2048]{1,0:T(1,128)S(1)} %get-tuple-element.10.refs_0_), channel_id=1, source_target_pairs={{0,3},{1,2},{2,1},{3,0},{4,7},{5,6},{6,5},{7,4},{8,11},{9,10},{10,... | collective-permute-start | bytes 24584 | tf_op jit(solution)/shard_map/ppermute | solution.py:222
  25.7 3.7 %collective-permute-start.7 = (f32[1,2048]{1,0:T(1,128)S(1)}, f32[1,2048]{1,0:T(1,128)S(1)}, u32[]{:S(2)}, u32[]{:S(2)}) collective-permute-start(f32[1,2048]{1,0:T(1,128)S(1)} %get-tuple-element.10.refs_0_), channel_id=1, source_target_pairs={{0,2},{1,3},{2,0},{3,1},{4,6},{5,7},{6,4},{7,5},{8,10},{9,11},{10,... | collective-permute-start | bytes 24584 | tf_op jit(solution)/shard_map/ppermute | solution.py:222
  26.3 3.7 %collective-permute-start.6 = (f32[1,2048]{1,0:T(1,128)S(1)}, f32[1,2048]{1,0:T(1,128)S(1)}, u32[]{:S(2)}, u32[]{:S(2)}) collective-permute-start(f32[1,2048]{1,0:T(1,128)S(1)} %get-tuple-element.10.refs_0_), channel_id=1, source_target_pairs={{0,1},{1,0},{2,3},{3,2},{4,5},{5,4},{6,7},{7,6},{8,9},{9,8},{10,11... | collective-permute-start | bytes 24584 | tf_op jit(solution)/shard_map/ppermute | solution.py:222
  29.9 0.8 %copy-start.1 = (bf16[512,64]{0,1:T(8,128)(2,1)S(1)}, bf16[512,64]{0,1:T(8,128)(2,1)}, u32[]{:S(2)}) copy-start(bf16[512,64]{0,1:T(8,128)(2,1)} %param.3) | copy-start | bytes 196612
  33.6 1.9 %collective-permute-start.12 = (f32[1024,128]{1,0:T(8,128)S(1)}, f32[1024,128]{1,0:T(8,128)S(1)}, u32[]{:S(2)}, u32[]{:S(2)}) collective-permute-start(f32[1024,128]{1,0:T(8,128)S(1)} %get-tuple-element.12), channel_id=1, source_target_pairs={{0,8},{8,0},{1,9},{9,1},{2,10},{10,2},{3,11},{11,3},{4,12},{12,4},... | collective-permute-start | bytes 1572872 | tf_op jit(solution)/shard_map/ppermute | solution.py:225
  35.7 10.0 %collective-permute-start.13 = (f32[72,512]{1,0:T(8,128)S(1)}, f32[72,512]{1,0:T(8,128)S(1)}, u32[]{:S(2)}, u32[]{:S(2)}) collective-permute-start(f32[72,512]{1,0:T(8,128)S(1)} %get-tuple-element.14), channel_id=1, source_target_pairs={{0,4},{1,5},{2,6},{3,7},{4,0},{5,1},{6,2},{7,3},{8,12},{9,13},{10,... | collective-permute-start | bytes 442376 | tf_op jit(solution)/shard_map/ppermute | solution.py:222

commit v2 on v0

v2 whole, which is shorter than its diff:
```python
import functools
import math

import jax
import jax.numpy as jnp
from jax import lax
from jax.experimental import pallas as pl
from jax.experimental.pallas import tpu as pltpu
from jax.sharding import PartitionSpec as P

MIB = 2**20
NT = (((1,), (1,)), ((), ()))
VMEM_SPEC = pl.BlockSpec(memory_space=pltpu.VMEM)


def by_blocks(piece, tile_fn):
    count = piece.shape[0]
    size = 512
    groups = piece.reshape(count // size, size, piece.shape[1])
    firsts = jnp.arange(count // size, dtype=jnp.int32) * size
    return lax.map(lambda item: tile_fn(item[0], item[1]), (groups, firsts))


def plain_device(points, vectors):
    rows_dev = points.shape[0]
    feats = points.shape[1]
    n_col = lax.axis_size("col")
    n_row = lax.axis_size("row")
    half = rows_dev * n_col
    total_pts = half * n_row
    row_pos = lax.axis_index("row")
    col_pos = lax.axis_index("col")
    width = 1.05 * math.sqrt(feats)
    col_points = lax.all_gather(points, "row", axis=0, tiled=True)
    col_vectors = lax.all_gather(vectors, "row", axis=0, tiled=True)
    local = jnp.arange(n_row * rows_dev, dtype=jnp.int32)
    col_ids = local // rows_dev * half + col_pos * rows_dev + local % rows_dev
    col_norms = jnp.sum(col_points.astype(jnp.float32) ** 2, axis=1)
    row_base = row_pos * half
    piece = lax.all_gather(points, "col", axis=0, tiled=True)

    def kernel_tile(block, first):
        norms = jnp.sum(block.astype(jnp.float32) ** 2, axis=1)
        cross = lax.dot_general(block, col_points, NT, preferred_element_type=jnp.float32)
        dist = norms[:, None] + col_norms[None, :] - 2.0 * cross
        values = jnp.exp((2.0 * feats - dist) / width)
        rows = row_base + first + jnp.arange(block.shape[0], dtype=jnp.int32)
        return jnp.where(rows[:, None] == col_ids[None, :], jnp.zeros_like(values), values)

    sums = by_blocks(piece, lambda block, first: jnp.sum(kernel_tile(block, first), axis=1))
    own_sums = lax.psum_scatter(sums.reshape(-1), "col", scatter_dimension=0, tiled=True)
    own_density = own_sums / total_pts
    col_density = lax.all_gather(own_density, "row", axis=0, tiled=True)

    def product_tile(block, first):
        weight = kernel_tile(block, first) / col_density[None, :]
        degree = jnp.sum(weight, axis=1)
        numer = jnp.dot(
            weight.astype(jnp.bfloat16), col_vectors, preferred_element_type=jnp.float32
        )
        return (numer, degree)

    numer, degree = by_blocks(piece, product_tile)
    numer = numer.reshape(piece.shape[0], vectors.shape[1])
    numer_own = lax.psum_scatter(numer, "col", scatter_dimension=0, tiled=True)
    degree_own = lax.psum_scatter(
        degree.reshape(-1), "col", scatter_dimension=0, tiled=True
    )
    return (numer_own / degree_own[:, None], jnp.log(own_density))


def augment(pts, first):
    count, feats = pts.shape
    square = pts.astype(jnp.float32)
    square = square * square
    high = square.astype(jnp.bfloat16)
    low = (square - high.astype(jnp.float32)).astype(jnp.bfloat16)
    pair = jnp.concatenate([high, low], axis=1)
    norm = jnp.dot(
        pair, jnp.ones((2 * feats, 128), jnp.bfloat16), preferred_element_type=jnp.float32
    )
    q = 0.5 * feats - 0.5 * norm
    q0 = q.astype(jnp.bfloat16).astype(jnp.float32)
    rest = q - q0
    q1 = rest.astype(jnp.bfloat16).astype(jnp.float32)
    q2 = rest - q1
    lane = lax.broadcasted_iota(jnp.int32, (count, 128), 1)
    other = 3 - first
    extra = jnp.where((lane >= other) & (lane < other + 3), 1.0, 0.0)
    extra = jnp.where(lane == first + 2, q2, extra)
    extra = jnp.where(lane == first + 1, q1, extra)
    extra = jnp.where(lane == first, q0, extra)
    return jnp.concatenate([pts, extra.astype(jnp.bfloat16)], axis=1)


def kernel_body(counts, unit, scale, diagonal, bm, bn, *refs):
    refs = list(refs)
    raw_rows, done_rows, raw_cols, done_cols, before = [
        [refs.pop(0) for _ in range(count)] for count in counts
    ]
    k_ref, sum_ref = refs.pop(0), refs.pop(0)
    if raw_rows:
        made = refs.pop(0)
        for u, ref in enumerate(raw_rows):
            made[u * unit : (u + 1) * unit, :] = augment(ref[...], 0)
        done_rows = [made] + done_rows
    if raw_cols:
        made = refs.pop(0)
        for u, ref in enumerate(raw_cols):
            made[u * unit : (u + 1) * unit, :] = augment(ref[...], 3)
        done_cols = done_cols + [made]
    c_at = 0
    for col_ref in done_cols:
        for c0 in range(0, col_ref.shape[0], bn):
            total = jnp.zeros((8, bn), jnp.float32)
            r_at = 0
            for row_ref in done_rows:
                for r0 in range(0, row_ref.shape[0], bm):
                    half_log = lax.dot_general(
                        row_ref[r0 : r0 + bm, :],
                        col_ref[c0 : c0 + bn, :],
                        NT,
                        preferred_element_type=jnp.float32,
                    )
                    value = jnp.exp2(half_log * scale)
                    if diagonal and r_at // unit == 0 and c_at // unit == 0:
                        i = lax.broadcasted_iota(jnp.int32, (bm, bn), 0) + r_at
                        j = lax.broadcasted_iota(jnp.int32, (bm, bn), 1) + c_at
                        value = jnp.where(i == j, 0.0, value)
                    k_ref[r_at : r_at + bm, c_at : c_at + bn] = value
                    total = total + jnp.sum(value.reshape(bm // 8, 8, bn), axis=0)
                    r_at += bm
            out = jnp.sum(total, axis=0, keepdims=True)
            at = 0
            for ref in before:
                if at <= c_at < at + ref.shape[1]:
                    out = out + ref[:, c_at - at : c_at - at + bn]
                at += ref.shape[1]
            sum_ref[0:1, c_at : c_at + bn] = out
            c_at += bn


def on_chip(body, shapes, name, limit, flops, *args):
    moved = sum(math.prod(x.shape) * x.dtype.itemsize for x in args)
    return pl.pallas_call(
        body,
        out_shape=shapes,
        in_specs=[VMEM_SPEC] * len(args),
        out_specs=tuple(VMEM_SPEC for _ in shapes),
        compiler_params=pltpu.CompilerParams(vmem_limit_bytes=limit * MIB),
        cost_estimate=pl.CostEstimate(
            flops=int(flops), bytes_accessed=moved, transcendentals=0
        ),
        name=name,
    )(*args)


def kernel_tile(raw_rows, done_rows, raw_cols, done_cols, before, diagonal, name):
    groups = [raw_rows, done_rows, raw_cols, done_cols, before]
    unit, feats = (raw_rows + raw_cols)[0].shape
    wide = feats + 128
    n_rows = sum(x.shape[0] for x in raw_rows + done_rows)
    n_cols = sum(x.shape[0] for x in raw_cols + done_cols)
    scale = 2.0 * math.log2(math.e) / (1.05 * math.sqrt(feats))
    shapes = [
        pltpu.VMEM((n_rows, n_cols), jnp.float32),
        pltpu.VMEM((1, n_cols), jnp.float32),
    ]
    for raw in (raw_rows, raw_cols):
        if raw:
            shapes.append(pltpu.VMEM((len(raw) * unit, wide), jnp.bfloat16))
    body = functools.partial(
        kernel_body, [len(g) for g in groups], unit, scale, diagonal, 256, 512
    )
    args = [x for g in groups for x in g]
    return on_chip(body, tuple(shapes), name, 12, 4 * n_rows * n_cols * wide, *args)


def density_body(n_cols, unit, points_all, *refs):
    sums = refs[:n_cols]
    vecs = refs[n_cols : 2 * n_cols]
    inverse_ref, vec_all, log_ref = refs[2 * n_cols :]
    width = vecs[0].shape[0]
    for v in range(n_cols):
        total = sums[0][:, v * unit : (v + 1) * unit]
        for u in range(1, n_cols):
            w = v ^ u
            total = total + sums[u][:, w * unit : (w + 1) * unit]
        density = total / points_all
        if v == 0:
            log_ref[...] = jnp.log(density)
        inverse_ref[:, v * unit : (v + 1) * unit] = 1.0 / density
        vec_all[0:width, v * unit : (v + 1) * unit] = vecs[v][...]
    ones = lax.broadcasted_iota(jnp.int32, (128 - width, n_cols * unit), 0) == 0
    vec_all[width:128, :] = jnp.where(ones, 1.0, 0.0).astype(jnp.bfloat16)


def product(out_ref, k_refs, r0, count, inverse_ref, vec_all, bm):
    for r in range(0, count, bm):
        numer = None
        at = 0
        for k_ref in k_refs:
            cols = slice(at, at + k_ref.shape[1])
            weight = k_ref[r0 + r : r0 + r + bm, :] * inverse_ref[:, cols]
            part = lax.dot_general(
                weight.astype(jnp.bfloat16),
                vec_all[:, cols],
                NT,
                preferred_element_type=jnp.float32,
            )
            numer = part if numer is None else numer + part
            at += k_ref.shape[1]
        out_ref[r : r + bm, :] = numer


def first_product_body(n_cols, unit, points_all, bm, k_ref, *refs):
    out_ref, *made = refs[2 * n_cols :]
    density_body(n_cols, unit, points_all, *refs[: 2 * n_cols], *made)
    product(out_ref, [k_ref], 0, k_ref.shape[0], made[0], made[1], bm)


def next_product_body(n_k, r0, bm, *refs):
    inverse_ref, vec_all, out_ref = refs[n_k:]
    product(out_ref, refs[:n_k], r0, out_ref.shape[0], inverse_ref, vec_all, bm)


def far_body(width, keep_ref, got_ref, out_ref):
    both = (keep_ref[...] + got_ref[...]).T
    high = both[width : width + 1, :].astype(jnp.bfloat16).astype(jnp.float32)
    low = both[width : width + 1, :] - high
    zero = jnp.zeros((14, both.shape[1]), jnp.float32)
    out = jnp.concatenate([both[0:width, :], high, low, zero], axis=0)
    out_ref[...] = out.astype(jnp.bfloat16)


def finish_body(own_ref, got_ref, far_ref, out_ref):
    width = out_ref.shape[0]
    near = (own_ref[...] + got_ref[...]).T
    far = far_ref[...].astype(jnp.float32)
    degree = near[width : width + 1, :] + (
        far[width : width + 1, :] + far[width + 1 : width + 2, :]
    )
    out_ref[...] = (near[0:width, :] + far[0:width, :]) / degree


def grid_device(points, vectors):
    n_col = lax.axis_size("col")
    unit = points.shape[0]
    width = vectors.shape[1]
    points_all = float(unit * n_col * lax.axis_size("row"))
    n_units = n_col // 2
    n_wide = n_units * unit

    def across(x, mask):
        return lax.ppermute(x, "col", [(i, i ^ mask) for i in range(n_col)])

    def sibling(x):
        return lax.ppermute(x, "row", [(0, 1), (1, 0)])

    beside = sibling(points)
    far = across(points, n_units)
    held = {0: points}
    bit = n_units // 2
    while bit:
        for u in list(held):
            held[u | bit] = across(held[u], bit)
        bit //= 2
    cols = [held[u] for u in range(n_units)]
    far_beside = sibling(far)
    k_near, sums, rows_near, cols_near = kernel_tile(
        [points, beside], [], cols[:-1], [], [], True, "near"
    )
    k_last, sums_last, cols_last = kernel_tile(
        [], [rows_near], cols[-1:], [], [], False, "last"
    )
    cols_all = [cols_near, cols_last]
    k_far, sums, _ = kernel_tile([far], [], [], cols_all, [sums, sums_last], False, "far")
    k_beside, sums, _ = kernel_tile(
        [far_beside], [], [], cols_all, [sums], False, "far_beside"
    )
    vecs = [vectors.T] + [across(vectors.T, u) for u in range(1, n_units)]
    all_sums = [sums] + [across(sums, u) for u in range(1, n_units)]

    flops = 2 * unit * n_wide * 128
    block = pltpu.VMEM((unit, 128), jnp.float32)
    give_far, inverse, vec_all, log_density = on_chip(
        functools.partial(first_product_body, n_units, unit, points_all, 256),
        (
            block,
            pltpu.VMEM((1, n_wide), jnp.float32),
            pltpu.VMEM((128, n_wide), jnp.bfloat16),
            jax.ShapeDtypeStruct((1, unit), jnp.float32),
        ),
        "product_far_beside",
        8,
        flops,
        k_beside,
        *all_sums,
        *vecs,
    )

    def next_product(ks, r0, name):
        body = functools.partial(next_product_body, len(ks), r0, 256)
        return on_chip(body, (block,), name, 8, flops, *ks, inverse, vec_all)[0]

    got_far = sibling(give_far)
    keep_far = next_product([k_far], 0, "product_far")
    (away,) = on_chip(
        functools.partial(far_body, width),
        (pltpu.VMEM((width + 16, unit), jnp.bfloat16),),
        "sum_far",
        8,
        1,
        keep_far,
        got_far,
    )
    back = across(away, n_units)
    give = next_product([k_near, k_last], unit, "product_beside")
    got = sibling(give)
    keep = next_product([k_near, k_last], 0, "product_own")
    (smoothed,) = on_chip(
        finish_body,
        (jax.ShapeDtypeStruct((width, unit), jnp.float32),),
        "finish",
        8,
        1,
        keep,
        got,
        back,
    )
    return (smoothed.T, log_density.reshape(unit))


def solution(mesh):
    n_col = mesh.shape["col"]
    n_row = mesh.shape["row"]
    placed = (P(("parts", "row", "col"), None), P(("parts", "row", "col"), None))

    def run(points, vectors):
        unit, feats = points.shape
        paired = n_row == 2 and n_col >= 2 and n_col & (n_col - 1) == 0
        tile_bytes = 4 * (4 * unit) * (n_col // 2 * unit)
        shaped = unit % 512 == 0 and feats == 128 and vectors.shape[1] <= 120
        if paired and shaped and tile_bytes <= 16 * MIB:
            return grid_device(points, vectors)
        return plain_device(points, vectors)

    return jax.shard_map(
        run,
        mesh=mesh,
        in_specs=placed,
        out_specs=(P(("parts", "row", "col"), None), P(("parts", "row", "col"))),
        check_vma=False,
    )
```

time: 245 us -> 38.6 us (0.16)
  blocking collectives: 74 us -> 0 us
  waiting for transfers between devices: 66.2 us -> 9.52 us
  matrix products: 33.8 us -> 0 us
  local copies, waits for them, and re-layouts: 24.8 us -> 0.91 us
  other arithmetic: 19.5 us -> 0 us
  starting transfers between devices: 0.08 us -> 18 us
  between operations: 14.8 us -> 0.71 us
  loops' own time: 11 us -> 0 us
  Pallas kernels: 0 us -> 9.32 us
    unnamed x2 -> x0, blocking collectives: 68 us -> none
    all_gather x1 -> x0, waiting for transfers between devices: 37.7 us -> none  [on_device(): piece = lax.all_gather(points, 'col', axis=0, tiled=True)]
    dot_general x24 -> x0, matrix products: 33.8 us -> none  [the longest x16 30.2 us: kernel_tile(): lax.dot_general(block, col_points, (((1,), (1,)), ((), ())), preferred_el...]
    reduce_scatter x1 -> x0, waiting for transfers between devices: 27.8 us -> none  [on_device(): lax.psum_scatter(numer, 'col', scatter_dimension=0, tiled=True)]
    ppermute x0 -> x15, starting transfers between devices: none -> 18 us  [the longest x11 16.9 us: across(): return lax.ppermute(x, 'col', [(i, i ^ mask) for i in range(n_col)])]
    reduce_sum x17 -> x0, other arithmetic: 17.1 us -> none  [the longest x16 16.9 us: kernel_tile(): norms = jnp.sum(block.astype(jnp.float32) ** 2, axis=1)]
    dynamic_update_slice x32 -> x0, local copies, waits for them, and re-layouts: 11.1 us -> none  [by_blocks(): return lax.map(lambda item: tile_fn(item[0], item[1]), (groups, firsts))]
    another operation x2 -> x0, loops' own time: 11 us -> none  [by_blocks(): return lax.map(lambda item: tile_fn(item[0], item[1]), (groups, firsts))]
  transfers between devices with their start and end apart: 2 -> 15, of which waited for: 2 -> 7; matrix products, arithmetic and copies ran while one was open for 1% -> 0% of each run, Pallas kernels for 0% -> 19%
where the time goes in v2:
time: 38.6 us; the launch traced here: 38.5 us
  starting transfers between devices  18 us (47%)
  waiting for transfers between devices  9.52 us (25%)
  Pallas kernels  9.32 us (24%)
  local copies, waits for them, and re-layouts  0.91 us (2%)
  between operations  0.71 us (2%)
    ppermute x11, starting transfers between devices, across(): return lax.ppermute(x, 'col', [(i, i ^ mask) for i in range(n_col)])  16.9 us
    ppermute x11, waiting for transfers between devices, across(): return lax.ppermute(x, 'col', [(i, i ^ mask) for i in range(n_col)])  9.51 us
    pallas_call x10, Pallas kernels, on_chip(): pl.pallas_call(body, out_shape=shapes, in_specs=[VMEM_SPEC] * len(args),...  9.32 us
    ppermute x4, starting transfers between devices, sibling(): return lax.ppermute(x, 'row', [(0, 1), (1, 0)])  1.1 us
    unnamed x4, local copies, waits for them, and re-layouts  0.91 us
  transfers between devices with their start and end apart: 15, of which 7 were waited for; matrix products, arithmetic and copies ran while one was open for 0% of the time, Pallas kernels for 19%

profile of v2, /device:TPU:0, one launch (start us, length us, event | category | flops | bytes accessed | tf_op | source)
XLA Modules:
  0.0 38.5 jit_solution(9842808495978874885)
XLA Ops:
  0.6 0.5 %collective-permute-start = (bf16[512,128]{1,0:T(8,128)(2,1)}, bf16[512,128]{1,0:T(8,128)(2,1)S(1)}, u32[]{:S(2)}, u32[]{:S(2)}) collective-permute-start(bf16[512,128]{1,0:T(8,128)(2,1)} %refs_2_.1), channel_id=1, source_target_pairs={{0,8},{8,0},{1,9},{9,1},{2,10},{10,2},{3,11},{11,3},{4,12},{12,4},... | collective-permute-start | bytes 393224 | tf_op jit(solution)/shard_map/ppermute | solution.py:258
  1.1 2.6 %collective-permute-start.1 = (bf16[512,128]{1,0:T(8,128)(2,1)}, bf16[512,128]{1,0:T(8,128)(2,1)S(1)}, u32[]{:S(2)}, u32[]{:S(2)}) collective-permute-start(bf16[512,128]{1,0:T(8,128)(2,1)} %refs_2_.1), channel_id=1, source_target_pairs={{0,1},{1,0},{2,3},{3,2},{4,5},{5,4},{6,7},{7,6},{8,9},{9,8},{10,11... | collective-permute-start | bytes 393224 | tf_op jit(solution)/shard_map/ppermute | solution.py:255
  3.7 1.6 %collective-permute-start.2 = (bf16[512,128]{1,0:T(8,128)(2,1)}, bf16[512,128]{1,0:T(8,128)(2,1)S(1)}, u32[]{:S(2)}, u32[]{:S(2)}) collective-permute-start(bf16[512,128]{1,0:T(8,128)(2,1)} %refs_2_.1), channel_id=1, source_target_pairs={{0,2},{1,3},{2,0},{3,1},{4,6},{5,7},{6,4},{7,5},{8,10},{9,11},{10,... | collective-permute-start | bytes 393224 | tf_op jit(solution)/shard_map/ppermute | solution.py:255
  5.3 2.6 %collective-permute-start.4 = (bf16[512,128]{1,0:T(8,128)(2,1)}, bf16[512,128]{1,0:T(8,128)(2,1)S(1)}, u32[]{:S(2)}, u32[]{:S(2)}) collective-permute-start(bf16[512,128]{1,0:T(8,128)(2,1)} %refs_2_.1), channel_id=1, source_target_pairs={{0,4},{1,5},{2,6},{3,7},{4,0},{5,1},{6,2},{7,3},{8,12},{9,13},{10,... | collective-permute-start | bytes 393224 | tf_op jit(solution)/shard_map/ppermute | solution.py:255
  7.9 0.5 %collective-permute-start.9 = (bf16[64,512]{1,0:T(8,128)(2,1)}, bf16[64,512]{1,0:T(8,128)(2,1)S(1)}, u32[]{:S(2)}, u32[]{:S(2)}) collective-permute-start(bf16[64,512]{1,0:T(8,128)(2,1)} %bitcast.3), channel_id=1, source_target_pairs={{0,1},{1,0},{2,3},{3,2},{4,5},{5,4},{6,7},{7,6},{8,9},{9,8},{10,11... | collective-permute-start | bytes 196616 | tf_op jit(solution)/shard_map/ppermute | solution.py:255
  8.4 0.5 %collective-permute-start.10 = (bf16[64,512]{1,0:T(8,128)(2,1)}, bf16[64,512]{1,0:T(8,128)(2,1)S(1)}, u32[]{:S(2)}, u32[]{:S(2)}) collective-permute-start(bf16[64,512]{1,0:T(8,128)(2,1)} %bitcast.4), channel_id=1, source_target_pairs={{0,2},{1,3},{2,0},{3,1},{4,6},{5,7},{6,4},{7,5},{8,10},{9,11},{10,... | collective-permute-start | bytes 196616 | tf_op jit(solution)/shard_map/ppermute | solution.py:255
  8.9 2.5 %collective-permute-start.11 = (bf16[64,512]{1,0:T(8,128)(2,1)}, bf16[64,512]{1,0:T(8,128)(2,1)S(1)}, u32[]{:S(2)}, u32[]{:S(2)}) collective-permute-start(bf16[64,512]{1,0:T(8,128)(2,1)} %bitcast.5), channel_id=1, source_target_pairs={{0,3},{1,2},{2,1},{3,0},{4,7},{5,6},{6,5},{7,4},{8,11},{9,10},{10,... | collective-permute-start | bytes 196616 | tf_op jit(solution)/shard_map/ppermute | solution.py:255
  11.4 1.2 %collective-permute-done.2.refs_4_ = bf16[512,128]{1,0:T(8,128)(2,1)S(1)} collective-permute-done((bf16[512,128]{1,0:T(8,128)(2,1)}, bf16[512,128]{1,0:T(8,128)(2,1)S(1)}, u32[]{:S(2)}, u32[]{:S(2)}) %collective-permute-start.2) | collective-permute-done | bytes 131104 | tf_op jit(solution)/shard_map/ppermute | solution.py:255
  12.6 1.4 %collective-permute-done.4.refs_0_ = bf16[512,128]{1,0:T(8,128)(2,1)S(1)} collective-permute-done((bf16[512,128]{1,0:T(8,128)(2,1)}, bf16[512,128]{1,0:T(8,128)(2,1)S(1)}, u32[]{:S(2)}, u32[]{:S(2)}) %collective-permute-start.4) | collective-permute-done | bytes 131104 | tf_op jit(solution)/shard_map/ppermute | solution.py:255
  14.0 0.0 collective-permute-start.5
  14.0 0.9 %copy-done.1 = bf16[512,128]{1,0:T(8,128)(2,1)S(1)} copy-done((bf16[512,128]{1,0:T(8,128)(2,1)S(1)}, bf16[512,128]{1,0:T(8,128)(2,1)}, u32[]{:S(2)}) %copy-start.1) | copy-done | bytes 131096
  14.9 1.9 %near.1 = (f32[1024,1536]{1,0:T(8,128)S(1)}, f32[1,1536]{1,0:T(1,128)S(1)}, bf16[1024,256]{1,0:T(8,128)(2,1)S(1)}, bf16[1536,256]{1,0:T(8,128)(2,1)S(1)}) custom-call(bf16[512,128]{1,0:T(8,128)(2,1)S(1)} %copy-done.1, bf16[512,128]{1,0:T(8,128)(2,1)S(1)} %collective-permute-done.refs_1_, bf16[512,128]{1,0:T(8,128)(2,1)S(1)} %copy-done.1, ...), custom_call_target="tpu_custom_call" | custom-call | flops 1610612736 | bytes 655360 | tf_op jit(solution)/shard_map/near/pallas_call | solution.py:145
  16.8 0.8 %collective-permute-done.3.refs_1_ = bf16[512,128]{1,0:T(8,128)(2,1)S(1)} collective-permute-done((bf16[512,128]{1,0:T(8,128)(2,1)S(1)}, bf16[512,128]{1,0:T(8,128)(2,1)S(1)}, u32[]{:S(2)}, u32[]{:S(2)}) %collective-permute-start.3) | collective-permute-done | bytes 131104 | tf_op jit(solution)/shard_map/ppermute | solution.py:255
  17.6 0.7 %last.1 = (f32[1024,512]{1,0:T(8,128)S(1)}, f32[1,512]{1,0:T(1,128)S(1)}, bf16[512,256]{1,0:T(8,128)(2,1)S(1)}) custom-call(bf16[1024,256]{1,0:T(8,128)(2,1)S(1)} %get-tuple-element.18.refs_0_, bf16[512,128]{1,0:T(8,128)(2,1)S(1)} %collective-permute-done.3.refs_1_), custom_call_target="tpu_custom_call" | custom-call | flops 536870912 | bytes 655360 | tf_op jit(solution)/shard_map/last/pallas_call | solution.py:145
  18.3 0.0 copy-start
  18.3 1.5 %far.1 = (f32[512,2048]{1,0:T(8,128)S(1)}, f32[1,2048]{1,0:T(1,128)S(1)}, bf16[512,256]{1,0:T(8,128)(2,1)}) custom-call(bf16[512,128]{1,0:T(8,128)(2,1)S(1)} %collective-permute-done.4.refs_0_, bf16[1536,256]{1,0:T(8,128)(2,1)S(1)} %get-tuple-element.20.refs_1_, bf16[512,256]{1,0:T(8,128)(2,1)S(1)} %get-tuple-element.21.refs_2_, ...), custom_call_target="tpu_custom_call" | custom-call | flops 1073741824 | bytes 1187840 | tf_op jit(solution)/shard_map/far/pallas_call | solution.py:145
  19.9 1.0 %far_beside.1 = (f32[512,2048]{1,0:T(8,128)S(1)}, f32[1,2048]{1,0:T(1,128)S(1)}, bf16[512,256]{1,0:T(8,128)(2,1)}) custom-call(bf16[512,128]{1,0:T(8,128)(2,1)S(1)} %collective-permute-done.5.refs_0_, bf16[1536,256]{1,0:T(8,128)(2,1)S(1)} %get-tuple-element.20.refs_1_, bf16[512,256]{1,0:T(8,128)(2,1)S(1)} %get-tuple-element.21.refs_2_, ...), custom_call_target="tpu_custom_call" | custom-call | flops 1073741824 | bytes 1187840 | tf_op jit(solution)/shard_map/far_beside/pallas_call | solution.py:145
  20.9 0.4 %collective-permute-start.6 = (f32[1,2048]{1,0:T(1,128)S(1)}, f32[1,2048]{1,0:T(1,128)S(1)}, u32[]{:S(2)}, u32[]{:S(2)}) collective-permute-start(f32[1,2048]{1,0:T(1,128)S(1)} %get-tuple-element.26.refs_0_), channel_id=1, source_target_pairs={{0,1},{1,0},{2,3},{3,2},{4,5},{5,4},{6,7},{7,6},{8,9},{9,8},{10,11... | collective-permute-start | bytes 24584 | tf_op jit(solution)/shard_map/ppermute | solution.py:255
  21.3 1.0 %collective-permute-start.7 = (f32[1,2048]{1,0:T(1,128)S(1)}, f32[1,2048]{1,0:T(1,128)S(1)}, u32[]{:S(2)}, u32[]{:S(2)}) collective-permute-start(f32[1,2048]{1,0:T(1,128)S(1)} %get-tuple-element.26.refs_0_), channel_id=1, source_target_pairs={{0,2},{1,3},{2,0},{3,1},{4,6},{5,7},{6,4},{7,5},{8,10},{9,11},{10,... | collective-permute-start | bytes 24584 | tf_op jit(solution)/shard_map/ppermute | solution.py:255
  22.3 2.0 %collective-permute-start.8 = (f32[1,2048]{1,0:T(1,128)S(1)}, f32[1,2048]{1,0:T(1,128)S(1)}, u32[]{:S(2)}, u32[]{:S(2)}) collective-permute-start(f32[1,2048]{1,0:T(1,128)S(1)} %get-tuple-element.26.refs_0_), channel_id=1, source_target_pairs={{0,3},{1,2},{2,1},{3,0},{4,7},{5,6},{6,5},{7,4},{8,11},{9,10},{10,... | collective-permute-start | bytes 24584 | tf_op jit(solution)/shard_map/ppermute | solution.py:255
  24.4 0.2 collective-permute-done.6.refs_1_
  24.5 0.4 %collective-permute-done.7.refs_2_ = f32[1,2048]{1,0:T(1,128)S(1)} collective-permute-done((f32[1,2048]{1,0:T(1,128)S(1)}, f32[1,2048]{1,0:T(1,128)S(1)}, u32[]{:S(2)}, u32[]{:S(2)}) %collective-permute-start.7) | collective-permute-done | bytes 8224 | tf_op jit(solution)/shard_map/ppermute | solution.py:255
  24.9 1.9 %collective-permute-done.8.refs_3_ = f32[1,2048]{1,0:T(1,128)S(1)} collective-permute-done((f32[1,2048]{1,0:T(1,128)S(1)}, f32[1,2048]{1,0:T(1,128)S(1)}, u32[]{:S(2)}, u32[]{:S(2)}) %collective-permute-start.8) | collective-permute-done | bytes 8224 | tf_op jit(solution)/shard_map/ppermute | solution.py:255
  26.9 1.2 %product_far_beside.1 = (f32[512,128]{1,0:T(8,128)S(1)}, f32[1,2048]{1,0:T(1,128)S(1)}, bf16[128,2048]{1,0:T(8,128)(2,1)S(1)}, f32[1,512]{1,0:T(1,128)}) custom-call(f32[512,2048]{1,0:T(8,128)S(1)} %get-tuple-element.25.k_ref, f32[1,2048]{1,0:T(1,128)S(1)} %get-tuple-element.26.refs_0_, f32[1,2048]{1,0:T(1,128)S(1)} %collective-permute-done.6.refs_1_, ...), custom_call_target="tpu_custom_call" | custom-call | flops 268435456 | bytes 4489216 | tf_op jit(solution)/shard_map/product_far_beside/pallas_call | solution.py:145
  28.1 0.7 %product_beside.1 = f32[512,128]{1,0:T(8,128)S(1)} custom-call(f32[1024,1536]{1,0:T(8,128)S(1)} %get-tuple-element.17.refs_0_, f32[1024,512]{1,0:T(8,128)S(1)} %get-tuple-element.19.refs_1_, f32[1,2048]{1,0:T(1,128)S(1)} %get-tuple-element.27.refs_2_.refs_1_, bf16[128,2048]{1,0:T(8,128)(2,1)S(1)} %get-tuple-element.28.refs_3_.refs_2_), custom_call_target="tpu_custom_call" | custom-call | flops 268435456 | bytes 8921088 | tf_op jit(solution)/shard_map/product_beside/pallas_call | solution.py:145
  28.8 0.6 %collective-permute-start.12 = (f32[512,128]{1,0:T(8,128)S(1)}, f32[512,128]{1,0:T(8,128)S(1)}, u32[]{:S(2)}, u32[]{:S(2)}) collective-permute-start(f32[512,128]{1,0:T(8,128)S(1)} %product_beside.1), channel_id=1, source_target_pairs={{0,8},{8,0},{1,9},{9,1},{2,10},{10,2},{3,11},{11,3},{4,12},{12,4},... | collective-permute-start | bytes 786440 | tf_op jit(solution)/shard_map/ppermute | solution.py:258
  29.3 0.7 %product_far.1.keep_ref = f32[512,128]{1,0:T(8,128)S(1)} custom-call(f32[512,2048]{1,0:T(8,128)S(1)} %get-tuple-element.29.refs_0_, f32[1,2048]{1,0:T(1,128)S(1)} %get-tuple-element.27.refs_2_.refs_1_, bf16[128,2048]{1,0:T(8,128)(2,1)S(1)} %get-tuple-element.28.refs_3_.refs_2_), custom_call_target="tpu_custom_call" | custom-call | flops 268435456 | bytes 4726784 | tf_op jit(solution)/shard_map/product_far/pallas_call | solution.py:145
  30.0 0.1 sum_far.1
  30.2 3.2 %collective-permute-start.14 = (bf16[80,512]{1,0:T(8,128)(2,1)S(1)}, bf16[80,512]{1,0:T(8,128)(2,1)S(1)}, u32[]{:S(2)}, u32[]{:S(2)}) collective-permute-start(bf16[80,512]{1,0:T(8,128)(2,1)S(1)} %sum_far.1), channel_id=1, source_target_pairs={{0,4},{1,5},{2,6},{3,7},{4,0},{5,1},{6,2},{7,3},{8,12},{9,13},{10,... | collective-permute-start | bytes 245768 | tf_op jit(solution)/shard_map/ppermute | solution.py:255
  33.4 0.7 %product_own.1.own_ref = f32[512,128]{1,0:T(8,128)S(1)} custom-call(f32[1024,1536]{1,0:T(8,128)S(1)} %get-tuple-element.17.refs_0_, f32[1024,512]{1,0:T(8,128)S(1)} %get-tuple-element.19.refs_1_, f32[1,2048]{1,0:T(1,128)S(1)} %get-tuple-element.27.refs_2_.refs_1_, bf16[128,2048]{1,0:T(8,128)(2,1)S(1)} %get-tuple-element.28.refs_3_.refs_2_), custom_call_target="tpu_custom_call" | custom-call | flops 268435456 | bytes 8921088 | tf_op jit(solution)/shard_map/product_own/pallas_call | solution.py:145
  34.1 3.6 %collective-permute-done.14.far_ref = bf16[80,512]{1,0:T(8,128)(2,1)S(1)} collective-permute-done((bf16[80,512]{1,0:T(8,128)(2,1)S(1)}, bf16[80,512]{1,0:T(8,128)(2,1)S(1)}, u32[]{:S(2)}, u32[]{:S(2)}) %collective-permute-start.14) | collective-permute-done | bytes 81952 | tf_op jit(solution)/shard_map/ppermute | solution.py:255
  37.7 0.8 %finish.1 = f32[64,512]{1,0:T(8,128)} custom-call(f32[512,128]{1,0:T(8,128)S(1)} %product_own.1.own_ref, f32[512,128]{1,0:T(8,128)S(1)} %collective-permute-done.12.got_ref, bf16[80,512]{1,0:T(8,128)(2,1)S(1)} %collective-permute-done.14.far_ref), custom_call_target="tpu_custom_call" | custom-call | flops 1 | bytes 606208 | tf_op jit(solution)/shard_map/finish/pallas_call | solution.py:145
  (12 shorter events, 0.0 us)
Async XLA Ops:
  0.6 7.8 %collective-permute-start = (bf16[512,128]{1,0:T(8,128)(2,1)}, bf16[512,128]{1,0:T(8,128)(2,1)S(1)}, u32[]{:S(2)}, u32[]{:S(2)}) collective-permute-start(bf16[512,128]{1,0:T(8,128)(2,1)} %refs_2_.1), channel_id=1, source_target_pairs={{0,8},{8,0},{1,9},{9,1},{2,10},{10,2},{3,11},{11,3},{4,12},{12,4},... | collective-permute-start | bytes 393224 | tf_op jit(solution)/shard_map/ppermute | solution.py:258
  1.1 7.7 %collective-permute-start.1 = (bf16[512,128]{1,0:T(8,128)(2,1)}, bf16[512,128]{1,0:T(8,128)(2,1)S(1)}, u32[]{:S(2)}, u32[]{:S(2)}) collective-permute-start(bf16[512,128]{1,0:T(8,128)(2,1)} %refs_2_.1), channel_id=1, source_target_pairs={{0,1},{1,0},{2,3},{3,2},{4,5},{5,4},{6,7},{7,6},{8,9},{9,8},{10,11... | collective-permute-start | bytes 393224 | tf_op jit(solution)/shard_map/ppermute | solution.py:255
  3.7 8.9 %collective-permute-start.2 = (bf16[512,128]{1,0:T(8,128)(2,1)}, bf16[512,128]{1,0:T(8,128)(2,1)S(1)}, u32[]{:S(2)}, u32[]{:S(2)}) collective-permute-start(bf16[512,128]{1,0:T(8,128)(2,1)} %refs_2_.1), channel_id=1, source_target_pairs={{0,2},{1,3},{2,0},{3,1},{4,6},{5,7},{6,4},{7,5},{8,10},{9,11},{10,... | collective-permute-start | bytes 393224 | tf_op jit(solution)/shard_map/ppermute | solution.py:255
  5.3 8.7 %collective-permute-start.4 = (bf16[512,128]{1,0:T(8,128)(2,1)}, bf16[512,128]{1,0:T(8,128)(2,1)S(1)}, u32[]{:S(2)}, u32[]{:S(2)}) collective-permute-start(bf16[512,128]{1,0:T(8,128)(2,1)} %refs_2_.1), channel_id=1, source_target_pairs={{0,4},{1,5},{2,6},{3,7},{4,0},{5,1},{6,2},{7,3},{8,12},{9,13},{10,... | collective-permute-start | bytes 393224 | tf_op jit(solution)/shard_map/ppermute | solution.py:255
  7.9 14.4 %collective-permute-start.9 = (bf16[64,512]{1,0:T(8,128)(2,1)}, bf16[64,512]{1,0:T(8,128)(2,1)S(1)}, u32[]{:S(2)}, u32[]{:S(2)}) collective-permute-start(bf16[64,512]{1,0:T(8,128)(2,1)} %bitcast.3), channel_id=1, source_target_pairs={{0,1},{1,0},{2,3},{3,2},{4,5},{5,4},{6,7},{7,6},{8,9},{9,8},{10,11... | collective-permute-start | bytes 196616 | tf_op jit(solution)/shard_map/ppermute | solution.py:255
  8.4 15.9 %collective-permute-start.10 = (bf16[64,512]{1,0:T(8,128)(2,1)}, bf16[64,512]{1,0:T(8,128)(2,1)S(1)}, u32[]{:S(2)}, u32[]{:S(2)}) collective-permute-start(bf16[64,512]{1,0:T(8,128)(2,1)} %bitcast.4), channel_id=1, source_target_pairs={{0,2},{1,3},{2,0},{3,1},{4,6},{5,7},{6,4},{7,5},{8,10},{9,11},{10,... | collective-permute-start | bytes 196616 | tf_op jit(solution)/shard_map/ppermute | solution.py:255
  8.9 15.5 %collective-permute-start.11 = (bf16[64,512]{1,0:T(8,128)(2,1)}, bf16[64,512]{1,0:T(8,128)(2,1)S(1)}, u32[]{:S(2)}, u32[]{:S(2)}) collective-permute-start(bf16[64,512]{1,0:T(8,128)(2,1)} %bitcast.5), channel_id=1, source_target_pairs={{0,3},{1,2},{2,1},{3,0},{4,7},{5,6},{6,5},{7,4},{8,11},{9,10},{10,... | collective-permute-start | bytes 196616 | tf_op jit(solution)/shard_map/ppermute | solution.py:255
  12.6 5.0 %collective-permute-start.3 = (bf16[512,128]{1,0:T(8,128)(2,1)S(1)}, bf16[512,128]{1,0:T(8,128)(2,1)S(1)}, u32[]{:S(2)}, u32[]{:S(2)}) collective-permute-start(bf16[512,128]{1,0:T(8,128)(2,1)S(1)} %collective-permute-done.2.refs_4_), channel_id=1, source_target_pairs={{0,1},{1,0},{2,3},{3,2},{4,5},{5,4},{6,7},{7,6},{8,9},{9,8},{10,11... | collective-permute-start | bytes 393224 | tf_op jit(solution)/shard_map/ppermute | solution.py:255
  14.0 5.9 %collective-permute-start.5 = (bf16[512,128]{1,0:T(8,128)(2,1)S(1)}, bf16[512,128]{1,0:T(8,128)(2,1)S(1)}, u32[]{:S(2)}, u32[]{:S(2)}) collective-permute-start(bf16[512,128]{1,0:T(8,128)(2,1)S(1)} %collective-permute-done.4.refs_0_), channel_id=1, source_target_pairs={{0,8},{8,0},{1,9},{9,1},{2,10},{10,2},{3,11},{11,3},{4,12},{12,4},... | collective-permute-start | bytes 393224 | tf_op jit(solution)/shard_map/ppermute | solution.py:258
  14.0 0.9 %copy-start.1 = (bf16[512,128]{1,0:T(8,128)(2,1)S(1)}, bf16[512,128]{1,0:T(8,128)(2,1)}, u32[]{:S(2)}) copy-start(bf16[512,128]{1,0:T(8,128)(2,1)} %refs_2_.1) | copy-start | bytes 393220
  18.3 8.6 %copy-start = (bf16[512,64]{0,1:T(8,128)(2,1)S(1)}, bf16[512,64]{0,1:T(8,128)(2,1)}, u32[]{:S(2)}) copy-start(bf16[512,64]{0,1:T(8,128)(2,1)} %param.3) | copy-start | bytes 196612
  20.9 3.7 %collective-permute-start.6 = (f32[1,2048]{1,0:T(1,128)S(1)}, f32[1,2048]{1,0:T(1,128)S(1)}, u32[]{:S(2)}, u32[]{:S(2)}) collective-permute-start(f32[1,2048]{1,0:T(1,128)S(1)} %get-tuple-element.26.refs_0_), channel_id=1, source_target_pairs={{0,1},{1,0},{2,3},{3,2},{4,5},{5,4},{6,7},{7,6},{8,9},{9,8},{10,11... | collective-permute-start | bytes 24584 | tf_op jit(solution)/shard_map/ppermute | solution.py:255
  21.3 3.7 %collective-permute-start.7 = (f32[1,2048]{1,0:T(1,128)S(1)}, f32[1,2048]{1,0:T(1,128)S(1)}, u32[]{:S(2)}, u32[]{:S(2)}) collective-permute-start(f32[1,2048]{1,0:T(1,128)S(1)} %get-tuple-element.26.refs_0_), channel_id=1, source_target_pairs={{0,2},{1,3},{2,0},{3,1},{4,6},{5,7},{6,4},{7,5},{8,10},{9,11},{10,... | collective-permute-start | bytes 24584 | tf_op jit(solution)/shard_map/ppermute | solution.py:255
  22.3 4.6 %collective-permute-start.8 = (f32[1,2048]{1,0:T(1,128)S(1)}, f32[1,2048]{1,0:T(1,128)S(1)}, u32[]{:S(2)}, u32[]{:S(2)}) collective-permute-start(f32[1,2048]{1,0:T(1,128)S(1)} %get-tuple-element.26.refs_0_), channel_id=1, source_target_pairs={{0,3},{1,2},{2,1},{3,0},{4,7},{5,6},{6,5},{7,4},{8,11},{9,10},{10,... | collective-permute-start | bytes 24584 | tf_op jit(solution)/shard_map/ppermute | solution.py:255
  28.1 2.0 %collective-permute-start.13 = (f32[512,128]{1,0:T(8,128)S(1)}, f32[512,128]{1,0:T(8,128)S(1)}, u32[]{:S(2)}, u32[]{:S(2)}) collective-permute-start(f32[512,128]{1,0:T(8,128)S(1)} %get-tuple-element.30), channel_id=1, source_target_pairs={{0,8},{8,0},{1,9},{9,1},{2,10},{10,2},{3,11},{11,3},{4,12},{12,4},... | collective-permute-start | bytes 786440 | tf_op jit(solution)/shard_map/ppermute | solution.py:258
  28.8 5.3 %collective-permute-start.12 = (f32[512,128]{1,0:T(8,128)S(1)}, f32[512,128]{1,0:T(8,128)S(1)}, u32[]{:S(2)}, u32[]{:S(2)}) collective-permute-start(f32[512,128]{1,0:T(8,128)S(1)} %product_beside.1), channel_id=1, source_target_pairs={{0,8},{8,0},{1,9},{9,1},{2,10},{10,2},{3,11},{11,3},{4,12},{12,4},... | collective-permute-start | bytes 786440 | tf_op jit(solution)/shard_map/ppermute | solution.py:258
  30.2 7.5 %collective-permute-start.14 = (bf16[80,512]{1,0:T(8,128)(2,1)S(1)}, bf16[80,512]{1,0:T(8,128)(2,1)S(1)}, u32[]{:S(2)}, u32[]{:S(2)}) collective-permute-start(bf16[80,512]{1,0:T(8,128)(2,1)S(1)} %sum_far.1), channel_id=1, source_target_pairs={{0,4},{1,5},{2,6},{3,7},{4,0},{5,1},{6,2},{7,3},{8,12},{9,13},{10,... | collective-permute-start | bytes 245768 | tf_op jit(solution)/shard_map/ppermute | solution.py:255

commit v3 on v2

--- a/solution.py
+++ b/solution.py
@@ -95,20 +95,21 @@
 
 def kernel_body(counts, unit, scale, diagonal, bm, bn, *refs):
     refs = list(refs)
-    raw_rows, done_rows, raw_cols, done_cols, before = [
+    raw_rows, done_rows, raw_cols, done_cols, before, vectors = [
         [refs.pop(0) for _ in range(count)] for count in counts
     ]
     k_ref, sum_ref = refs.pop(0), refs.pop(0)
-    if raw_rows:
-        made = refs.pop(0)
-        for u, ref in enumerate(raw_rows):
-            made[u * unit : (u + 1) * unit, :] = augment(ref[...], 0)
-        done_rows = [made] + done_rows
+    pack_ref = refs.pop(0) if vectors else None
     if raw_cols:
         made = refs.pop(0)
         for u, ref in enumerate(raw_cols):
             made[u * unit : (u + 1) * unit, :] = augment(ref[...], 3)
         done_cols = done_cols + [made]
+    if raw_rows:
+        made = refs.pop(0)
+        for u, ref in enumerate(raw_rows):
+            made[u * unit : (u + 1) * unit, :] = augment(ref[...], 0)
+        done_rows = done_rows + [made]
     c_at = 0
     for col_ref in done_cols:
         for c0 in range(0, col_ref.shape[0], bn):
@@ -138,59 +139,83 @@
                 at += ref.shape[1]
             sum_ref[0:1, c_at : c_at + bn] = out
             c_at += bn
-
-
-def on_chip(body, shapes, name, limit, flops, *args):
-    moved = sum(math.prod(x.shape) * x.dtype.itemsize for x in args)
+    for ref in vectors:
+        width = ref.shape[0]
+        terms = []
+        for at in range(0, c_at, unit):
+            terms.extend(three_terms(sum_ref[0:1, at : at + unit]))
+        terms.append(jnp.zeros((16 - len(terms), unit), jnp.float32))
+        pack_ref[0:width, :] = ref[...]
+        pack_ref[width:, :] = jnp.concatenate(terms, axis=0).astype(jnp.bfloat16)
+
+
+def on_chip(body, shapes, name, limit, *args, scratch=()):
     return pl.pallas_call(
         body,
-        out_shape=shapes,
+        out_shape=tuple(shapes),
         in_specs=[VMEM_SPEC] * len(args),
         out_specs=tuple(VMEM_SPEC for _ in shapes),
+        scratch_shapes=list(scratch),
         compiler_params=pltpu.CompilerParams(vmem_limit_bytes=limit * MIB),
-        cost_estimate=pl.CostEstimate(
-            flops=int(flops), bytes_accessed=moved, transcendentals=0
-        ),
         name=name,
     )(*args)
 
 
-def kernel_tile(raw_rows, done_rows, raw_cols, done_cols, before, diagonal, name):
-    groups = [raw_rows, done_rows, raw_cols, done_cols, before]
+def kernel_tile(name, raw_rows, done_rows, raw_cols, done_cols, before=(), vectors=(), **kw):
+    diagonal = kw.get("diagonal", False)
+    groups = [raw_rows, done_rows, raw_cols, done_cols, before, vectors]
     unit, feats = (raw_rows + raw_cols)[0].shape
     wide = feats + 128
-    n_rows = sum(x.shape[0] for x in raw_rows + done_rows)
-    n_cols = sum(x.shape[0] for x in raw_cols + done_cols)
+    n_rows = unit * len(raw_rows) + sum(x.shape[0] for x in done_rows)
+    n_cols = unit * len(raw_cols) + sum(x.shape[0] for x in done_cols)
     scale = 2.0 * math.log2(math.e) / (1.05 * math.sqrt(feats))
     shapes = [
         pltpu.VMEM((n_rows, n_cols), jnp.float32),
         pltpu.VMEM((1, n_cols), jnp.float32),
     ]
-    for raw in (raw_rows, raw_cols):
-        if raw:
-            shapes.append(pltpu.VMEM((len(raw) * unit, wide), jnp.bfloat16))
-    body = functools.partial(
-        kernel_body, [len(g) for g in groups], unit, scale, diagonal, 256, 512
-    )
+    for x in vectors:
+        shapes.append(pltpu.VMEM((x.shape[0] + 16, unit), jnp.bfloat16))
+    scratch = []
+    if raw_cols:
+        shapes.append(pltpu.VMEM((len(raw_cols) * unit, wide), jnp.bfloat16))
+    if raw_rows:
+        made = pltpu.VMEM((len(raw_rows) * unit, wide), jnp.bfloat16)
+        (shapes if raw_cols else scratch).append(made)
+    counts = [len(g) for g in groups]
+    body = functools.partial(kernel_body, counts, unit, scale, diagonal, 256, 512)
     args = [x for g in groups for x in g]
-    return on_chip(body, tuple(shapes), name, 12, 4 * n_rows * n_cols * wide, *args)
-
-
-def density_body(n_cols, unit, points_all, *refs):
-    sums = refs[:n_cols]
-    vecs = refs[n_cols : 2 * n_cols]
-    inverse_ref, vec_all, log_ref = refs[2 * n_cols :]
-    width = vecs[0].shape[0]
+    return on_chip(body, shapes, name, 12, *args, scratch=scratch)
+
+
+def own_body(points_ref, vector_ref, row_ref, col_ref, copy_ref):
+    row_ref[...] = augment(points_ref[...], 0)
+    col_ref[...] = augment(points_ref[...], 3)
+    copy_ref[...] = vector_ref[...]
+
+
+def three_terms(x):
+    high = x.astype(jnp.bfloat16).astype(jnp.float32)
+    rest = x - high
+    middle = rest.astype(jnp.bfloat16).astype(jnp.float32)
+    return high, middle, rest - middle
+
+
+def density_body(unit, points_all, own_ref, packs, vec_all, inverse_ref, density_ref):
+    n_cols = len(packs)
+    width = packs[0].shape[0] - 16
+    given = [None] + [ref[width:, :].astype(jnp.float32) for ref in packs[1:]]
     for v in range(n_cols):
-        total = sums[0][:, v * unit : (v + 1) * unit]
+        cols = slice(v * unit, (v + 1) * unit)
+        total = own_ref[:, cols]
         for u in range(1, n_cols):
-            w = v ^ u
-            total = total + sums[u][:, w * unit : (w + 1) * unit]
+            w = 3 * (v ^ u)
+            row = given[u]
+            total = total + (row[w : w + 1] + (row[w + 1 : w + 2] + row[w + 2 : w + 3]))
         density = total / points_all
         if v == 0:
-            log_ref[...] = jnp.log(density)
-        inverse_ref[:, v * unit : (v + 1) * unit] = 1.0 / density
-        vec_all[0:width, v * unit : (v + 1) * unit] = vecs[v][...]
+            density_ref[...] = density
+        inverse_ref[:, cols] = 1.0 / density
+        vec_all[0:width, cols] = packs[v][0:width, :]
     ones = lax.broadcasted_iota(jnp.int32, (128 - width, n_cols * unit), 0) == 0
     vec_all[width:128, :] = jnp.where(ones, 1.0, 0.0).astype(jnp.bfloat16)
 
@@ -213,10 +238,10 @@
         out_ref[r : r + bm, :] = numer
 
 
-def first_product_body(n_cols, unit, points_all, bm, k_ref, *refs):
-    out_ref, *made = refs[2 * n_cols :]
-    density_body(n_cols, unit, points_all, *refs[: 2 * n_cols], *made)
-    product(out_ref, [k_ref], 0, k_ref.shape[0], made[0], made[1], bm)
+def first_product_body(unit, points_all, bm, k_ref, own_ref, *refs):
+    *packs, out_ref, vec_all, inverse_ref, density_ref = refs
+    density_body(unit, points_all, own_ref, packs, vec_all, inverse_ref, density_ref)
+    product(out_ref, [k_ref], 0, k_ref.shape[0], inverse_ref, vec_all, bm)
 
 
 def next_product_body(n_k, r0, bm, *refs):
@@ -233,19 +258,27 @@
     out_ref[...] = out.astype(jnp.bfloat16)
 
 
-def finish_body(own_ref, got_ref, far_ref, out_ref):
+def near_body(own_ref, got_ref, density_ref, out_ref, log_ref):
+    log_ref[...] = jnp.log(density_ref[...])
+    out_ref[...] = (own_ref[...] + got_ref[...]).T[0 : out_ref.shape[0], :]
+
+
+def finish_body(near_ref, far_ref, out_ref):
     width = out_ref.shape[0]
-    near = (own_ref[...] + got_ref[...]).T
     far = far_ref[...].astype(jnp.float32)
-    degree = near[width : width + 1, :] + (
+    degree = near_ref[width : width + 1, :] + (
         far[width : width + 1, :] + far[width + 1 : width + 2, :]
     )
-    out_ref[...] = (near[0:width, :] + far[0:width, :]) / degree
+    out_ref[...] = (near_ref[0:width, :] + far[0:width, :]) / degree
+
+
+def after(x, *others):
+    return lax.optimization_barrier((x, *others))[0]
 
 
 def grid_device(points, vectors):
     n_col = lax.axis_size("col")
-    unit = points.shape[0]
+    unit, feats = points.shape
     width = vectors.shape[1]
     points_all = float(unit * n_col * lax.axis_size("row"))
     n_units = n_col // 2
@@ -257,75 +290,89 @@
     def sibling(x):
         return lax.ppermute(x, "row", [(0, 1), (1, 0)])
 
+    far = across(points, n_units)
     beside = sibling(points)
-    far = across(points, n_units)
+    augmented = pltpu.VMEM((unit, feats + 128), jnp.bfloat16)
+    row_own, col_own, vec_own = on_chip(
+        own_body,
+        (augmented, augmented, pltpu.VMEM((width, unit), jnp.bfloat16)),
+        "own",
+        8,
+        points,
+        vectors.T,
+    )
     held = {0: points}
     bit = n_units // 2
     while bit:
         for u in list(held):
-            held[u | bit] = across(held[u], bit)
+            held[u | bit] = across(after(held[u], col_own) if u else held[u], bit)
         bit //= 2
-    cols = [held[u] for u in range(n_units)]
-    far_beside = sibling(far)
-    k_near, sums, rows_near, cols_near = kernel_tile(
-        [points, beside], [], cols[:-1], [], [], True, "near"
-    )
+    cols = [held[u] for u in range(1, n_units)]
+    k_near, sums_near, cols_near, row_beside = kernel_tile(
+        "near", [beside], [row_own], cols[:-1], [col_own], diagonal=True
+    )
+    far_beside = sibling(after(far, sums_near))
     k_last, sums_last, cols_last = kernel_tile(
-        [], [rows_near], cols[-1:], [], [], False, "last"
-    )
-    cols_all = [cols_near, cols_last]
-    k_far, sums, _ = kernel_tile([far], [], [], cols_all, [sums, sums_last], False, "far")
-    k_beside, sums, _ = kernel_tile(
-        [far_beside], [], [], cols_all, [sums], False, "far_beside"
-    )
-    vecs = [vectors.T] + [across(vectors.T, u) for u in range(1, n_units)]
-    all_sums = [sums] + [across(sums, u) for u in range(1, n_units)]
-
-    flops = 2 * unit * n_wide * 128
+        "last", [], [row_own, row_beside], cols[-1:], []
+    )
+    cols_all = [col_own, cols_near, cols_last]
+    k_far, sums = kernel_tile("far", [far], [], [], cols_all, [sums_near, sums_last])
+    k_beside, sums, pack = kernel_tile(
+        "far_beside", [far_beside], [], [], cols_all, [sums], [vec_own]
+    )
+    packs = [pack] + [across(pack, u) for u in range(1, n_units)]
+
     block = pltpu.VMEM((unit, 128), jnp.float32)
-    give_far, inverse, vec_all, log_density = on_chip(
-        functools.partial(first_product_body, n_units, unit, points_all, 256),
+    give_far, vec_all, inverse, density = on_chip(
+        functools.partial(first_product_body, unit, points_all, 256),
         (
             block,
+            pltpu.VMEM((128, n_wide), jnp.bfloat16),
             pltpu.VMEM((1, n_wide), jnp.float32),
-            pltpu.VMEM((128, n_wide), jnp.bfloat16),
-            jax.ShapeDtypeStruct((1, unit), jnp.float32),
+            pltpu.VMEM((1, unit), jnp.float32),
         ),
         "product_far_beside",
         8,
-        flops,
         k_beside,
-        *all_sums,
-        *vecs,
-    )
-
-    def next_product(ks, r0, name):
+        sums,
+        *packs,
+    )
+
+    def next_product(name, ks, r0):
         body = functools.partial(next_product_body, len(ks), r0, 256)
-        return on_chip(body, (block,), name, 8, flops, *ks, inverse, vec_all)[0]
+        return on_chip(body, (block,), name, 8, *ks, inverse, vec_all)[0]
 
     got_far = sibling(give_far)
-    keep_far = next_product([k_far], 0, "product_far")
+    keep_far = next_product("product_far", [k_far], 0)
     (away,) = on_chip(
         functools.partial(far_body, width),
         (pltpu.VMEM((width + 16, unit), jnp.bfloat16),),
         "sum_far",
         8,
-        1,
         keep_far,
         got_far,
     )
     back = across(away, n_units)
-    give = next_product([k_near, k_last], unit, "product_beside")
-    got = sibling(give)
-    keep = next_product([k_near, k_last], 0, "product_own")
+    got = sibling(next_product("product_beside", [k_near, k_last], unit))
+    keep = next_product("product_own", [k_near, k_last], 0)
+    near, log_density = on_chip(
+        near_body,
+        (
+            pltpu.VMEM((width + 8, unit), jnp.float32),
+            jax.ShapeDtypeStruct((1, unit), jnp.float32),
+        ),
+        "sum_near",
+        8,
+        keep,
+        got,
+        density,
+    )
     (smoothed,) = on_chip(
         finish_body,
         (jax.ShapeDtypeStruct((width, unit), jnp.float32),),
         "finish",
         8,
-        1,
-        keep,
-        got,
+        near,
         back,
     )
     return (smoothed.T, log_density.reshape(unit))
@@ -338,10 +385,12 @@
 
     def run(points, vectors):
         unit, feats = points.shape
-        paired = n_row == 2 and n_col >= 2 and n_col & (n_col - 1) == 0
+        paired = n_row == 2 and n_col >= 8 and n_col & (n_col - 1) == 0
         tile_bytes = 4 * (4 * unit) * (n_col // 2 * unit)
-        shaped = unit % 512 == 0 and feats == 128 and vectors.shape[1] <= 120
-        if paired and shaped and tile_bytes <= 16 * MIB:
+        width = vectors.shape[1]
+        shaped = unit % 512 == 0 and feats == 128 and width % 16 == 0 and width <= 112
+        few = 3 * (n_col // 2) <= 16
+        if paired and shaped and few and tile_bytes <= 16 * MIB:
             return grid_device(points, vectors)
         return plain_device(points, vectors)
 

time: 38.6 us -> 36 us (0.933)
  starting transfers between devices: 18 us -> 13.2 us
  waiting for transfers between devices: 9.52 us -> 11.4 us
  local copies, waits for them, and re-layouts: 0.91 us -> 1.78 us
  Pallas kernels: 9.32 us -> 8.65 us
    ppermute x11 -> x8, starting transfers between devices: 16.9 us -> 12.5 us  [across(): return lax.ppermute(x, 'col', [(i, i ^ mask) for i in range(n_col)])]
    ppermute x11 -> x8, waiting for transfers between devices: 9.51 us -> 11.4 us  [across(): return lax.ppermute(x, 'col', [(i, i ^ mask) for i in range(n_col)])]
    unnamed x4, local copies, waits for them, and re-layouts: 0.91 us -> 1.78 us
    pallas_call x10 -> x12, Pallas kernels: 9.32 us -> 8.65 us  [on_chip(): pl.pallas_call(body, out_shape=tuple(shapes), in_specs=[VMEM_SPEC] * len(...]
    ppermute x4, starting transfers between devices: 1.1 us -> 0.64 us  [sibling(): return lax.ppermute(x, 'row', [(0, 1), (1, 0)])]
  transfers between devices with their start and end apart: 15 -> 12, of which waited for: 7 -> 5; matrix products, arithmetic and copies ran while one was open for 0% -> 0% of each run, Pallas kernels for 19% -> 18%
where the time goes in v3:
time: 36 us; the launch traced here: 35.8 us
  starting transfers between devices  13.2 us (37%)
  waiting for transfers between devices  11.4 us (32%)
  Pallas kernels  8.65 us (24%)
  local copies, waits for them, and re-layouts  1.78 us (5%)
  between operations  0.75 us (2%)
    ppermute x8, starting transfers between devices, across(): return lax.ppermute(x, 'col', [(i, i ^ mask) for i in range(n_col)])  12.5 us
    ppermute x8, waiting for transfers between devices, across(): return lax.ppermute(x, 'col', [(i, i ^ mask) for i in range(n_col)])  11.4 us
    pallas_call x12, Pallas kernels, on_chip(): pl.pallas_call(body, out_shape=tuple(shapes), in_specs=[VMEM_SPEC] * len(...  8.65 us
    unnamed x4, local copies, waits for them, and re-layouts  1.78 us
  transfers between devices with their start and end apart: 12, of which 5 were waited for; matrix products, arithmetic and copies ran while one was open for 0% of the time, Pallas kernels for 18%

profile of v3, /device:TPU:0, one launch (start us, length us, event | category | flops | bytes accessed | tf_op | source)
XLA Modules:
  0.0 35.8 jit_solution(10631966623283167436)
XLA Ops:
  0.6 3.1 %collective-permute-start.2 = (bf16[512,128]{1,0:T(8,128)(2,1)}, bf16[512,128]{1,0:T(8,128)(2,1)S(1)}, u32[]{:S(2)}, u32[]{:S(2)}) collective-permute-start(bf16[512,128]{1,0:T(8,128)(2,1)} %points_ref.1), channel_id=1, source_target_pairs={{0,2},{1,3},{2,0},{3,1},{4,6},{5,7},{6,4},{7,5},{8,10},{9,11},{10,... | collective-permute-start | bytes 393224 | tf_op jit(solution)/shard_map/ppermute | solution.py:288
  3.7 1.5 %collective-permute-start.1 = (bf16[512,128]{1,0:T(8,128)(2,1)}, bf16[512,128]{1,0:T(8,128)(2,1)S(1)}, u32[]{:S(2)}, u32[]{:S(2)}) collective-permute-start(bf16[512,128]{1,0:T(8,128)(2,1)} %points_ref.1), channel_id=1, source_target_pairs={{0,1},{1,0},{2,3},{3,2},{4,5},{5,4},{6,7},{7,6},{8,9},{9,8},{10,11... | collective-permute-start | bytes 393224 | tf_op jit(solution)/shard_map/ppermute | solution.py:288
  5.2 2.6 %collective-permute-start.4 = (bf16[512,128]{1,0:T(8,128)(2,1)}, bf16[512,128]{1,0:T(8,128)(2,1)S(1)}, u32[]{:S(2)}, u32[]{:S(2)}) collective-permute-start(bf16[512,128]{1,0:T(8,128)(2,1)} %points_ref.1), channel_id=1, source_target_pairs={{0,4},{1,5},{2,6},{3,7},{4,0},{5,1},{6,2},{7,3},{8,12},{9,13},{10,... | collective-permute-start | bytes 393224 | tf_op jit(solution)/shard_map/ppermute | solution.py:288
  7.8 0.9 %copy-done = bf16[512,128]{1,0:T(8,128)(2,1)S(1)} copy-done((bf16[512,128]{1,0:T(8,128)(2,1)S(1)}, bf16[512,128]{1,0:T(8,128)(2,1)}, u32[]{:S(2)}) %copy-start) | copy-done | bytes 131096
  8.8 0.8 %copy-done.1 = bf16[512,64]{0,1:T(8,128)(2,1)S(1)} copy-done((bf16[512,64]{0,1:T(8,128)(2,1)S(1)}, bf16[512,64]{0,1:T(8,128)(2,1)}, u32[]{:S(2)}) %copy-start.1) | copy-done | bytes 65560
  9.6 0.4 %own.1 = (bf16[512,256]{1,0:T(8,128)(2,1)S(1)}, bf16[512,256]{1,0:T(8,128)(2,1)S(1)}, bf16[64,512]{1,0:T(8,128)(2,1)S(1)}) custom-call(bf16[512,128]{1,0:T(8,128)(2,1)S(1)} %copy-done, bf16[64,512]{1,0:T(8,128)(2,1)S(1)} %bitcast.3), custom_call_target="tpu_custom_call" | custom-call | tf_op jit(solution)/shard_map/own/pallas_call | solution.py:153
  10.0 0.6 %collective-permute-start.3 = (bf16[512,128]{1,0:T(8,128)(2,1)S(1)}, bf16[512,128]{1,0:T(8,128)(2,1)S(1)}, u32[]{:S(2)}, u32[]{:S(2)}) collective-permute-start(bf16[512,128]{1,0:T(8,128)(2,1)S(1)} %collective-permute-done.2.refs_3_), channel_id=1, source_target_pairs={{0,1},{1,0},{2,3},{3,2},{4,5},{5,4},{6,7},{7,6},{8,9},{9,8},{10,11... | collective-permute-start | bytes 393224 | tf_op jit(solution)/shard_map/ppermute | solution.py:288
  10.6 0.0 collective-permute-done.1.refs_2_
  10.6 0.0 collective-permute-done.refs_0_
  10.6 1.5 %near.1 = (f32[1024,1536]{1,0:T(8,128)S(1)}, f32[1,1536]{1,0:T(1,128)S(1)}, bf16[1024,256]{1,0:T(8,128)(2,1)S(1)}, bf16[512,256]{1,0:T(8,128)(2,1)S(1)}) custom-call(bf16[512,128]{1,0:T(8,128)(2,1)S(1)} %collective-permute-done.refs_0_, bf16[512,256]{1,0:T(8,128)(2,1)S(1)} %get-tuple-element.25.refs_1_.refs_0_, ...), custom_call_target="tpu_custom_call" | custom-call | tf_op jit(solution)/shard_map/near/pallas_call | solution.py:153
  12.1 3.0 %collective-permute-done.4.refs_0_ = bf16[512,128]{1,0:T(8,128)(2,1)S(1)} collective-permute-done((bf16[512,128]{1,0:T(8,128)(2,1)}, bf16[512,128]{1,0:T(8,128)(2,1)S(1)}, u32[]{:S(2)}, u32[]{:S(2)}) %collective-permute-start.4) | collective-permute-done | bytes 131104 | tf_op jit(solution)/shard_map/ppermute | solution.py:288
  15.0 0.0 collective-permute-start.5
  15.0 0.7 %collective-permute-done.3.refs_2_ = bf16[512,128]{1,0:T(8,128)(2,1)S(1)} collective-permute-done((bf16[512,128]{1,0:T(8,128)(2,1)S(1)}, bf16[512,128]{1,0:T(8,128)(2,1)S(1)}, u32[]{:S(2)}, u32[]{:S(2)}) %collective-permute-start.3) | collective-permute-done | bytes 131104 | tf_op jit(solution)/shard_map/ppermute | solution.py:288
  15.7 0.7 %last.1 = (f32[1024,512]{1,0:T(8,128)S(1)}, f32[1,512]{1,0:T(1,128)S(1)}, bf16[512,256]{1,0:T(8,128)(2,1)S(1)}) custom-call(bf16[512,256]{1,0:T(8,128)(2,1)S(1)} %get-tuple-element.25.refs_1_.refs_0_, bf16[512,256]{1,0:T(8,128)(2,1)S(1)} %get-tuple-element.28.refs_1_, bf16[512,128]{1,0:T(8,128)(2,1)S(1)} %collective-permute-done.3.refs_2_), custom_call_target="tpu_custom_call" | custom-call | tf_op jit(solution)/shard_map/last/pallas_call | solution.py:153
  16.4 0.9 %far.1 = (f32[512,2048]{1,0:T(8,128)S(1)}, f32[1,2048]{1,0:T(1,128)S(1)}) custom-call(bf16[512,128]{1,0:T(8,128)(2,1)S(1)} %collective-permute-done.4.refs_0_, bf16[512,256]{1,0:T(8,128)(2,1)S(1)} %get-tuple-element.26.refs_4_.refs_1_, bf16[1024,256]{1,0:T(8,128)(2,1)S(1)} %get-tuple-element.33.refs_2_, bf16[512,256]{1,0:T(8,128)(2,1)S(1)} %get-tuple-element.34.refs_3_, ...), custom_call_target="tpu_custom_call" | custom-call | tf_op jit(solution)/shard_map/far/pallas_call | solution.py:153
  17.3 0.9 %far_beside.1 = (f32[512,2048]{1,0:T(8,128)S(1)}, f32[1,2048]{1,0:T(1,128)S(1)}, bf16[80,512]{1,0:T(8,128)(2,1)S(1)}) custom-call(bf16[512,128]{1,0:T(8,128)(2,1)S(1)} %collective-permute-done.5.refs_0_, bf16[512,256]{1,0:T(8,128)(2,1)S(1)} %get-tuple-element.26.refs_4_.refs_1_, bf16[1024,256]{1,0:T(8,128)(2,1)S(1)} %get-tuple-element.33.refs_2_, ...), custom_call_target="tpu_custom_call" | custom-call | tf_op jit(solution)/shard_map/far_beside/pallas_call | solution.py:153
  18.3 0.5 %collective-permute-start.8 = (bf16[80,512]{1,0:T(8,128)(2,1)S(1)}, bf16[80,512]{1,0:T(8,128)(2,1)S(1)}, u32[]{:S(2)}, u32[]{:S(2)}) collective-permute-start(bf16[80,512]{1,0:T(8,128)(2,1)S(1)} %get-tuple-element.40.refs_0_), channel_id=1, source_target_pairs={{0,3},{1,2},{2,1},{3,0},{4,7},{5,6},{6,5},{7,4},{8,11},{9,10},{10,... | collective-permute-start | bytes 245768 | tf_op jit(solution)/shard_map/ppermute | solution.py:288
  18.7 1.6 %collective-permute-start.7 = (bf16[80,512]{1,0:T(8,128)(2,1)S(1)}, bf16[80,512]{1,0:T(8,128)(2,1)S(1)}, u32[]{:S(2)}, u32[]{:S(2)}) collective-permute-start(bf16[80,512]{1,0:T(8,128)(2,1)S(1)} %get-tuple-element.40.refs_0_), channel_id=1, source_target_pairs={{0,2},{1,3},{2,0},{3,1},{4,6},{5,7},{6,4},{7,5},{8,10},{9,11},{10,... | collective-permute-start | bytes 245768 | tf_op jit(solution)/shard_map/ppermute | solution.py:288
  20.3 1.5 %collective-permute-start.6 = (bf16[80,512]{1,0:T(8,128)(2,1)S(1)}, bf16[80,512]{1,0:T(8,128)(2,1)S(1)}, u32[]{:S(2)}, u32[]{:S(2)}) collective-permute-start(bf16[80,512]{1,0:T(8,128)(2,1)S(1)} %get-tuple-element.40.refs_0_), channel_id=1, source_target_pairs={{0,1},{1,0},{2,3},{3,2},{4,5},{5,4},{6,7},{7,6},{8,9},{9,8},{10,11... | collective-permute-start | bytes 245768 | tf_op jit(solution)/shard_map/ppermute | solution.py:288
  21.8 2.5 %collective-permute-done.8.refs_3_ = bf16[80,512]{1,0:T(8,128)(2,1)S(1)} collective-permute-done((bf16[80,512]{1,0:T(8,128)(2,1)S(1)}, bf16[80,512]{1,0:T(8,128)(2,1)S(1)}, u32[]{:S(2)}, u32[]{:S(2)}) %collective-permute-start.8) | collective-permute-done | bytes 81952 | tf_op jit(solution)/shard_map/ppermute | solution.py:288
  24.4 0.9 %collective-permute-done.6.refs_1_ = bf16[80,512]{1,0:T(8,128)(2,1)S(1)} collective-permute-done((bf16[80,512]{1,0:T(8,128)(2,1)S(1)}, bf16[80,512]{1,0:T(8,128)(2,1)S(1)}, u32[]{:S(2)}, u32[]{:S(2)}) %collective-permute-start.6) | collective-permute-done | bytes 81952 | tf_op jit(solution)/shard_map/ppermute | solution.py:288
  25.2 0.7 %product_far_beside.1 = (f32[512,128]{1,0:T(8,128)S(1)}, bf16[128,2048]{1,0:T(8,128)(2,1)S(1)}, f32[1,2048]{1,0:T(1,128)S(1)}, f32[1,512]{1,0:T(1,128)S(1)}) custom-call(f32[512,2048]{1,0:T(8,128)S(1)} %get-tuple-element.38.k_ref, f32[1,2048]{1,0:T(1,128)S(1)} %get-tuple-element.39.own_ref, bf16[80,512]{1,0:T(8,128)(2,1)S(1)} %get-tuple-element.40.refs_0_, ...), custom_call_target="tpu_custom_call" | custom-call | tf_op jit(solution)/shard_map/product_far_beside/pallas_call | solution.py:153
  25.9 0.1 collective-permute-start.10
  26.0 0.7 %product_beside.1 = f32[512,128]{1,0:T(8,128)S(1)} custom-call(f32[1024,1536]{1,0:T(8,128)S(1)} %get-tuple-element.27.refs_0_, f32[1024,512]{1,0:T(8,128)S(1)} %get-tuple-element.30.refs_1_, f32[1,2048]{1,0:T(1,128)S(1)} %get-tuple-element.41.refs_2_.refs_1_, bf16[128,2048]{1,0:T(8,128)(2,1)S(1)} %get-tuple-element.42.refs_3_.refs_2_), custom_call_target="tpu_custom_call" | custom-call | tf_op jit(solution)/shard_map/product_beside/pallas_call | solution.py:153
  26.7 0.6 %collective-permute-start.9 = (f32[512,128]{1,0:T(8,128)S(1)}, f32[512,128]{1,0:T(8,128)S(1)}, u32[]{:S(2)}, u32[]{:S(2)}) collective-permute-start(f32[512,128]{1,0:T(8,128)S(1)} %product_beside.1), channel_id=1, source_target_pairs={{0,8},{8,0},{1,9},{9,1},{2,10},{10,2},{3,11},{11,3},{4,12},{12,4},... | collective-permute-start | bytes 786440 | tf_op jit(solution)/shard_map/ppermute | solution.py:291
  27.3 0.7 %product_far.1.keep_ref = f32[512,128]{1,0:T(8,128)S(1)} custom-call(f32[512,2048]{1,0:T(8,128)S(1)} %get-tuple-element.45.refs_0_, f32[1,2048]{1,0:T(1,128)S(1)} %get-tuple-element.41.refs_2_.refs_1_, bf16[128,2048]{1,0:T(8,128)(2,1)S(1)} %get-tuple-element.42.refs_3_.refs_2_), custom_call_target="tpu_custom_call" | custom-call | tf_op jit(solution)/shard_map/product_far/pallas_call | solution.py:153
  28.0 0.1 sum_far.1
  28.1 1.2 %collective-permute-start.11 = (bf16[80,512]{1,0:T(8,128)(2,1)S(1)}, bf16[80,512]{1,0:T(8,128)(2,1)S(1)}, u32[]{:S(2)}, u32[]{:S(2)}) collective-permute-start(bf16[80,512]{1,0:T(8,128)(2,1)S(1)} %sum_far.1), channel_id=1, source_target_pairs={{0,4},{1,5},{2,6},{3,7},{4,0},{5,1},{6,2},{7,3},{8,12},{9,13},{10,... | collective-permute-start | bytes 245768 | tf_op jit(solution)/shard_map/ppermute | solution.py:288
  29.4 0.7 %product_own.1.own_ref = f32[512,128]{1,0:T(8,128)S(1)} custom-call(f32[1024,1536]{1,0:T(8,128)S(1)} %get-tuple-element.27.refs_0_, f32[1024,512]{1,0:T(8,128)S(1)} %get-tuple-element.30.refs_1_, f32[1,2048]{1,0:T(1,128)S(1)} %get-tuple-element.41.refs_2_.refs_1_, bf16[128,2048]{1,0:T(8,128)(2,1)S(1)} %get-tuple-element.42.refs_3_.refs_2_), custom_call_target="tpu_custom_call" | custom-call | tf_op jit(solution)/shard_map/product_own/pallas_call | solution.py:153
  30.1 0.6 %sum_near.1 = (f32[72,512]{1,0:T(8,128)S(1)}, f32[1,512]{1,0:T(1,128)}) custom-call(f32[512,128]{1,0:T(8,128)S(1)} %product_own.1.own_ref, f32[512,128]{1,0:T(8,128)S(1)} %collective-permute-done.9.got_ref, f32[1,512]{1,0:T(1,128)S(1)} %get-tuple-element.43.density_ref), custom_call_target="tpu_custom_call" | custom-call | tf_op jit(solution)/shard_map/sum_near/pallas_call | solution.py:153
  30.7 4.4 %collective-permute-done.11.far_ref = bf16[80,512]{1,0:T(8,128)(2,1)S(1)} collective-permute-done((bf16[80,512]{1,0:T(8,128)(2,1)S(1)}, bf16[80,512]{1,0:T(8,128)(2,1)S(1)}, u32[]{:S(2)}, u32[]{:S(2)}) %collective-permute-start.11) | collective-permute-done | bytes 81952 | tf_op jit(solution)/shard_map/ppermute | solution.py:288
  35.1 0.7 %finish.1 = f32[64,512]{1,0:T(8,128)} custom-call(f32[72,512]{1,0:T(8,128)S(1)} %get-tuple-element.44.near_ref, bf16[80,512]{1,0:T(8,128)(2,1)S(1)} %collective-permute-done.11.far_ref), custom_call_target="tpu_custom_call" | custom-call | tf_op jit(solution)/shard_map/finish/pallas_call | solution.py:153
  (8 shorter events, 0.0 us)
Async XLA Ops:
  0.6 9.4 %collective-permute-start.2 = (bf16[512,128]{1,0:T(8,128)(2,1)}, bf16[512,128]{1,0:T(8,128)(2,1)S(1)}, u32[]{:S(2)}, u32[]{:S(2)}) collective-permute-start(bf16[512,128]{1,0:T(8,128)(2,1)} %points_ref.1), channel_id=1, source_target_pairs={{0,2},{1,3},{2,0},{3,1},{4,6},{5,7},{6,4},{7,5},{8,10},{9,11},{10,... | collective-permute-start | bytes 393224 | tf_op jit(solution)/shard_map/ppermute | solution.py:288
  3.7 6.9 %collective-permute-start.1 = (bf16[512,128]{1,0:T(8,128)(2,1)}, bf16[512,128]{1,0:T(8,128)(2,1)S(1)}, u32[]{:S(2)}, u32[]{:S(2)}) collective-permute-start(bf16[512,128]{1,0:T(8,128)(2,1)} %points_ref.1), channel_id=1, source_target_pairs={{0,1},{1,0},{2,3},{3,2},{4,5},{5,4},{6,7},{7,6},{8,9},{9,8},{10,11... | collective-permute-start | bytes 393224 | tf_op jit(solution)/shard_map/ppermute | solution.py:288
  5.2 5.3 %collective-permute-start = (bf16[512,128]{1,0:T(8,128)(2,1)}, bf16[512,128]{1,0:T(8,128)(2,1)S(1)}, u32[]{:S(2)}, u32[]{:S(2)}) collective-permute-start(bf16[512,128]{1,0:T(8,128)(2,1)} %points_ref.1), channel_id=1, source_target_pairs={{0,8},{8,0},{1,9},{9,1},{2,10},{10,2},{3,11},{11,3},{4,12},{12,4},... | collective-permute-start | bytes 393224 | tf_op jit(solution)/shard_map/ppermute | solution.py:291
  5.2 9.8 %collective-permute-start.4 = (bf16[512,128]{1,0:T(8,128)(2,1)}, bf16[512,128]{1,0:T(8,128)(2,1)S(1)}, u32[]{:S(2)}, u32[]{:S(2)}) collective-permute-start(bf16[512,128]{1,0:T(8,128)(2,1)} %points_ref.1), channel_id=1, source_target_pairs={{0,4},{1,5},{2,6},{3,7},{4,0},{5,1},{6,2},{7,3},{8,12},{9,13},{10,... | collective-permute-start | bytes 393224 | tf_op jit(solution)/shard_map/ppermute | solution.py:288
  7.8 0.9 %copy-start = (bf16[512,128]{1,0:T(8,128)(2,1)S(1)}, bf16[512,128]{1,0:T(8,128)(2,1)}, u32[]{:S(2)}) copy-start(bf16[512,128]{1,0:T(8,128)(2,1)} %points_ref.1) | copy-start | bytes 393220
  8.8 0.8 %copy-start.1 = (bf16[512,64]{0,1:T(8,128)(2,1)S(1)}, bf16[512,64]{0,1:T(8,128)(2,1)}, u32[]{:S(2)}) copy-start(bf16[512,64]{0,1:T(8,128)(2,1)} %param.3) | copy-start | bytes 196612
  10.0 5.7 %collective-permute-start.3 = (bf16[512,128]{1,0:T(8,128)(2,1)S(1)}, bf16[512,128]{1,0:T(8,128)(2,1)S(1)}, u32[]{:S(2)}, u32[]{:S(2)}) collective-permute-start(bf16[512,128]{1,0:T(8,128)(2,1)S(1)} %collective-permute-done.2.refs_3_), channel_id=1, source_target_pairs={{0,1},{1,0},{2,3},{3,2},{4,5},{5,4},{6,7},{7,6},{8,9},{9,8},{10,11... | collective-permute-start | bytes 393224 | tf_op jit(solution)/shard_map/ppermute | solution.py:288
  15.0 2.3 %collective-permute-start.5 = (bf16[512,128]{1,0:T(8,128)(2,1)S(1)}, bf16[512,128]{1,0:T(8,128)(2,1)S(1)}, u32[]{:S(2)}, u32[]{:S(2)}) collective-permute-start(bf16[512,128]{1,0:T(8,128)(2,1)S(1)} %collective-permute-done.4.refs_0_), channel_id=1, source_target_pairs={{0,8},{8,0},{1,9},{9,1},{2,10},{10,2},{3,11},{11,3},{4,12},{12,4},... | collective-permute-start | bytes 393224 | tf_op jit(solution)/shard_map/ppermute | solution.py:291
  18.3 6.1 %collective-permute-start.8 = (bf16[80,512]{1,0:T(8,128)(2,1)S(1)}, bf16[80,512]{1,0:T(8,128)(2,1)S(1)}, u32[]{:S(2)}, u32[]{:S(2)}) collective-permute-start(bf16[80,512]{1,0:T(8,128)(2,1)S(1)} %get-tuple-element.40.refs_0_), channel_id=1, source_target_pairs={{0,3},{1,2},{2,1},{3,0},{4,7},{5,6},{6,5},{7,4},{8,11},{9,10},{10,... | collective-permute-start | bytes 245768 | tf_op jit(solution)/shard_map/ppermute | solution.py:288
  18.7 5.6 %collective-permute-start.7 = (bf16[80,512]{1,0:T(8,128)(2,1)S(1)}, bf16[80,512]{1,0:T(8,128)(2,1)S(1)}, u32[]{:S(2)}, u32[]{:S(2)}) collective-permute-start(bf16[80,512]{1,0:T(8,128)(2,1)S(1)} %get-tuple-element.40.refs_0_), channel_id=1, source_target_pairs={{0,2},{1,3},{2,0},{3,1},{4,6},{5,7},{6,4},{7,5},{8,10},{9,11},{10,... | collective-permute-start | bytes 245768 | tf_op jit(solution)/shard_map/ppermute | solution.py:288
  20.3 4.9 %collective-permute-start.6 = (bf16[80,512]{1,0:T(8,128)(2,1)S(1)}, bf16[80,512]{1,0:T(8,128)(2,1)S(1)}, u32[]{:S(2)}, u32[]{:S(2)}) collective-permute-start(bf16[80,512]{1,0:T(8,128)(2,1)S(1)} %get-tuple-element.40.refs_0_), channel_id=1, source_target_pairs={{0,1},{1,0},{2,3},{3,2},{4,5},{5,4},{6,7},{7,6},{8,9},{9,8},{10,11... | collective-permute-start | bytes 245768 | tf_op jit(solution)/shard_map/ppermute | solution.py:288
  25.9 2.1 %collective-permute-start.10 = (f32[512,128]{1,0:T(8,128)S(1)}, f32[512,128]{1,0:T(8,128)S(1)}, u32[]{:S(2)}, u32[]{:S(2)}) collective-permute-start(f32[512,128]{1,0:T(8,128)S(1)} %get-tuple-element.46), channel_id=1, source_target_pairs={{0,8},{8,0},{1,9},{9,1},{2,10},{10,2},{3,11},{11,3},{4,12},{12,4},... | collective-permute-start | bytes 786440 | tf_op jit(solution)/shard_map/ppermute | solution.py:291
  26.7 3.3 %collective-permute-start.9 = (f32[512,128]{1,0:T(8,128)S(1)}, f32[512,128]{1,0:T(8,128)S(1)}, u32[]{:S(2)}, u32[]{:S(2)}) collective-permute-start(f32[512,128]{1,0:T(8,128)S(1)} %product_beside.1), channel_id=1, source_target_pairs={{0,8},{8,0},{1,9},{9,1},{2,10},{10,2},{3,11},{11,3},{4,12},{12,4},... | collective-permute-start | bytes 786440 | tf_op jit(solution)/shard_map/ppermute | solution.py:291
  28.1 7.0 %collective-permute-start.11 = (bf16[80,512]{1,0:T(8,128)(2,1)S(1)}, bf16[80,512]{1,0:T(8,128)(2,1)S(1)}, u32[]{:S(2)}, u32[]{:S(2)}) collective-permute-start(bf16[80,512]{1,0:T(8,128)(2,1)S(1)} %sum_far.1), channel_id=1, source_target_pairs={{0,4},{1,5},{2,6},{3,7},{4,0},{5,1},{6,2},{7,3},{8,12},{9,13},{10,... | collective-permute-start | bytes 245768 | tf_op jit(solution)/shard_map/ppermute | solution.py:288

commit v4 on v3

v4 whole, which is shorter than its diff:
```python
import functools
import math

import jax
import jax.numpy as jnp
from jax import lax
from jax.experimental import pallas as pl
from jax.experimental.pallas import tpu as pltpu
from jax.sharding import PartitionSpec as P

MIB = 2**20
NT = (((1,), (1,)), ((), ()))
VMEM_SPEC = pl.BlockSpec(memory_space=pltpu.VMEM)


def by_blocks(piece, tile_fn):
    count = piece.shape[0]
    size = 512
    groups = piece.reshape(count // size, size, piece.shape[1])
    firsts = jnp.arange(count // size, dtype=jnp.int32) * size
    return lax.map(lambda item: tile_fn(item[0], item[1]), (groups, firsts))


def plain_device(points, vectors):
    rows_dev = points.shape[0]
    feats = points.shape[1]
    n_col = lax.axis_size("col")
    n_row = lax.axis_size("row")
    half = rows_dev * n_col
    total_pts = half * n_row
    row_pos = lax.axis_index("row")
    col_pos = lax.axis_index("col")
    width = 1.05 * math.sqrt(feats)
    col_points = lax.all_gather(points, "row", axis=0, tiled=True)
    col_vectors = lax.all_gather(vectors, "row", axis=0, tiled=True)
    local = jnp.arange(n_row * rows_dev, dtype=jnp.int32)
    col_ids = local // rows_dev * half + col_pos * rows_dev + local % rows_dev
    col_norms = jnp.sum(col_points.astype(jnp.float32) ** 2, axis=1)
    row_base = row_pos * half
    piece = lax.all_gather(points, "col", axis=0, tiled=True)

    def kernel_tile(block, first):
        norms = jnp.sum(block.astype(jnp.float32) ** 2, axis=1)
        cross = lax.dot_general(block, col_points, NT, preferred_element_type=jnp.float32)
        dist = norms[:, None] + col_norms[None, :] - 2.0 * cross
        values = jnp.exp((2.0 * feats - dist) / width)
        rows = row_base + first + jnp.arange(block.shape[0], dtype=jnp.int32)
        return jnp.where(rows[:, None] == col_ids[None, :], jnp.zeros_like(values), values)

    sums = by_blocks(piece, lambda block, first: jnp.sum(kernel_tile(block, first), axis=1))
    own_sums = lax.psum_scatter(sums.reshape(-1), "col", scatter_dimension=0, tiled=True)
    own_density = own_sums / total_pts
    col_density = lax.all_gather(own_density, "row", axis=0, tiled=True)

    def product_tile(block, first):
        weight = kernel_tile(block, first) / col_density[None, :]
        degree = jnp.sum(weight, axis=1)
        numer = jnp.dot(
            weight.astype(jnp.bfloat16), col_vectors, preferred_element_type=jnp.float32
        )
        return (numer, degree)

    numer, degree = by_blocks(piece, product_tile)
    numer = numer.reshape(piece.shape[0], vectors.shape[1])
    numer_own = lax.psum_scatter(numer, "col", scatter_dimension=0, tiled=True)
    degree_own = lax.psum_scatter(
        degree.reshape(-1), "col", scatter_dimension=0, tiled=True
    )
    return (numer_own / degree_own[:, None], jnp.log(own_density))


def augment(pts, first):
    count, feats = pts.shape
    square = pts.astype(jnp.float32)
    square = square * square
    high = square.astype(jnp.bfloat16)
    low = (square - high.astype(jnp.float32)).astype(jnp.bfloat16)
    pair = jnp.concatenate([high, low], axis=1)
    norm = jnp.dot(
        pair, jnp.ones((2 * feats, 128), jnp.bfloat16), preferred_element_type=jnp.float32
    )
    q = 0.5 * feats - 0.5 * norm
    q0 = q.astype(jnp.bfloat16).astype(jnp.float32)
    rest = q - q0
    q1 = rest.astype(jnp.bfloat16).astype(jnp.float32)
    q2 = rest - q1
    lane = lax.broadcasted_iota(jnp.int32, (count, 128), 1)
    other = 3 - first
    extra = jnp.where((lane >= other) & (lane < other + 3), 1.0, 0.0)
    extra = jnp.where(lane == first + 2, q2, extra)
    extra = jnp.where(lane == first + 1, q1, extra)
    extra = jnp.where(lane == first, q0, extra)
    return jnp.concatenate([pts, extra.astype(jnp.bfloat16)], axis=1)


def kernel_body(counts, unit, scale, diagonal, bm, bn, *refs):
    refs = list(refs)
    raw_rows, done_rows, raw_cols, done_cols, before, ahead = [
        [refs.pop(0) for _ in range(count)] for count in counts
    ]
    k_ref, sum_ref = refs.pop(0), refs.pop(0)
    if raw_rows:
        made = refs.pop(0)
        for u, ref in enumerate(raw_rows):
            made[u * unit : (u + 1) * unit, :] = augment(ref[...], 0)
        done_rows = done_rows + [made]
    if raw_cols:
        made = refs.pop(0)
        for u, ref in enumerate(raw_cols):
            made[u * unit : (u + 1) * unit, :] = augment(ref[...], 3)
        done_cols = done_cols + [made]
    skip = 0
    for ref in ahead:
        sum_ref[0:1, skip : skip + ref.shape[1]] = ref[...]
        skip += ref.shape[1]
    c_at = 0
    for col_ref in done_cols:
        for c0 in range(0, col_ref.shape[0], bn):
            total = jnp.zeros((8, bn), jnp.float32)
            r_at = 0
            for row_ref in done_rows:
                for r0 in range(0, row_ref.shape[0], bm):
                    half_log = lax.dot_general(
                        row_ref[r0 : r0 + bm, :],
                        col_ref[c0 : c0 + bn, :],
                        NT,
                        preferred_element_type=jnp.float32,
                    )
                    value = jnp.exp2(half_log * scale)
                    if diagonal and r_at // unit == 0 and c_at // unit == 0:
                        i = lax.broadcasted_iota(jnp.int32, (bm, bn), 0) + r_at
                        j = lax.broadcasted_iota(jnp.int32, (bm, bn), 1) + c_at
                        value = jnp.where(i == j, 0.0, value)
                    k_ref[r_at : r_at + bm, c_at : c_at + bn] = value
                    total = total + jnp.sum(value.reshape(bm // 8, 8, bn), axis=0)
                    r_at += bm
            out = jnp.sum(total, axis=0, keepdims=True)
            at = 0
            for ref in before:
                if at <= c_at < at + ref.shape[1]:
                    out = out + ref[:, c_at - at : c_at - at + bn]
                at += ref.shape[1]
            sum_ref[0:1, skip + c_at : skip + c_at + bn] = out
            c_at += bn


def on_chip(body, shapes, name, limit, *args, scratch=()):
    return pl.pallas_call(
        body,
        out_shape=tuple(shapes),
        in_specs=[VMEM_SPEC] * len(args),
        out_specs=tuple(VMEM_SPEC for _ in shapes),
        scratch_shapes=list(scratch),
        compiler_params=pltpu.CompilerParams(vmem_limit_bytes=limit * MIB),
        name=name,
    )(*args)


def kernel_tile(
    name, raw_rows, done_rows, raw_cols, done_cols, before=(), ahead=(), diagonal=False
):
    groups = [raw_rows, done_rows, raw_cols, done_cols, before, ahead]
    unit, feats = (raw_rows + raw_cols)[0].shape
    wide = feats + 128
    n_rows = unit * len(raw_rows) + sum(x.shape[0] for x in done_rows)
    n_cols = unit * len(raw_cols) + sum(x.shape[0] for x in done_cols)
    scale = 2.0 * math.log2(math.e) / (1.05 * math.sqrt(feats))
    shapes = [
        pltpu.VMEM((n_rows, n_cols), jnp.float32),
        pltpu.VMEM((1, n_cols + sum(x.shape[1] for x in ahead)), jnp.float32),
    ]
    scratch = []
    for raw in (raw_rows, raw_cols):
        if raw:
            made = pltpu.VMEM((len(raw) * unit, wide), jnp.bfloat16)
            (scratch if ahead else shapes).append(made)
    counts = [len(g) for g in groups]
    body = functools.partial(kernel_body, counts, unit, scale, diagonal, 256, 512)
    args = [x for g in groups for x in g]
    return on_chip(body, shapes, name, 12, *args, scratch=scratch)


def own_body(points_ref, vector_ref, row_ref, col_ref, copy_ref):
    row_ref[...] = augment(points_ref[...], 0)
    col_ref[...] = augment(points_ref[...], 3)
    copy_ref[...] = vector_ref[...]


def vectors_body(*refs):
    *vecs, vec_all = refs
    width, unit = vecs[0].shape
    for v, ref in enumerate(vecs):
        vec_all[0:width, v * unit : (v + 1) * unit] = ref[...]
    ones = lax.broadcasted_iota(jnp.int32, (128 - width, len(vecs) * unit), 0) == 0
    vec_all[width:128, :] = jnp.where(ones, 1.0, 0.0).astype(jnp.bfloat16)


def density_body(unit, points_all, sums, inverse_ref, density_ref):
    n_cols = len(sums)
    for v in range(n_cols):
        cols = slice(v * unit, (v + 1) * unit)
        total = sums[0][:, cols]
        for u in range(1, n_cols):
            w = v ^ u
            total = total + sums[u][:, w * unit : (w + 1) * unit]
        density = total / points_all
        if v == 0:
            density_ref[...] = density
        inverse_ref[:, cols] = 1.0 / density


def product(k_refs, firsts, r, bm, inverse_ref, vec_all):
    numer = None
    at = 0
    for k_ref, first in zip(k_refs, firsts):
        cols = slice(at, at + k_ref.shape[1])
        weight = k_ref[first + r : first + r + bm, :] * inverse_ref[:, cols]
        part = lax.dot_general(
            weight.astype(jnp.bfloat16),
            vec_all[:, cols],
            NT,
            preferred_element_type=jnp.float32,
        )
        numer = part if numer is None else numer + part
        at += k_ref.shape[1]
    return numer.T


def give(out_ref, k_refs, firsts, inverse_ref, vec_all, bm):
    width = out_ref.shape[0] - 16
    for r in range(0, out_ref.shape[1], bm):
        numer = product(k_refs, firsts, r, bm, inverse_ref, vec_all)
        degree = numer[width : width + 1, :]
        high = degree.astype(jnp.bfloat16).astype(jnp.float32)
        zero = jnp.zeros((14, bm), jnp.float32)
        tail = jnp.concatenate([high, degree - high, zero], axis=0)
        out_ref[0:width, r : r + bm] = numer[0:width, :].astype(jnp.bfloat16)
        out_ref[width:, r : r + bm] = tail.astype(jnp.bfloat16)


def first_give_body(unit, points_all, first, bm, n_sums, k_near, k_side, vec_all, *refs):
    sums = refs[:n_sums]
    out_ref, inverse_ref, density_ref = refs[n_sums:]
    density_body(unit, points_all, sums, inverse_ref, density_ref)
    give(out_ref, [k_near, k_side], [first, first], inverse_ref, vec_all, bm)


def next_give_body(firsts, bm, *refs):
    *k_refs, vec_all, inverse_ref, out_ref = refs
    give(out_ref, k_refs, firsts, inverse_ref, vec_all, bm)


def keep_body(bm, *refs):
    *k_refs, vec_all, inverse_ref, density_ref, out_ref, log_ref = refs
    height, unit = out_ref.shape
    firsts = [0] * len(k_refs)
    for r in range(0, unit, bm):
        numer = product(k_refs, firsts, r, bm, inverse_ref, vec_all)
        out_ref[:, r : r + bm] = numer[0:height, :]
    log_ref[...] = jnp.log(density_ref[...])


def finish_body(near_ref, *refs):
    *far_refs, out_ref = refs
    width = out_ref.shape[0]
    numer = near_ref[0:width, :]
    degree = near_ref[width : width + 1, :]
    for ref in far_refs:
        far = ref[...].astype(jnp.float32)
        numer = numer + far[0:width, :]
        degree = degree + (far[width : width + 1, :] + far[width + 1 : width + 2, :])
    out_ref[...] = numer / degree


def after(x, *others):
    return lax.optimization_barrier((x, *others))[0]


def grid_device(points, vectors):
    n_col = lax.axis_size("col")
    unit, feats = points.shape
    width = vectors.shape[1]
    points_all = float(unit * n_col * lax.axis_size("row"))
    n_units = n_col // 2

    def across(x, mask):
        return lax.ppermute(x, "col", [(i, i ^ mask) for i in range(n_col)])

    def sibling(x):
        return lax.ppermute(x, "row", [(0, 1), (1, 0)])

    far = across(points, n_units)
    beside = sibling(points)
    augmented = pltpu.VMEM((unit, feats + 128), jnp.bfloat16)
    vec = vectors.T
    row_own, col_own, vec_own = on_chip(
        own_body,
        (augmented, augmented, pltpu.VMEM((width, unit), jnp.bfloat16)),
        "own",
        8,
        points,
        vec,
    )
    held = {0: points}
    bit = n_units // 2
    while bit:
        for u in list(held):
            held[u | bit] = across(held[u], bit)
        bit //= 2
    rows = [held[u] for u in range(1, n_units)]
    far_beside = sibling(after(far, col_own))
    n_wide = 4 * unit

    vec_far = across(after(vec, far), n_units)
    k_near, sums_near, rows_near, cols_near = kernel_tile(
        "near", rows[:-1], [row_own], [beside, far], [col_own], diagonal=True
    )
    k_last, sums_last, row_last = kernel_tile(
        "last", rows[-1:], [], [], [col_own, cols_near], [sums_near]
    )
    k_side, sums = kernel_tile(
        "side", [], [row_own, rows_near, row_last], [far_beside], [], [], [sums_last]
    )
    sums_far = across(sums, n_units)
    all_sums = [sums, sibling(sums), sums_far, sibling(sums_far)]

    vecs = [vec_own, sibling(vec), vec_far, sibling(after(vec_far, sums_far))]
    (vec_all,) = on_chip(
        vectors_body, (pltpu.VMEM((128, n_wide), jnp.bfloat16),), "vectors", 4, *vecs
    )

    packed = pltpu.VMEM((width + 16, unit), jnp.bfloat16)
    away, inverse, density = on_chip(
        functools.partial(first_give_body, unit, points_all, unit, 256, len(all_sums)),
        (
            packed,
            pltpu.VMEM((1, n_wide), jnp.float32),
            pltpu.VMEM((1, unit), jnp.float32),
        ),
        "give_first",
        8,
        k_near,
        k_side,
        vec_all,
        *all_sums,
    )
    back = [across(away, 1)]
    for u in range(2, n_units):
        last = u == n_units - 1
        (away,) = on_chip(
            functools.partial(next_give_body, [0 if last else u * unit, u * unit], 256),
            (packed,),
            "give",
            8,
            k_last if last else k_near,
            k_side,
            vec_all,
            after(inverse, away),
        )
        back.append(across(away, u))
    near, log_density = on_chip(
        functools.partial(keep_body, 256),
        (
            pltpu.VMEM((width + 8, unit), jnp.float32),
            jax.ShapeDtypeStruct((1, unit), jnp.float32),
        ),
        "keep",
        8,
        k_near,
        k_side,
        vec_all,
        inverse,
        density,
    )
    (smoothed,) = on_chip(
        finish_body,
        (jax.ShapeDtypeStruct((width, unit), jnp.float32),),
        "finish",
        8,
        near,
        *back,
    )
    return (smoothed.T, log_density.reshape(unit))


def solution(mesh):
    n_col = mesh.shape["col"]
    n_row = mesh.shape["row"]
    placed = (P(("parts", "row", "col"), None), P(("parts", "row", "col"), None))

    def run(points, vectors):
        unit, feats = points.shape
        paired = n_row == 2 and n_col >= 8 and n_col & (n_col - 1) == 0
        tile_bytes = 4 * (4 * unit) * (n_col // 2 * unit)
        width = vectors.shape[1]
        shaped = unit % 512 == 0 and feats == 128 and width % 16 == 0 and width <= 112
        if paired and shaped and tile_bytes <= 16 * MIB:
            return grid_device(points, vectors)
        return plain_device(points, vectors)

    return jax.shard_map(
        run,
        mesh=mesh,
        in_specs=placed,
        out_specs=(P(("parts", "row", "col"), None), P(("parts", "row", "col"))),
        check_vma=False,
    )
```

time: 36 us -> 34.7 us (0.964)
  waiting for transfers between devices: 11.4 us -> 9.04 us
  starting transfers between devices: 13.2 us -> 14.4 us
  local copies, waits for them, and re-layouts: 1.78 us -> 0.93 us
  Pallas kernels: 8.65 us -> 9.4 us
    ppermute x8 -> x9, waiting for transfers between devices: 11.4 us -> 7.9 us  [across(): return lax.ppermute(x, 'col', [(i, i ^ mask) for i in range(n_col)])]
    ppermute x8 -> x9, starting transfers between devices: 12.5 us -> 13.9 us  [across(): return lax.ppermute(x, 'col', [(i, i ^ mask) for i in range(n_col)])]
    ppermute x4 -> x6, waiting for transfers between devices: 0.01 us -> 1.13 us  [sibling(): return lax.ppermute(x, 'row', [(0, 1), (1, 0)])]
    unnamed x4 -> x2, local copies, waits for them, and re-layouts: 1.78 us -> 0.93 us
    pallas_call x12 -> x10, Pallas kernels: 8.65 us -> 9.4 us  [on_chip(): pl.pallas_call(body, out_shape=tuple(shapes), in_specs=[VMEM_SPEC] * len(...]
  transfers between devices with their start and end apart: 12 -> 15, of which waited for: 5 -> 9; matrix products, arithmetic and copies ran while one was open for 0% -> 0% of each run, Pallas kernels for 18% -> 18%
where the time goes in v4:
time: 34.7 us; the launch traced here: 34.5 us
  starting transfers between devices  14.4 us (41%)
  Pallas kernels  9.4 us (27%)
  waiting for transfers between devices  9.04 us (26%)
  local copies, waits for them, and re-layouts  0.93 us (3%)
  between operations  0.71 us (2%)
    ppermute x9, starting transfers between devices, across(): return lax.ppermute(x, 'col', [(i, i ^ mask) for i in range(n_col)])  13.9 us
    pallas_call x10, Pallas kernels, on_chip(): pl.pallas_call(body, out_shape=tuple(shapes), in_specs=[VMEM_SPEC] * len(...  9.4 us
    ppermute x9, waiting for transfers between devices, across(): return lax.ppermute(x, 'col', [(i, i ^ mask) for i in range(n_col)])  7.9 us
    ppermute x6, waiting for transfers between devices, sibling(): return lax.ppermute(x, 'row', [(0, 1), (1, 0)])  1.13 us
    unnamed x2, local copies, waits for them, and re-layouts  0.93 us
  transfers between devices with their start and end apart: 15, of which 9 were waited for; matrix products, arithmetic and copies ran while one was open for 0% of the time, Pallas kernels for 18%

profile of v4, /device:TPU:0, one launch (start us, length us, event | category | flops | bytes accessed | tf_op | source)
XLA Modules:
  0.0 34.5 jit_solution(6203445460191667388)
XLA Ops:
  0.6 3.1 %collective-permute-start.1 = (bf16[512,128]{1,0:T(8,128)(2,1)}, bf16[512,128]{1,0:T(8,128)(2,1)S(1)}, u32[]{:S(2)}, u32[]{:S(2)}) collective-permute-start(bf16[512,128]{1,0:T(8,128)(2,1)} %points_ref.1), channel_id=1, source_target_pairs={{0,2},{1,3},{2,0},{3,1},{4,6},{5,7},{6,4},{7,5},{8,10},{9,11},{10,... | collective-permute-start | bytes 393224 | tf_op jit(solution)/shard_map/ppermute | solution.py:287
  3.7 2.6 %collective-permute-start.3 = (bf16[512,128]{1,0:T(8,128)(2,1)}, bf16[512,128]{1,0:T(8,128)(2,1)S(1)}, u32[]{:S(2)}, u32[]{:S(2)}) collective-permute-start(bf16[512,128]{1,0:T(8,128)(2,1)} %points_ref.1), channel_id=1, source_target_pairs={{0,4},{1,5},{2,6},{3,7},{4,0},{5,1},{6,2},{7,3},{8,12},{9,13},{10,... | collective-permute-start | bytes 393224 | tf_op jit(solution)/shard_map/ppermute | solution.py:287
  6.3 1.5 %collective-permute-start = (bf16[512,128]{1,0:T(8,128)(2,1)}, bf16[512,128]{1,0:T(8,128)(2,1)S(1)}, u32[]{:S(2)}, u32[]{:S(2)}) collective-permute-start(bf16[512,128]{1,0:T(8,128)(2,1)} %points_ref.1), channel_id=1, source_target_pairs={{0,1},{1,0},{2,3},{3,2},{4,5},{5,4},{6,7},{7,6},{8,9},{9,8},{10,11... | collective-permute-start | bytes 393224 | tf_op jit(solution)/shard_map/ppermute | solution.py:287
  7.8 0.9 %copy-done = bf16[512,128]{1,0:T(8,128)(2,1)S(1)} copy-done((bf16[512,128]{1,0:T(8,128)(2,1)S(1)}, bf16[512,128]{1,0:T(8,128)(2,1)}, u32[]{:S(2)}) %copy-start) | copy-done | bytes 131096
  8.8 1.2 %own.1 = (bf16[512,256]{1,0:T(8,128)(2,1)S(1)}, bf16[512,256]{1,0:T(8,128)(2,1)S(1)}, bf16[64,512]{1,0:T(8,128)(2,1)S(1)}) custom-call(bf16[512,128]{1,0:T(8,128)(2,1)S(1)} %copy-done, bf16[64,512]{1,0:T(8,128)(2,1)} %bitcast.vector_ref), custom_call_target="tpu_custom_call" | custom-call | tf_op jit(solution)/shard_map/own/pallas_call | solution.py:148
  10.0 0.0 collective-permute-done.1.refs_1_
  10.0 1.1 %collective-permute-start.4 = (bf16[512,128]{1,0:T(8,128)(2,1)S(1)}, bf16[512,128]{1,0:T(8,128)(2,1)S(1)}, u32[]{:S(2)}, u32[]{:S(2)}) collective-permute-start(bf16[512,128]{1,0:T(8,128)(2,1)S(1)} %collective-permute-done.1.refs_1_), channel_id=1, source_target_pairs={{0,1},{1,0},{2,3},{3,2},{4,5},{5,4},{6,7},{7,6},{8,9},{9,8},{10,11... | collective-permute-start | bytes 393224 | tf_op jit(solution)/shard_map/ppermute | solution.py:287
  11.1 1.6 %collective-permute-done.3.refs_4_ = bf16[512,128]{1,0:T(8,128)(2,1)S(1)} collective-permute-done((bf16[512,128]{1,0:T(8,128)(2,1)}, bf16[512,128]{1,0:T(8,128)(2,1)S(1)}, u32[]{:S(2)}, u32[]{:S(2)}) %collective-permute-start.3) | collective-permute-done | bytes 131104 | tf_op jit(solution)/shard_map/ppermute | solution.py:287
  12.7 0.0 collective-permute-start.5
  12.7 0.3 collective-permute-start.7
  13.0 2.0 %near.1 = (f32[1536,1536]{1,0:T(8,128)S(1)}, f32[1,1536]{1,0:T(1,128)S(1)}, bf16[1024,256]{1,0:T(8,128)(2,1)S(1)}, bf16[1024,256]{1,0:T(8,128)(2,1)S(1)}) custom-call(bf16[512,128]{1,0:T(8,128)(2,1)S(1)} %collective-permute-done.refs_0_, bf16[512,128]{1,0:T(8,128)(2,1)S(1)} %collective-permute-done.1.refs_1_, ...), custom_call_target="tpu_custom_call" | custom-call | tf_op jit(solution)/shard_map/near/pallas_call | solution.py:148
  15.0 0.9 %collective-permute-done.4.refs_0_ = bf16[512,128]{1,0:T(8,128)(2,1)S(1)} collective-permute-done((bf16[512,128]{1,0:T(8,128)(2,1)S(1)}, bf16[512,128]{1,0:T(8,128)(2,1)S(1)}, u32[]{:S(2)}, u32[]{:S(2)}) %collective-permute-start.4) | collective-permute-done | bytes 131104 | tf_op jit(solution)/shard_map/ppermute | solution.py:287
  15.9 0.8 %last.1 = (f32[512,1536]{1,0:T(8,128)S(1)}, f32[1,1536]{1,0:T(1,128)S(1)}, bf16[512,256]{1,0:T(8,128)(2,1)S(1)}) custom-call(bf16[512,128]{1,0:T(8,128)(2,1)S(1)} %collective-permute-done.4.refs_0_, bf16[512,256]{1,0:T(8,128)(2,1)S(1)} %get-tuple-element.25.refs_5_.refs_1_, bf16[1024,256]{1,0:T(8,128)(2,1)S(1)} %get-tuple-element.28.refs_2_, ...), custom_call_target="tpu_custom_call" | custom-call | tf_op jit(solution)/shard_map/last/pallas_call | solution.py:148
  16.7 1.0 %side.1 = (f32[2048,512]{1,0:T(8,128)S(1)}, f32[1,2048]{1,0:T(1,128)S(1)}) custom-call(bf16[512,256]{1,0:T(8,128)(2,1)S(1)} %get-tuple-element.24.refs_2_.refs_0_, bf16[1024,256]{1,0:T(8,128)(2,1)S(1)} %get-tuple-element.27.refs_1_, bf16[512,256]{1,0:T(8,128)(2,1)S(1)} %get-tuple-element.30.refs_2_, bf16[512,128]{1,0:T(8,128)(2,1)S(1)} %collective-permute-done.5.refs_3_, ...), custom_call_target="tpu_custom_call" | custom-call | tf_op jit(solution)/shard_map/side/pallas_call | solution.py:148
  17.7 1.8 %collective-permute-start.8 = (f32[1,2048]{1,0:T(1,128)S(1)}, f32[1,2048]{1,0:T(1,128)S(1)}, u32[]{:S(2)}, u32[]{:S(2)}) collective-permute-start(f32[1,2048]{1,0:T(1,128)S(1)} %get-tuple-element.36.refs_0_), channel_id=1, source_target_pairs={{0,4},{1,5},{2,6},{3,7},{4,0},{5,1},{6,2},{7,3},{8,12},{9,13},{10,... | collective-permute-start | bytes 24584 | tf_op jit(solution)/shard_map/ppermute | solution.py:287
  19.5 0.1 collective-permute-done.7.refs_2_
  19.5 2.8 %collective-permute-done.8.refs_2_ = f32[1,2048]{1,0:T(1,128)S(1)} collective-permute-done((f32[1,2048]{1,0:T(1,128)S(1)}, f32[1,2048]{1,0:T(1,128)S(1)}, u32[]{:S(2)}, u32[]{:S(2)}) %collective-permute-start.8) | collective-permute-done | bytes 8224 | tf_op jit(solution)/shard_map/ppermute | solution.py:287
  22.3 0.5 %collective-permute-start.10 = (f32[1,2048]{1,0:T(1,128)S(1)}, f32[1,2048]{1,0:T(1,128)S(1)}, u32[]{:S(2)}, u32[]{:S(2)}) collective-permute-start(f32[1,2048]{1,0:T(1,128)S(1)} %get-tuple-element.36.refs_0_), channel_id=1, source_target_pairs={{0,8},{8,0},{1,9},{9,1},{2,10},{10,2},{3,11},{11,3},{4,12},{12,4},... | collective-permute-start | bytes 24584 | tf_op jit(solution)/shard_map/ppermute | solution.py:290
  22.8 0.0 collective-permute-start.11
  22.8 0.7 %collective-permute-done.9.refs_3_ = bf16[64,512]{1,0:T(8,128)(2,1)S(1)} collective-permute-done((bf16[64,512]{1,0:T(8,128)(2,1)S(1)}, bf16[64,512]{1,0:T(8,128)(2,1)S(1)}, u32[]{:S(2)}, u32[]{:S(2)}) %collective-permute-start.9) | collective-permute-done | bytes 65568 | tf_op jit(solution)/shard_map/ppermute | solution.py:290
  23.6 0.0 collective-permute-done.10.refs_1_
  23.7 0.3 collective-permute-done.11.refs_3_
  24.0 0.8 %give_first.1 = (bf16[80,512]{1,0:T(8,128)(2,1)S(1)}, f32[1,2048]{1,0:T(1,128)S(1)}, f32[1,512]{1,0:T(1,128)S(1)}) custom-call(f32[1536,1536]{1,0:T(8,128)S(1)} %get-tuple-element.26.k_near.refs_0_, f32[2048,512]{1,0:T(8,128)S(1)} %get-tuple-element.33.k_side.refs_1_, bf16[128,2048]{1,0:T(8,128)(2,1)S(1)} %vectors.1.vec_all.refs_2_, ...), custom_call_target="tpu_custom_call" | custom-call | tf_op jit(solution)/shard_map/give_first/pallas_call | solution.py:148
  24.8 0.8 %give.2 = bf16[80,512]{1,0:T(8,128)(2,1)S(1)} custom-call(f32[1536,1536]{1,0:T(8,128)S(1)} %get-tuple-element.26.k_near.refs_0_, f32[2048,512]{1,0:T(8,128)S(1)} %get-tuple-element.33.k_side.refs_1_, bf16[128,2048]{1,0:T(8,128)(2,1)S(1)} %vectors.1.vec_all.refs_2_, f32[1,2048]{1,0:T(1,128)S(1)} %get-tuple-element.44.refs_3_), custom_call_target="tpu_custom_call" | custom-call | tf_op jit(solution)/shard_map/give/pallas_call | solution.py:148
  25.6 0.8 %give.3 = bf16[80,512]{1,0:T(8,128)(2,1)S(1)} custom-call(f32[512,1536]{1,0:T(8,128)S(1)} %get-tuple-element.43.refs_0_, f32[2048,512]{1,0:T(8,128)S(1)} %get-tuple-element.33.k_side.refs_1_, bf16[128,2048]{1,0:T(8,128)(2,1)S(1)} %vectors.1.vec_all.refs_2_, f32[1,2048]{1,0:T(1,128)S(1)} %get-tuple-element.44.refs_3_), custom_call_target="tpu_custom_call" | custom-call | tf_op jit(solution)/shard_map/give/pallas_call | solution.py:148
  26.4 2.8 %collective-permute-start.14 = (bf16[80,512]{1,0:T(8,128)(2,1)S(1)}, bf16[80,512]{1,0:T(8,128)(2,1)S(1)}, u32[]{:S(2)}, u32[]{:S(2)}) collective-permute-start(bf16[80,512]{1,0:T(8,128)(2,1)S(1)} %give.3), channel_id=1, source_target_pairs={{0,3},{1,2},{2,1},{3,0},{4,7},{5,6},{6,5},{7,4},{8,11},{9,10},{10,... | collective-permute-start | bytes 245768 | tf_op jit(solution)/shard_map/ppermute | solution.py:287
  29.2 0.7 %collective-permute-start.12 = (bf16[80,512]{1,0:T(8,128)(2,1)S(1)}, bf16[80,512]{1,0:T(8,128)(2,1)S(1)}, u32[]{:S(2)}, u32[]{:S(2)}) collective-permute-start(bf16[80,512]{1,0:T(8,128)(2,1)S(1)} %get-tuple-element.41), channel_id=1, source_target_pairs={{0,1},{1,0},{2,3},{3,2},{4,5},{5,4},{6,7},{7,6},{8,9},{9,8},{10,11... | collective-permute-start | bytes 245768 | tf_op jit(solution)/shard_map/ppermute | solution.py:287
  30.0 1.3 %keep.1 = (f32[72,512]{1,0:T(8,128)S(1)}, f32[1,512]{1,0:T(1,128)}) custom-call(f32[1536,1536]{1,0:T(8,128)S(1)} %get-tuple-element.26.k_near.refs_0_, f32[2048,512]{1,0:T(8,128)S(1)} %get-tuple-element.33.k_side.refs_1_, bf16[128,2048]{1,0:T(8,128)(2,1)S(1)} %vectors.1.vec_all.refs_2_, f32[1,2048]{1,0:T(1,128)S(1)} %get-tuple-element.44.refs_3_, ...), custom_call_target="tpu_custom_call" | custom-call | tf_op jit(solution)/shard_map/keep/pallas_call | solution.py:148
  31.3 1.1 %collective-permute-done.14.refs_2_ = bf16[80,512]{1,0:T(8,128)(2,1)S(1)} collective-permute-done((bf16[80,512]{1,0:T(8,128)(2,1)S(1)}, bf16[80,512]{1,0:T(8,128)(2,1)S(1)}, u32[]{:S(2)}, u32[]{:S(2)}) %collective-permute-start.14) | collective-permute-done | bytes 81952 | tf_op jit(solution)/shard_map/ppermute | solution.py:287
  32.4 1.3 %collective-permute-done.13.refs_1_ = bf16[80,512]{1,0:T(8,128)(2,1)S(1)} collective-permute-done((bf16[80,512]{1,0:T(8,128)(2,1)S(1)}, bf16[80,512]{1,0:T(8,128)(2,1)S(1)}, u32[]{:S(2)}, u32[]{:S(2)}) %collective-permute-start.13) | collective-permute-done | bytes 81952 | tf_op jit(solution)/shard_map/ppermute | solution.py:287
  33.7 0.1 collective-permute-done.12.refs_0_
  33.8 0.7 %finish.1 = f32[64,512]{1,0:T(8,128)} custom-call(f32[72,512]{1,0:T(8,128)S(1)} %get-tuple-element.40.near_ref, bf16[80,512]{1,0:T(8,128)(2,1)S(1)} %collective-permute-done.12.refs_0_, bf16[80,512]{1,0:T(8,128)(2,1)S(1)} %collective-permute-done.13.refs_1_, bf16[80,512]{1,0:T(8,128)(2,1)S(1)} %collective-permute-done.14.refs_2_), custom_call_target="tpu_custom_call" | custom-call | tf_op jit(solution)/shard_map/finish/pallas_call | solution.py:148
  (10 shorter events, 0.1 us)
Async XLA Ops:
  0.6 9.4 %collective-permute-start.1 = (bf16[512,128]{1,0:T(8,128)(2,1)}, bf16[512,128]{1,0:T(8,128)(2,1)S(1)}, u32[]{:S(2)}, u32[]{:S(2)}) collective-permute-start(bf16[512,128]{1,0:T(8,128)(2,1)} %points_ref.1), channel_id=1, source_target_pairs={{0,2},{1,3},{2,0},{3,1},{4,6},{5,7},{6,4},{7,5},{8,10},{9,11},{10,... | collective-permute-start | bytes 393224 | tf_op jit(solution)/shard_map/ppermute | solution.py:287
  3.7 8.9 %collective-permute-start.3 = (bf16[512,128]{1,0:T(8,128)(2,1)}, bf16[512,128]{1,0:T(8,128)(2,1)S(1)}, u32[]{:S(2)}, u32[]{:S(2)}) collective-permute-start(bf16[512,128]{1,0:T(8,128)(2,1)} %points_ref.1), channel_id=1, source_target_pairs={{0,4},{1,5},{2,6},{3,7},{4,0},{5,1},{6,2},{7,3},{8,12},{9,13},{10,... | collective-permute-start | bytes 393224 | tf_op jit(solution)/shard_map/ppermute | solution.py:287
  6.3 6.7 %collective-permute-start = (bf16[512,128]{1,0:T(8,128)(2,1)}, bf16[512,128]{1,0:T(8,128)(2,1)S(1)}, u32[]{:S(2)}, u32[]{:S(2)}) collective-permute-start(bf16[512,128]{1,0:T(8,128)(2,1)} %points_ref.1), channel_id=1, source_target_pairs={{0,1},{1,0},{2,3},{3,2},{4,5},{5,4},{6,7},{7,6},{8,9},{9,8},{10,11... | collective-permute-start | bytes 393224 | tf_op jit(solution)/shard_map/ppermute | solution.py:287
  7.8 5.2 %collective-permute-start.2 = (bf16[512,128]{1,0:T(8,128)(2,1)}, bf16[512,128]{1,0:T(8,128)(2,1)S(1)}, u32[]{:S(2)}, u32[]{:S(2)}) collective-permute-start(bf16[512,128]{1,0:T(8,128)(2,1)} %points_ref.1), channel_id=1, source_target_pairs={{0,8},{8,0},{1,9},{9,1},{2,10},{10,2},{3,11},{11,3},{4,12},{12,4},... | collective-permute-start | bytes 393224 | tf_op jit(solution)/shard_map/ppermute | solution.py:290
  7.8 0.9 %copy-start = (bf16[512,128]{1,0:T(8,128)(2,1)S(1)}, bf16[512,128]{1,0:T(8,128)(2,1)}, u32[]{:S(2)}) copy-start(bf16[512,128]{1,0:T(8,128)(2,1)} %points_ref.1) | copy-start | bytes 393220
  10.0 5.9 %collective-permute-start.4 = (bf16[512,128]{1,0:T(8,128)(2,1)S(1)}, bf16[512,128]{1,0:T(8,128)(2,1)S(1)}, u32[]{:S(2)}, u32[]{:S(2)}) collective-permute-start(bf16[512,128]{1,0:T(8,128)(2,1)S(1)} %collective-permute-done.1.refs_1_), channel_id=1, source_target_pairs={{0,1},{1,0},{2,3},{3,2},{4,5},{5,4},{6,7},{7,6},{8,9},{9,8},{10,11... | collective-permute-start | bytes 393224 | tf_op jit(solution)/shard_map/ppermute | solution.py:287
  12.7 4.0 %collective-permute-start.5 = (bf16[512,128]{1,0:T(8,128)(2,1)S(1)}, bf16[512,128]{1,0:T(8,128)(2,1)S(1)}, u32[]{:S(2)}, u32[]{:S(2)}) collective-permute-start(bf16[512,128]{1,0:T(8,128)(2,1)S(1)} %collective-permute-done.3.refs_4_), channel_id=1, source_target_pairs={{0,8},{8,0},{1,9},{9,1},{2,10},{10,2},{3,11},{11,3},{4,12},{12,4},... | collective-permute-start | bytes 393224 | tf_op jit(solution)/shard_map/ppermute | solution.py:290
  12.7 6.9 %collective-permute-start.7 = (bf16[64,512]{1,0:T(8,128)(2,1)}, bf16[64,512]{1,0:T(8,128)(2,1)S(1)}, u32[]{:S(2)}, u32[]{:S(2)}) collective-permute-start(bf16[64,512]{1,0:T(8,128)(2,1)} %bitcast.vector_ref), channel_id=1, source_target_pairs={{0,4},{1,5},{2,6},{3,7},{4,0},{5,1},{6,2},{7,3},{8,12},{9,13},{10,... | collective-permute-start | bytes 196616 | tf_op jit(solution)/shard_map/ppermute | solution.py:287
  17.7 4.6 %collective-permute-start.8 = (f32[1,2048]{1,0:T(1,128)S(1)}, f32[1,2048]{1,0:T(1,128)S(1)}, u32[]{:S(2)}, u32[]{:S(2)}) collective-permute-start(f32[1,2048]{1,0:T(1,128)S(1)} %get-tuple-element.36.refs_0_), channel_id=1, source_target_pairs={{0,4},{1,5},{2,6},{3,7},{4,0},{5,1},{6,2},{7,3},{8,12},{9,13},{10,... | collective-permute-start | bytes 24584 | tf_op jit(solution)/shard_map/ppermute | solution.py:287
  19.5 3.4 %collective-permute-start.6 = (bf16[64,512]{1,0:T(8,128)(2,1)}, bf16[64,512]{1,0:T(8,128)(2,1)S(1)}, u32[]{:S(2)}, u32[]{:S(2)}) collective-permute-start(bf16[64,512]{1,0:T(8,128)(2,1)} %bitcast.vector_ref), channel_id=1, source_target_pairs={{0,8},{8,0},{1,9},{9,1},{2,10},{10,2},{3,11},{11,3},{4,12},{12,4},... | collective-permute-start | bytes 196616 | tf_op jit(solution)/shard_map/ppermute | solution.py:290
  22.3 1.3 %collective-permute-start.9 = (bf16[64,512]{1,0:T(8,128)(2,1)S(1)}, bf16[64,512]{1,0:T(8,128)(2,1)S(1)}, u32[]{:S(2)}, u32[]{:S(2)}) collective-permute-start(bf16[64,512]{1,0:T(8,128)(2,1)S(1)} %collective-permute-done.7.refs_2_), channel_id=1, source_target_pairs={{0,8},{8,0},{1,9},{9,1},{2,10},{10,2},{3,11},{11,3},{4,12},{12,4},... | collective-permute-start | bytes 196616 | tf_op jit(solution)/shard_map/ppermute | solution.py:290
  22.3 1.3 %collective-permute-start.10 = (f32[1,2048]{1,0:T(1,128)S(1)}, f32[1,2048]{1,0:T(1,128)S(1)}, u32[]{:S(2)}, u32[]{:S(2)}) collective-permute-start(f32[1,2048]{1,0:T(1,128)S(1)} %get-tuple-element.36.refs_0_), channel_id=1, source_target_pairs={{0,8},{8,0},{1,9},{9,1},{2,10},{10,2},{3,11},{11,3},{4,12},{12,4},... | collective-permute-start | bytes 24584 | tf_op jit(solution)/shard_map/ppermute | solution.py:290
  22.8 1.2 %collective-permute-start.11 = (f32[1,2048]{1,0:T(1,128)S(1)}, f32[1,2048]{1,0:T(1,128)S(1)}, u32[]{:S(2)}, u32[]{:S(2)}) collective-permute-start(f32[1,2048]{1,0:T(1,128)S(1)} %collective-permute-done.8.refs_2_), channel_id=1, source_target_pairs={{0,8},{8,0},{1,9},{9,1},{2,10},{10,2},{3,11},{11,3},{4,12},{12,4},... | collective-permute-start | bytes 24584 | tf_op jit(solution)/shard_map/ppermute | solution.py:290
  26.4 6.0 %collective-permute-start.14 = (bf16[80,512]{1,0:T(8,128)(2,1)S(1)}, bf16[80,512]{1,0:T(8,128)(2,1)S(1)}, u32[]{:S(2)}, u32[]{:S(2)}) collective-permute-start(bf16[80,512]{1,0:T(8,128)(2,1)S(1)} %give.3), channel_id=1, source_target_pairs={{0,3},{1,2},{2,1},{3,0},{4,7},{5,6},{6,5},{7,4},{8,11},{9,10},{10,... | collective-permute-start | bytes 245768 | tf_op jit(solution)/shard_map/ppermute | solution.py:287
  29.2 4.4 %collective-permute-start.13 = (bf16[80,512]{1,0:T(8,128)(2,1)S(1)}, bf16[80,512]{1,0:T(8,128)(2,1)S(1)}, u32[]{:S(2)}, u32[]{:S(2)}) collective-permute-start(bf16[80,512]{1,0:T(8,128)(2,1)S(1)} %give.2), channel_id=1, source_target_pairs={{0,2},{1,3},{2,0},{3,1},{4,6},{5,7},{6,4},{7,5},{8,10},{9,11},{10,... | collective-permute-start | bytes 245768 | tf_op jit(solution)/shard_map/ppermute | solution.py:287
  29.2 4.6 %collective-permute-start.12 = (bf16[80,512]{1,0:T(8,128)(2,1)S(1)}, bf16[80,512]{1,0:T(8,128)(2,1)S(1)}, u32[]{:S(2)}, u32[]{:S(2)}) collective-permute-start(bf16[80,512]{1,0:T(8,128)(2,1)S(1)} %get-tuple-element.41), channel_id=1, source_target_pairs={{0,1},{1,0},{2,3},{3,2},{4,5},{5,4},{6,7},{7,6},{8,9},{9,8},{10,11... | collective-permute-start | bytes 245768 | tf_op jit(solution)/shard_map/ppermute | solution.py:287

commit v5 on v4

--- a/solution.py
+++ b/solution.py
@@ -175,7 +175,7 @@
             made = pltpu.VMEM((len(raw) * unit, wide), jnp.bfloat16)
             (scratch if ahead else shapes).append(made)
     counts = [len(g) for g in groups]
-    body = functools.partial(kernel_body, counts, unit, scale, diagonal, 256, 512)
+    body = functools.partial(kernel_body, counts, unit, scale, diagonal, 512, 256)
     args = [x for g in groups for x in g]
     return on_chip(body, shapes, name, 12, *args, scratch=scratch)
 
@@ -331,7 +331,7 @@
 
     packed = pltpu.VMEM((width + 16, unit), jnp.bfloat16)
     away, inverse, density = on_chip(
-        functools.partial(first_give_body, unit, points_all, unit, 256, len(all_sums)),
+        functools.partial(first_give_body, unit, points_all, unit, 512, len(all_sums)),
         (
             packed,
             pltpu.VMEM((1, n_wide), jnp.float32),
@@ -348,7 +348,7 @@
     for u in range(2, n_units):
         last = u == n_units - 1
         (away,) = on_chip(
-            functools.partial(next_give_body, [0 if last else u * unit, u * unit], 256),
+            functools.partial(next_give_body, [0 if last else u * unit, u * unit], 512),
             (packed,),
             "give",
             8,
@@ -359,7 +359,7 @@
         )
         back.append(across(away, u))
     near, log_density = on_chip(
-        functools.partial(keep_body, 256),
+        functools.partial(keep_body, 512),
         (
             pltpu.VMEM((width + 8, unit), jnp.float32),
             jax.ShapeDtypeStruct((1, unit), jnp.float32),

time: 34.7 us -> 34.5 us (level)
  no operation moved by 1% of the time
where the time goes in v5:
time: 34.5 us; the launch traced here: 34.3 us
  starting transfers between devices  14.4 us (42%)
  Pallas kernels  9.19 us (27%)
  waiting for transfers between devices  9.11 us (26%)
  local copies, waits for them, and re-layouts  0.93 us (3%)
  between operations  0.71 us (2%)
    ppermute x9, starting transfers between devices, across(): return lax.ppermute(x, 'col', [(i, i ^ mask) for i in range(n_col)])  13.9 us
    pallas_call x10, Pallas kernels, on_chip(): pl.pallas_call(body, out_shape=tuple(shapes), in_specs=[VMEM_SPEC] * len(...  9.19 us
    ppermute x9, waiting for transfers between devices, across(): return lax.ppermute(x, 'col', [(i, i ^ mask) for i in range(n_col)])  7.98 us
    ppermute x6, waiting for transfers between devices, sibling(): return lax.ppermute(x, 'row', [(0, 1), (1, 0)])  1.13 us
    unnamed x2, local copies, waits for them, and re-layouts  0.93 us
  transfers between devices with their start and end apart: 15, of which 9 were waited for; matrix products, arithmetic and copies ran while one was open for 0% of the time, Pallas kernels for 18%

profile of v5, /device:TPU:0, one launch (start us, length us, event | category | flops | bytes accessed | tf_op | source)
XLA Modules:
  0.0 34.3 jit_solution(11171069025629936756)
XLA Ops:
  0.6 3.1 %collective-permute-start.1 = (bf16[512,128]{1,0:T(8,128)(2,1)}, bf16[512,128]{1,0:T(8,128)(2,1)S(1)}, u32[]{:S(2)}, u32[]{:S(2)}) collective-permute-start(bf16[512,128]{1,0:T(8,128)(2,1)} %points_ref.1), channel_id=1, source_target_pairs={{0,2},{1,3},{2,0},{3,1},{4,6},{5,7},{6,4},{7,5},{8,10},{9,11},{10,... | collective-permute-start | bytes 393224 | tf_op jit(solution)/shard_map/ppermute | solution.py:287
  3.7 2.6 %collective-permute-start.3 = (bf16[512,128]{1,0:T(8,128)(2,1)}, bf16[512,128]{1,0:T(8,128)(2,1)S(1)}, u32[]{:S(2)}, u32[]{:S(2)}) collective-permute-start(bf16[512,128]{1,0:T(8,128)(2,1)} %points_ref.1), channel_id=1, source_target_pairs={{0,4},{1,5},{2,6},{3,7},{4,0},{5,1},{6,2},{7,3},{8,12},{9,13},{10,... | collective-permute-start | bytes 393224 | tf_op jit(solution)/shard_map/ppermute | solution.py:287
  6.3 1.5 %collective-permute-start = (bf16[512,128]{1,0:T(8,128)(2,1)}, bf16[512,128]{1,0:T(8,128)(2,1)S(1)}, u32[]{:S(2)}, u32[]{:S(2)}) collective-permute-start(bf16[512,128]{1,0:T(8,128)(2,1)} %points_ref.1), channel_id=1, source_target_pairs={{0,1},{1,0},{2,3},{3,2},{4,5},{5,4},{6,7},{7,6},{8,9},{9,8},{10,11... | collective-permute-start | bytes 393224 | tf_op jit(solution)/shard_map/ppermute | solution.py:287
  7.8 0.0 collective-permute-start.2
  7.8 0.9 %copy-done = bf16[512,128]{1,0:T(8,128)(2,1)S(1)} copy-done((bf16[512,128]{1,0:T(8,128)(2,1)S(1)}, bf16[512,128]{1,0:T(8,128)(2,1)}, u32[]{:S(2)}) %copy-start) | copy-done | bytes 131096
  8.8 1.2 %own.1 = (bf16[512,256]{1,0:T(8,128)(2,1)S(1)}, bf16[512,256]{1,0:T(8,128)(2,1)S(1)}, bf16[64,512]{1,0:T(8,128)(2,1)S(1)}) custom-call(bf16[512,128]{1,0:T(8,128)(2,1)S(1)} %copy-done, bf16[64,512]{1,0:T(8,128)(2,1)} %bitcast.vector_ref), custom_call_target="tpu_custom_call" | custom-call | tf_op jit(solution)/shard_map/own/pallas_call | solution.py:148
  10.0 1.1 %collective-permute-start.4 = (bf16[512,128]{1,0:T(8,128)(2,1)S(1)}, bf16[512,128]{1,0:T(8,128)(2,1)S(1)}, u32[]{:S(2)}, u32[]{:S(2)}) collective-permute-start(bf16[512,128]{1,0:T(8,128)(2,1)S(1)} %collective-permute-done.1.refs_1_), channel_id=1, source_target_pairs={{0,1},{1,0},{2,3},{3,2},{4,5},{5,4},{6,7},{7,6},{8,9},{9,8},{10,11... | collective-permute-start | bytes 393224 | tf_op jit(solution)/shard_map/ppermute | solution.py:287
  11.1 1.6 %collective-permute-done.3.refs_4_ = bf16[512,128]{1,0:T(8,128)(2,1)S(1)} collective-permute-done((bf16[512,128]{1,0:T(8,128)(2,1)}, bf16[512,128]{1,0:T(8,128)(2,1)S(1)}, u32[]{:S(2)}, u32[]{:S(2)}) %collective-permute-start.3) | collective-permute-done | bytes 131104 | tf_op jit(solution)/shard_map/ppermute | solution.py:287
  12.7 0.0 collective-permute-start.5
  12.7 0.3 collective-permute-start.7
  13.0 2.0 %near.1 = (f32[1536,1536]{1,0:T(8,128)S(1)}, f32[1,1536]{1,0:T(1,128)S(1)}, bf16[1024,256]{1,0:T(8,128)(2,1)S(1)}, bf16[1024,256]{1,0:T(8,128)(2,1)S(1)}) custom-call(bf16[512,128]{1,0:T(8,128)(2,1)S(1)} %collective-permute-done.refs_0_, bf16[512,128]{1,0:T(8,128)(2,1)S(1)} %collective-permute-done.1.refs_1_, ...), custom_call_target="tpu_custom_call" | custom-call | tf_op jit(solution)/shard_map/near/pallas_call | solution.py:148
  15.0 1.0 %collective-permute-done.4.refs_0_ = bf16[512,128]{1,0:T(8,128)(2,1)S(1)} collective-permute-done((bf16[512,128]{1,0:T(8,128)(2,1)S(1)}, bf16[512,128]{1,0:T(8,128)(2,1)S(1)}, u32[]{:S(2)}, u32[]{:S(2)}) %collective-permute-start.4) | collective-permute-done | bytes 131104 | tf_op jit(solution)/shard_map/ppermute | solution.py:287
  15.9 0.7 %last.1 = (f32[512,1536]{1,0:T(8,128)S(1)}, f32[1,1536]{1,0:T(1,128)S(1)}, bf16[512,256]{1,0:T(8,128)(2,1)S(1)}) custom-call(bf16[512,128]{1,0:T(8,128)(2,1)S(1)} %collective-permute-done.4.refs_0_, bf16[512,256]{1,0:T(8,128)(2,1)S(1)} %get-tuple-element.25.refs_5_.refs_1_, bf16[1024,256]{1,0:T(8,128)(2,1)S(1)} %get-tuple-element.28.refs_2_, ...), custom_call_target="tpu_custom_call" | custom-call | tf_op jit(solution)/shard_map/last/pallas_call | solution.py:148
  16.7 0.9 %side.1 = (f32[2048,512]{1,0:T(8,128)S(1)}, f32[1,2048]{1,0:T(1,128)S(1)}) custom-call(bf16[512,256]{1,0:T(8,128)(2,1)S(1)} %get-tuple-element.24.refs_2_.refs_0_, bf16[1024,256]{1,0:T(8,128)(2,1)S(1)} %get-tuple-element.27.refs_1_, bf16[512,256]{1,0:T(8,128)(2,1)S(1)} %get-tuple-element.30.refs_2_, bf16[512,128]{1,0:T(8,128)(2,1)S(1)} %collective-permute-done.5.refs_3_, ...), custom_call_target="tpu_custom_call" | custom-call | tf_op jit(solution)/shard_map/side/pallas_call | solution.py:148
  17.6 1.7 %collective-permute-start.8 = (f32[1,2048]{1,0:T(1,128)S(1)}, f32[1,2048]{1,0:T(1,128)S(1)}, u32[]{:S(2)}, u32[]{:S(2)}) collective-permute-start(f32[1,2048]{1,0:T(1,128)S(1)} %get-tuple-element.36.refs_0_), channel_id=1, source_target_pairs={{0,4},{1,5},{2,6},{3,7},{4,0},{5,1},{6,2},{7,3},{8,12},{9,13},{10,... | collective-permute-start | bytes 24584 | tf_op jit(solution)/shard_map/ppermute | solution.py:287
  19.4 0.2 collective-permute-done.7.refs_2_
  19.5 2.7 %collective-permute-done.8.refs_2_ = f32[1,2048]{1,0:T(1,128)S(1)} collective-permute-done((f32[1,2048]{1,0:T(1,128)S(1)}, f32[1,2048]{1,0:T(1,128)S(1)}, u32[]{:S(2)}, u32[]{:S(2)}) %collective-permute-start.8) | collective-permute-done | bytes 8224 | tf_op jit(solution)/shard_map/ppermute | solution.py:287
  22.3 0.5 %collective-permute-start.10 = (f32[1,2048]{1,0:T(1,128)S(1)}, f32[1,2048]{1,0:T(1,128)S(1)}, u32[]{:S(2)}, u32[]{:S(2)}) collective-permute-start(f32[1,2048]{1,0:T(1,128)S(1)} %get-tuple-element.36.refs_0_), channel_id=1, source_target_pairs={{0,8},{8,0},{1,9},{9,1},{2,10},{10,2},{3,11},{11,3},{4,12},{12,4},... | collective-permute-start | bytes 24584 | tf_op jit(solution)/shard_map/ppermute | solution.py:290
  22.8 0.0 collective-permute-start.11
  22.8 0.7 %collective-permute-done.9.refs_3_ = bf16[64,512]{1,0:T(8,128)(2,1)S(1)} collective-permute-done((bf16[64,512]{1,0:T(8,128)(2,1)S(1)}, bf16[64,512]{1,0:T(8,128)(2,1)S(1)}, u32[]{:S(2)}, u32[]{:S(2)}) %collective-permute-start.9) | collective-permute-done | bytes 65568 | tf_op jit(solution)/shard_map/ppermute | solution.py:290
  23.5 0.0 collective-permute-done.10.refs_1_
  23.6 0.3 %collective-permute-done.11.refs_3_ = f32[1,2048]{1,0:T(1,128)S(1)} collective-permute-done((f32[1,2048]{1,0:T(1,128)S(1)}, f32[1,2048]{1,0:T(1,128)S(1)}, u32[]{:S(2)}, u32[]{:S(2)}) %collective-permute-start.11) | collective-permute-done | bytes 8224 | tf_op jit(solution)/shard_map/ppermute | solution.py:290
  23.9 0.8 %give_first.1 = (bf16[80,512]{1,0:T(8,128)(2,1)S(1)}, f32[1,2048]{1,0:T(1,128)S(1)}, f32[1,512]{1,0:T(1,128)S(1)}) custom-call(f32[1536,1536]{1,0:T(8,128)S(1)} %get-tuple-element.26.k_near.refs_0_, f32[2048,512]{1,0:T(8,128)S(1)} %get-tuple-element.33.k_side.refs_1_, bf16[128,2048]{1,0:T(8,128)(2,1)S(1)} %vectors.1.vec_all.refs_2_, ...), custom_call_target="tpu_custom_call" | custom-call | tf_op jit(solution)/shard_map/give_first/pallas_call | solution.py:148
  24.7 0.8 %give.2 = bf16[80,512]{1,0:T(8,128)(2,1)S(1)} custom-call(f32[1536,1536]{1,0:T(8,128)S(1)} %get-tuple-element.26.k_near.refs_0_, f32[2048,512]{1,0:T(8,128)S(1)} %get-tuple-element.33.k_side.refs_1_, bf16[128,2048]{1,0:T(8,128)(2,1)S(1)} %vectors.1.vec_all.refs_2_, f32[1,2048]{1,0:T(1,128)S(1)} %get-tuple-element.44.refs_3_), custom_call_target="tpu_custom_call" | custom-call | tf_op jit(solution)/shard_map/give/pallas_call | solution.py:148
  25.5 0.8 %give.3 = bf16[80,512]{1,0:T(8,128)(2,1)S(1)} custom-call(f32[512,1536]{1,0:T(8,128)S(1)} %get-tuple-element.43.refs_0_, f32[2048,512]{1,0:T(8,128)S(1)} %get-tuple-element.33.k_side.refs_1_, bf16[128,2048]{1,0:T(8,128)(2,1)S(1)} %vectors.1.vec_all.refs_2_, f32[1,2048]{1,0:T(1,128)S(1)} %get-tuple-element.44.refs_3_), custom_call_target="tpu_custom_call" | custom-call | tf_op jit(solution)/shard_map/give/pallas_call | solution.py:148
  26.3 2.8 %collective-permute-start.14 = (bf16[80,512]{1,0:T(8,128)(2,1)S(1)}, bf16[80,512]{1,0:T(8,128)(2,1)S(1)}, u32[]{:S(2)}, u32[]{:S(2)}) collective-permute-start(bf16[80,512]{1,0:T(8,128)(2,1)S(1)} %give.3), channel_id=1, source_target_pairs={{0,3},{1,2},{2,1},{3,0},{4,7},{5,6},{6,5},{7,4},{8,11},{9,10},{10,... | collective-permute-start | bytes 245768 | tf_op jit(solution)/shard_map/ppermute | solution.py:287
  29.1 0.8 %collective-permute-start.12 = (bf16[80,512]{1,0:T(8,128)(2,1)S(1)}, bf16[80,512]{1,0:T(8,128)(2,1)S(1)}, u32[]{:S(2)}, u32[]{:S(2)}) collective-permute-start(bf16[80,512]{1,0:T(8,128)(2,1)S(1)} %get-tuple-element.41), channel_id=1, source_target_pairs={{0,1},{1,0},{2,3},{3,2},{4,5},{5,4},{6,7},{7,6},{8,9},{9,8},{10,11... | collective-permute-start | bytes 245768 | tf_op jit(solution)/shard_map/ppermute | solution.py:287
  29.8 1.3 %keep.1 = (f32[72,512]{1,0:T(8,128)S(1)}, f32[1,512]{1,0:T(1,128)}) custom-call(f32[1536,1536]{1,0:T(8,128)S(1)} %get-tuple-element.26.k_near.refs_0_, f32[2048,512]{1,0:T(8,128)S(1)} %get-tuple-element.33.k_side.refs_1_, bf16[128,2048]{1,0:T(8,128)(2,1)S(1)} %vectors.1.vec_all.refs_2_, f32[1,2048]{1,0:T(1,128)S(1)} %get-tuple-element.44.refs_3_, ...), custom_call_target="tpu_custom_call" | custom-call | tf_op jit(solution)/shard_map/keep/pallas_call | solution.py:148
  31.1 1.2 %collective-permute-done.14.refs_2_ = bf16[80,512]{1,0:T(8,128)(2,1)S(1)} collective-permute-done((bf16[80,512]{1,0:T(8,128)(2,1)S(1)}, bf16[80,512]{1,0:T(8,128)(2,1)S(1)}, u32[]{:S(2)}, u32[]{:S(2)}) %collective-permute-start.14) | collective-permute-done | bytes 81952 | tf_op jit(solution)/shard_map/ppermute | solution.py:287
  32.2 1.3 %collective-permute-done.13.refs_1_ = bf16[80,512]{1,0:T(8,128)(2,1)S(1)} collective-permute-done((bf16[80,512]{1,0:T(8,128)(2,1)S(1)}, bf16[80,512]{1,0:T(8,128)(2,1)S(1)}, u32[]{:S(2)}, u32[]{:S(2)}) %collective-permute-start.13) | collective-permute-done | bytes 81952 | tf_op jit(solution)/shard_map/ppermute | solution.py:287
  33.5 0.1 collective-permute-done.12.refs_0_
  33.6 0.7 %finish.1 = f32[64,512]{1,0:T(8,128)} custom-call(f32[72,512]{1,0:T(8,128)S(1)} %get-tuple-element.40.near_ref, bf16[80,512]{1,0:T(8,128)(2,1)S(1)} %collective-permute-done.12.refs_0_, bf16[80,512]{1,0:T(8,128)(2,1)S(1)} %collective-permute-done.13.refs_1_, bf16[80,512]{1,0:T(8,128)(2,1)S(1)} %collective-permute-done.14.refs_2_), custom_call_target="tpu_custom_call" | custom-call | tf_op jit(solution)/shard_map/finish/pallas_call | solution.py:148
  (10 shorter events, 0.1 us)
Async XLA Ops:
  0.6 9.4 %collective-permute-start.1 = (bf16[512,128]{1,0:T(8,128)(2,1)}, bf16[512,128]{1,0:T(8,128)(2,1)S(1)}, u32[]{:S(2)}, u32[]{:S(2)}) collective-permute-start(bf16[512,128]{1,0:T(8,128)(2,1)} %points_ref.1), channel_id=1, source_target_pairs={{0,2},{1,3},{2,0},{3,1},{4,6},{5,7},{6,4},{7,5},{8,10},{9,11},{10,... | collective-permute-start | bytes 393224 | tf_op jit(solution)/shard_map/ppermute | solution.py:287
  3.7 8.9 %collective-permute-start.3 = (bf16[512,128]{1,0:T(8,128)(2,1)}, bf16[512,128]{1,0:T(8,128)(2,1)S(1)}, u32[]{:S(2)}, u32[]{:S(2)}) collective-permute-start(bf16[512,128]{1,0:T(8,128)(2,1)} %points_ref.1), channel_id=1, source_target_pairs={{0,4},{1,5},{2,6},{3,7},{4,0},{5,1},{6,2},{7,3},{8,12},{9,13},{10,... | collective-permute-start | bytes 393224 | tf_op jit(solution)/shard_map/ppermute | solution.py:287
  6.3 6.7 %collective-permute-start = (bf16[512,128]{1,0:T(8,128)(2,1)}, bf16[512,128]{1,0:T(8,128)(2,1)S(1)}, u32[]{:S(2)}, u32[]{:S(2)}) collective-permute-start(bf16[512,128]{1,0:T(8,128)(2,1)} %points_ref.1), channel_id=1, source_target_pairs={{0,1},{1,0},{2,3},{3,2},{4,5},{5,4},{6,7},{7,6},{8,9},{9,8},{10,11... | collective-permute-start | bytes 393224 | tf_op jit(solution)/shard_map/ppermute | solution.py:287
  7.8 5.2 %collective-permute-start.2 = (bf16[512,128]{1,0:T(8,128)(2,1)}, bf16[512,128]{1,0:T(8,128)(2,1)S(1)}, u32[]{:S(2)}, u32[]{:S(2)}) collective-permute-start(bf16[512,128]{1,0:T(8,128)(2,1)} %points_ref.1), channel_id=1, source_target_pairs={{0,8},{8,0},{1,9},{9,1},{2,10},{10,2},{3,11},{11,3},{4,12},{12,4},... | collective-permute-start | bytes 393224 | tf_op jit(solution)/shard_map/ppermute | solution.py:290
  7.8 0.9 %copy-start = (bf16[512,128]{1,0:T(8,128)(2,1)S(1)}, bf16[512,128]{1,0:T(8,128)(2,1)}, u32[]{:S(2)}) copy-start(bf16[512,128]{1,0:T(8,128)(2,1)} %points_ref.1) | copy-start | bytes 393220
  10.0 5.9 %collective-permute-start.4 = (bf16[512,128]{1,0:T(8,128)(2,1)S(1)}, bf16[512,128]{1,0:T(8,128)(2,1)S(1)}, u32[]{:S(2)}, u32[]{:S(2)}) collective-permute-start(bf16[512,128]{1,0:T(8,128)(2,1)S(1)} %collective-permute-done.1.refs_1_), channel_id=1, source_target_pairs={{0,1},{1,0},{2,3},{3,2},{4,5},{5,4},{6,7},{7,6},{8,9},{9,8},{10,11... | collective-permute-start | bytes 393224 | tf_op jit(solution)/shard_map/ppermute | solution.py:287
  12.7 4.0 %collective-permute-start.5 = (bf16[512,128]{1,0:T(8,128)(2,1)S(1)}, bf16[512,128]{1,0:T(8,128)(2,1)S(1)}, u32[]{:S(2)}, u32[]{:S(2)}) collective-permute-start(bf16[512,128]{1,0:T(8,128)(2,1)S(1)} %collective-permute-done.3.refs_4_), channel_id=1, source_target_pairs={{0,8},{8,0},{1,9},{9,1},{2,10},{10,2},{3,11},{11,3},{4,12},{12,4},... | collective-permute-start | bytes 393224 | tf_op jit(solution)/shard_map/ppermute | solution.py:290
  12.7 6.9 %collective-permute-start.7 = (bf16[64,512]{1,0:T(8,128)(2,1)}, bf16[64,512]{1,0:T(8,128)(2,1)S(1)}, u32[]{:S(2)}, u32[]{:S(2)}) collective-permute-start(bf16[64,512]{1,0:T(8,128)(2,1)} %bitcast.vector_ref), channel_id=1, source_target_pairs={{0,4},{1,5},{2,6},{3,7},{4,0},{5,1},{6,2},{7,3},{8,12},{9,13},{10,... | collective-permute-start | bytes 196616 | tf_op jit(solution)/shard_map/ppermute | solution.py:287
  17.6 4.6 %collective-permute-start.8 = (f32[1,2048]{1,0:T(1,128)S(1)}, f32[1,2048]{1,0:T(1,128)S(1)}, u32[]{:S(2)}, u32[]{:S(2)}) collective-permute-start(f32[1,2048]{1,0:T(1,128)S(1)} %get-tuple-element.36.refs_0_), channel_id=1, source_target_pairs={{0,4},{1,5},{2,6},{3,7},{4,0},{5,1},{6,2},{7,3},{8,12},{9,13},{10,... | collective-permute-start | bytes 24584 | tf_op jit(solution)/shard_map/ppermute | solution.py:287
  19.4 3.4 %collective-permute-start.6 = (bf16[64,512]{1,0:T(8,128)(2,1)}, bf16[64,512]{1,0:T(8,128)(2,1)S(1)}, u32[]{:S(2)}, u32[]{:S(2)}) collective-permute-start(bf16[64,512]{1,0:T(8,128)(2,1)} %bitcast.vector_ref), channel_id=1, source_target_pairs={{0,8},{8,0},{1,9},{9,1},{2,10},{10,2},{3,11},{11,3},{4,12},{12,4},... | collective-permute-start | bytes 196616 | tf_op jit(solution)/shard_map/ppermute | solution.py:290
  22.2 1.3 %collective-permute-start.9 = (bf16[64,512]{1,0:T(8,128)(2,1)S(1)}, bf16[64,512]{1,0:T(8,128)(2,1)S(1)}, u32[]{:S(2)}, u32[]{:S(2)}) collective-permute-start(bf16[64,512]{1,0:T(8,128)(2,1)S(1)} %collective-permute-done.7.refs_2_), channel_id=1, source_target_pairs={{0,8},{8,0},{1,9},{9,1},{2,10},{10,2},{3,11},{11,3},{4,12},{12,4},... | collective-permute-start | bytes 196616 | tf_op jit(solution)/shard_map/ppermute | solution.py:290
  22.3 1.3 %collective-permute-start.10 = (f32[1,2048]{1,0:T(1,128)S(1)}, f32[1,2048]{1,0:T(1,128)S(1)}, u32[]{:S(2)}, u32[]{:S(2)}) collective-permute-start(f32[1,2048]{1,0:T(1,128)S(1)} %get-tuple-element.36.refs_0_), channel_id=1, source_target_pairs={{0,8},{8,0},{1,9},{9,1},{2,10},{10,2},{3,11},{11,3},{4,12},{12,4},... | collective-permute-start | bytes 24584 | tf_op jit(solution)/shard_map/ppermute | solution.py:290
  22.8 1.2 %collective-permute-start.11 = (f32[1,2048]{1,0:T(1,128)S(1)}, f32[1,2048]{1,0:T(1,128)S(1)}, u32[]{:S(2)}, u32[]{:S(2)}) collective-permute-start(f32[1,2048]{1,0:T(1,128)S(1)} %collective-permute-done.8.refs_2_), channel_id=1, source_target_pairs={{0,8},{8,0},{1,9},{9,1},{2,10},{10,2},{3,11},{11,3},{4,12},{12,4},... | collective-permute-start | bytes 24584 | tf_op jit(solution)/shard_map/ppermute | solution.py:290
  26.3 6.0 %collective-permute-start.14 = (bf16[80,512]{1,0:T(8,128)(2,1)S(1)}, bf16[80,512]{1,0:T(8,128)(2,1)S(1)}, u32[]{:S(2)}, u32[]{:S(2)}) collective-permute-start(bf16[80,512]{1,0:T(8,128)(2,1)S(1)} %give.3), channel_id=1, source_target_pairs={{0,3},{1,2},{2,1},{3,0},{4,7},{5,6},{6,5},{7,4},{8,11},{9,10},{10,... | collective-permute-start | bytes 245768 | tf_op jit(solution)/shard_map/ppermute | solution.py:287
  29.0 4.4 %collective-permute-start.13 = (bf16[80,512]{1,0:T(8,128)(2,1)S(1)}, bf16[80,512]{1,0:T(8,128)(2,1)S(1)}, u32[]{:S(2)}, u32[]{:S(2)}) collective-permute-start(bf16[80,512]{1,0:T(8,128)(2,1)S(1)} %give.2), channel_id=1, source_target_pairs={{0,2},{1,3},{2,0},{3,1},{4,6},{5,7},{6,4},{7,5},{8,10},{9,11},{10,... | collective-permute-start | bytes 245768 | tf_op jit(solution)/shard_map/ppermute | solution.py:287
  29.1 4.6 %collective-permute-start.12 = (bf16[80,512]{1,0:T(8,128)(2,1)S(1)}, bf16[80,512]{1,0:T(8,128)(2,1)S(1)}, u32[]{:S(2)}, u32[]{:S(2)}) collective-permute-start(bf16[80,512]{1,0:T(8,128)(2,1)S(1)} %get-tuple-element.41), channel_id=1, source_target_pairs={{0,1},{1,0},{2,3},{3,2},{4,5},{5,4},{6,7},{7,6},{8,9},{9,8},{10,11... | collective-permute-start | bytes 245768 | tf_op jit(solution)/shard_map/ppermute | solution.py:287

commit v6 on v5

--- a/solution.py
+++ b/solution.py
@@ -238,16 +238,15 @@
         out_ref[width:, r : r + bm] = tail.astype(jnp.bfloat16)
 
 
-def first_give_body(unit, points_all, first, bm, n_sums, k_near, k_side, vec_all, *refs):
+def give_body(unit, points_all, bm, n_sums, k_near, k_last, k_side, vec_all, *refs):
     sums = refs[:n_sums]
-    out_ref, inverse_ref, density_ref = refs[n_sums:]
+    *outs, inverse_ref, density_ref = refs[n_sums:]
     density_body(unit, points_all, sums, inverse_ref, density_ref)
-    give(out_ref, [k_near, k_side], [first, first], inverse_ref, vec_all, bm)
-
-
-def next_give_body(firsts, bm, *refs):
-    *k_refs, vec_all, inverse_ref, out_ref = refs
-    give(out_ref, k_refs, firsts, inverse_ref, vec_all, bm)
+    for u, out_ref in enumerate(outs, 1):
+        last = u == len(outs)
+        k_refs = [k_last if last else k_near, k_side]
+        firsts = [0 if last else u * unit, u * unit]
+        give(out_ref, k_refs, firsts, inverse_ref, vec_all, bm)
 
 
 def keep_body(bm, *refs):
@@ -330,34 +329,19 @@
     )
 
     packed = pltpu.VMEM((width + 16, unit), jnp.bfloat16)
-    away, inverse, density = on_chip(
-        functools.partial(first_give_body, unit, points_all, unit, 512, len(all_sums)),
-        (
-            packed,
-            pltpu.VMEM((1, n_wide), jnp.float32),
-            pltpu.VMEM((1, unit), jnp.float32),
-        ),
-        "give_first",
+    *away, inverse, density = on_chip(
+        functools.partial(give_body, unit, points_all, 512, len(all_sums)),
+        (packed,) * (n_units - 1)
+        + (pltpu.VMEM((1, n_wide), jnp.float32), pltpu.VMEM((1, unit), jnp.float32)),
+        "give",
         8,
         k_near,
+        k_last,
         k_side,
         vec_all,
         *all_sums,
     )
-    back = [across(away, 1)]
-    for u in range(2, n_units):
-        last = u == n_units - 1
-        (away,) = on_chip(
-            functools.partial(next_give_body, [0 if last else u * unit, u * unit], 512),
-            (packed,),
-            "give",
-            8,
-            k_last if last else k_near,
-            k_side,
-            vec_all,
-            after(inverse, away),
-        )
-        back.append(across(away, u))
+    back = [across(x, u) for u, x in enumerate(away, 1)]
     near, log_density = on_chip(
         functools.partial(keep_body, 512),
         (
@@ -378,7 +362,7 @@
         "finish",
         8,
         near,
-        *back,
+        *back[::-1],
     )
     return (smoothed.T, log_density.reshape(unit))
 

time: 34.5 us -> 34.1 us (0.988)
  Pallas kernels: 9.19 us -> 8.77 us
    pallas_call x10 -> x8, Pallas kernels: 9.19 us -> 8.77 us  [on_chip(): pl.pallas_call(body, out_shape=tuple(shapes), in_specs=[VMEM_SPEC] * len(...]
where the time goes in v6:
time: 34.1 us; the launch traced here: 33.9 us
  starting transfers between devices  14.4 us (42%)
  waiting for transfers between devices  9.1 us (27%)
  Pallas kernels  8.77 us (26%)
  local copies, waits for them, and re-layouts  0.93 us (3%)
  between operations  0.69 us (2%)
    ppermute x9, starting transfers between devices, across(): return lax.ppermute(x, 'col', [(i, i ^ mask) for i in range(n_col)])  13.9 us
    pallas_call x8, Pallas kernels, on_chip(): pl.pallas_call(body, out_shape=tuple(shapes), in_specs=[VMEM_SPEC] * len(...  8.77 us
    ppermute x9, waiting for transfers between devices, across(): return lax.ppermute(x, 'col', [(i, i ^ mask) for i in range(n_col)])  7.97 us
    ppermute x6, waiting for transfers between devices, sibling(): return lax.ppermute(x, 'row', [(0, 1), (1, 0)])  1.13 us
    unnamed x2, local copies, waits for them, and re-layouts  0.93 us
  transfers between devices with their start and end apart: 15, of which 9 were waited for; matrix products, arithmetic and copies ran while one was open for 0% of the time, Pallas kernels for 18%

profile of v6, /device:TPU:0, one launch (start us, length us, event | category | flops | bytes accessed | tf_op | source)
XLA Modules:
  0.0 33.9 jit_solution(3255899118054095631)
XLA Ops:
  0.6 3.1 %collective-permute-start.1 = (bf16[512,128]{1,0:T(8,128)(2,1)}, bf16[512,128]{1,0:T(8,128)(2,1)S(1)}, u32[]{:S(2)}, u32[]{:S(2)}) collective-permute-start(bf16[512,128]{1,0:T(8,128)(2,1)} %points_ref.1), channel_id=1, source_target_pairs={{0,2},{1,3},{2,0},{3,1},{4,6},{5,7},{6,4},{7,5},{8,10},{9,11},{10,... | collective-permute-start | bytes 393224 | tf_op jit(solution)/shard_map/ppermute | solution.py:286
  3.7 2.6 %collective-permute-start.3 = (bf16[512,128]{1,0:T(8,128)(2,1)}, bf16[512,128]{1,0:T(8,128)(2,1)S(1)}, u32[]{:S(2)}, u32[]{:S(2)}) collective-permute-start(bf16[512,128]{1,0:T(8,128)(2,1)} %points_ref.1), channel_id=1, source_target_pairs={{0,4},{1,5},{2,6},{3,7},{4,0},{5,1},{6,2},{7,3},{8,12},{9,13},{10,... | collective-permute-start | bytes 393224 | tf_op jit(solution)/shard_map/ppermute | solution.py:286
  6.3 1.5 %collective-permute-start = (bf16[512,128]{1,0:T(8,128)(2,1)}, bf16[512,128]{1,0:T(8,128)(2,1)S(1)}, u32[]{:S(2)}, u32[]{:S(2)}) collective-permute-start(bf16[512,128]{1,0:T(8,128)(2,1)} %points_ref.1), channel_id=1, source_target_pairs={{0,1},{1,0},{2,3},{3,2},{4,5},{5,4},{6,7},{7,6},{8,9},{9,8},{10,11... | collective-permute-start | bytes 393224 | tf_op jit(solution)/shard_map/ppermute | solution.py:286
  7.8 0.0 collective-permute-start.2
  7.8 0.9 %copy-done = bf16[512,128]{1,0:T(8,128)(2,1)S(1)} copy-done((bf16[512,128]{1,0:T(8,128)(2,1)S(1)}, bf16[512,128]{1,0:T(8,128)(2,1)}, u32[]{:S(2)}) %copy-start) | copy-done | bytes 131096
  8.8 1.2 %own.1 = (bf16[512,256]{1,0:T(8,128)(2,1)S(1)}, bf16[512,256]{1,0:T(8,128)(2,1)S(1)}, bf16[64,512]{1,0:T(8,128)(2,1)S(1)}) custom-call(bf16[512,128]{1,0:T(8,128)(2,1)S(1)} %copy-done, bf16[64,512]{1,0:T(8,128)(2,1)} %bitcast.vector_ref), custom_call_target="tpu_custom_call" | custom-call | tf_op jit(solution)/shard_map/own/pallas_call | solution.py:148
  10.0 0.0 collective-permute-done.1.refs_1_
  10.0 1.1 %collective-permute-start.4 = (bf16[512,128]{1,0:T(8,128)(2,1)S(1)}, bf16[512,128]{1,0:T(8,128)(2,1)S(1)}, u32[]{:S(2)}, u32[]{:S(2)}) collective-permute-start(bf16[512,128]{1,0:T(8,128)(2,1)S(1)} %collective-permute-done.1.refs_1_), channel_id=1, source_target_pairs={{0,1},{1,0},{2,3},{3,2},{4,5},{5,4},{6,7},{7,6},{8,9},{9,8},{10,11... | collective-permute-start | bytes 393224 | tf_op jit(solution)/shard_map/ppermute | solution.py:286
  11.1 1.6 %collective-permute-done.3.refs_4_ = bf16[512,128]{1,0:T(8,128)(2,1)S(1)} collective-permute-done((bf16[512,128]{1,0:T(8,128)(2,1)}, bf16[512,128]{1,0:T(8,128)(2,1)S(1)}, u32[]{:S(2)}, u32[]{:S(2)}) %collective-permute-start.3) | collective-permute-done | bytes 131104 | tf_op jit(solution)/shard_map/ppermute | solution.py:286
  12.7 0.3 collective-permute-start.7
  13.0 2.0 %near.1 = (f32[1536,1536]{1,0:T(8,128)S(1)}, f32[1,1536]{1,0:T(1,128)S(1)}, bf16[1024,256]{1,0:T(8,128)(2,1)S(1)}, bf16[1024,256]{1,0:T(8,128)(2,1)S(1)}) custom-call(bf16[512,128]{1,0:T(8,128)(2,1)S(1)} %collective-permute-done.refs_0_, bf16[512,128]{1,0:T(8,128)(2,1)S(1)} %collective-permute-done.1.refs_1_, ...), custom_call_target="tpu_custom_call" | custom-call | tf_op jit(solution)/shard_map/near/pallas_call | solution.py:148
  15.0 1.0 %collective-permute-done.4.refs_0_ = bf16[512,128]{1,0:T(8,128)(2,1)S(1)} collective-permute-done((bf16[512,128]{1,0:T(8,128)(2,1)S(1)}, bf16[512,128]{1,0:T(8,128)(2,1)S(1)}, u32[]{:S(2)}, u32[]{:S(2)}) %collective-permute-start.4) | collective-permute-done | bytes 131104 | tf_op jit(solution)/shard_map/ppermute | solution.py:286
  15.9 0.7 %last.1 = (f32[512,1536]{1,0:T(8,128)S(1)}, f32[1,1536]{1,0:T(1,128)S(1)}, bf16[512,256]{1,0:T(8,128)(2,1)S(1)}) custom-call(bf16[512,128]{1,0:T(8,128)(2,1)S(1)} %collective-permute-done.4.refs_0_, bf16[512,256]{1,0:T(8,128)(2,1)S(1)} %get-tuple-element.25.refs_5_.refs_1_, bf16[1024,256]{1,0:T(8,128)(2,1)S(1)} %get-tuple-element.28.refs_2_, ...), custom_call_target="tpu_custom_call" | custom-call | tf_op jit(solution)/shard_map/last/pallas_call | solution.py:148
  16.7 0.9 %side.1 = (f32[2048,512]{1,0:T(8,128)S(1)}, f32[1,2048]{1,0:T(1,128)S(1)}) custom-call(bf16[512,256]{1,0:T(8,128)(2,1)S(1)} %get-tuple-element.24.refs_2_.refs_0_, bf16[1024,256]{1,0:T(8,128)(2,1)S(1)} %get-tuple-element.27.refs_1_, bf16[512,256]{1,0:T(8,128)(2,1)S(1)} %get-tuple-element.30.refs_2_, bf16[512,128]{1,0:T(8,128)(2,1)S(1)} %collective-permute-done.5.refs_3_, ...), custom_call_target="tpu_custom_call" | custom-call | tf_op jit(solution)/shard_map/side/pallas_call | solution.py:148
  17.6 1.7 %collective-permute-start.8 = (f32[1,2048]{1,0:T(1,128)S(1)}, f32[1,2048]{1,0:T(1,128)S(1)}, u32[]{:S(2)}, u32[]{:S(2)}) collective-permute-start(f32[1,2048]{1,0:T(1,128)S(1)} %get-tuple-element.36.refs_0_), channel_id=1, source_target_pairs={{0,4},{1,5},{2,6},{3,7},{4,0},{5,1},{6,2},{7,3},{8,12},{9,13},{10,... | collective-permute-start | bytes 24584 | tf_op jit(solution)/shard_map/ppermute | solution.py:286
  19.4 0.2 collective-permute-done.7.refs_2_
  19.5 2.7 %collective-permute-done.8.refs_2_ = f32[1,2048]{1,0:T(1,128)S(1)} collective-permute-done((f32[1,2048]{1,0:T(1,128)S(1)}, f32[1,2048]{1,0:T(1,128)S(1)}, u32[]{:S(2)}, u32[]{:S(2)}) %collective-permute-start.8) | collective-permute-done | bytes 8224 | tf_op jit(solution)/shard_map/ppermute | solution.py:286
  22.3 0.5 %collective-permute-start.10 = (f32[1,2048]{1,0:T(1,128)S(1)}, f32[1,2048]{1,0:T(1,128)S(1)}, u32[]{:S(2)}, u32[]{:S(2)}) collective-permute-start(f32[1,2048]{1,0:T(1,128)S(1)} %get-tuple-element.36.refs_0_), channel_id=1, source_target_pairs={{0,8},{8,0},{1,9},{9,1},{2,10},{10,2},{3,11},{11,3},{4,12},{12,4},... | collective-permute-start | bytes 24584 | tf_op jit(solution)/shard_map/ppermute | solution.py:289
  22.8 0.0 collective-permute-start.11
  22.8 0.0 collective-permute-done.6.refs_1_
  22.8 0.7 %collective-permute-done.9.refs_3_ = bf16[64,512]{1,0:T(8,128)(2,1)S(1)} collective-permute-done((bf16[64,512]{1,0:T(8,128)(2,1)S(1)}, bf16[64,512]{1,0:T(8,128)(2,1)S(1)}, u32[]{:S(2)}, u32[]{:S(2)}) %collective-permute-start.9) | collective-permute-done | bytes 65568 | tf_op jit(solution)/shard_map/ppermute | solution.py:289
  23.5 0.0 collective-permute-done.10.refs_1_
  23.6 0.3 %collective-permute-done.11.refs_3_ = f32[1,2048]{1,0:T(1,128)S(1)} collective-permute-done((f32[1,2048]{1,0:T(1,128)S(1)}, f32[1,2048]{1,0:T(1,128)S(1)}, u32[]{:S(2)}, u32[]{:S(2)}) %collective-permute-start.11) | collective-permute-done | bytes 8224 | tf_op jit(solution)/shard_map/ppermute | solution.py:289
  23.9 1.9 %give.1 = (bf16[80,512]{1,0:T(8,128)(2,1)S(1)}, bf16[80,512]{1,0:T(8,128)(2,1)S(1)}, bf16[80,512]{1,0:T(8,128)(2,1)S(1)}, f32[1,2048]{1,0:T(1,128)S(1)}, f32[1,512]{1,0:T(1,128)S(1)}) custom-call(f32[1536,1536]{1,0:T(8,128)S(1)} %get-tuple-element.26.k_near.refs_0_, f32[512,1536]{1,0:T(8,128)S(1)} %get-tuple-element.38.k_last, ...), custom_call_target="tpu_custom_call" | custom-call | tf_op jit(solution)/shard_map/give/pallas_call | solution.py:148
  25.8 2.8 %collective-permute-start.12 = (bf16[80,512]{1,0:T(8,128)(2,1)S(1)}, bf16[80,512]{1,0:T(8,128)(2,1)S(1)}, u32[]{:S(2)}, u32[]{:S(2)}) collective-permute-start(bf16[80,512]{1,0:T(8,128)(2,1)S(1)} %get-tuple-element.42), channel_id=1, source_target_pairs={{0,3},{1,2},{2,1},{3,0},{4,7},{5,6},{6,5},{7,4},{8,11},{9,10},{10,... | collective-permute-start | bytes 245768 | tf_op jit(solution)/shard_map/ppermute | solution.py:286
  28.6 0.0 collective-permute-start.13
  28.6 0.8 %collective-permute-start.14 = (bf16[80,512]{1,0:T(8,128)(2,1)S(1)}, bf16[80,512]{1,0:T(8,128)(2,1)S(1)}, u32[]{:S(2)}, u32[]{:S(2)}) collective-permute-start(bf16[80,512]{1,0:T(8,128)(2,1)S(1)} %get-tuple-element.44), channel_id=1, source_target_pairs={{0,1},{1,0},{2,3},{3,2},{4,5},{5,4},{6,7},{7,6},{8,9},{9,8},{10,11... | collective-permute-start | bytes 245768 | tf_op jit(solution)/shard_map/ppermute | solution.py:286
  29.4 1.3 %keep.1 = (f32[72,512]{1,0:T(8,128)S(1)}, f32[1,512]{1,0:T(1,128)}) custom-call(f32[1536,1536]{1,0:T(8,128)S(1)} %get-tuple-element.26.k_near.refs_0_, f32[2048,512]{1,0:T(8,128)S(1)} %get-tuple-element.33.k_side.refs_1_, bf16[128,2048]{1,0:T(8,128)(2,1)S(1)} %vectors.1.vec_all.refs_2_, f32[1,2048]{1,0:T(1,128)S(1)} %get-tuple-element.39.refs_3_, ...), custom_call_target="tpu_custom_call" | custom-call | tf_op jit(solution)/shard_map/keep/pallas_call | solution.py:148
  30.6 1.1 %collective-permute-done.12.refs_0_ = bf16[80,512]{1,0:T(8,128)(2,1)S(1)} collective-permute-done((bf16[80,512]{1,0:T(8,128)(2,1)S(1)}, bf16[80,512]{1,0:T(8,128)(2,1)S(1)}, u32[]{:S(2)}, u32[]{:S(2)}) %collective-permute-start.12) | collective-permute-done | bytes 81952 | tf_op jit(solution)/shard_map/ppermute | solution.py:286
  31.8 1.3 %collective-permute-done.13.refs_1_ = bf16[80,512]{1,0:T(8,128)(2,1)S(1)} collective-permute-done((bf16[80,512]{1,0:T(8,128)(2,1)S(1)}, bf16[80,512]{1,0:T(8,128)(2,1)S(1)}, u32[]{:S(2)}, u32[]{:S(2)}) %collective-permute-start.13) | collective-permute-done | bytes 81952 | tf_op jit(solution)/shard_map/ppermute | solution.py:286
  33.1 0.1 collective-permute-done.14.refs_2_
  33.2 0.7 %finish.1 = f32[64,512]{1,0:T(8,128)} custom-call(f32[72,512]{1,0:T(8,128)S(1)} %get-tuple-element.41.near_ref, bf16[80,512]{1,0:T(8,128)(2,1)S(1)} %collective-permute-done.12.refs_0_, bf16[80,512]{1,0:T(8,128)(2,1)S(1)} %collective-permute-done.13.refs_1_, bf16[80,512]{1,0:T(8,128)(2,1)S(1)} %collective-permute-done.14.refs_2_), custom_call_target="tpu_custom_call" | custom-call | tf_op jit(solution)/shard_map/finish/pallas_call | solution.py:148
  (8 shorter events, 0.1 us)
Async XLA Ops:
  0.6 9.4 %collective-permute-start.1 = (bf16[512,128]{1,0:T(8,128)(2,1)}, bf16[512,128]{1,0:T(8,128)(2,1)S(1)}, u32[]{:S(2)}, u32[]{:S(2)}) collective-permute-start(bf16[512,128]{1,0:T(8,128)(2,1)} %points_ref.1), channel_id=1, source_target_pairs={{0,2},{1,3},{2,0},{3,1},{4,6},{5,7},{6,4},{7,5},{8,10},{9,11},{10,... | collective-permute-start | bytes 393224 | tf_op jit(solution)/shard_map/ppermute | solution.py:286
  3.7 8.9 %collective-permute-start.3 = (bf16[512,128]{1,0:T(8,128)(2,1)}, bf16[512,128]{1,0:T(8,128)(2,1)S(1)}, u32[]{:S(2)}, u32[]{:S(2)}) collective-permute-start(bf16[512,128]{1,0:T(8,128)(2,1)} %points_ref.1), channel_id=1, source_target_pairs={{0,4},{1,5},{2,6},{3,7},{4,0},{5,1},{6,2},{7,3},{8,12},{9,13},{10,... | collective-permute-start | bytes 393224 | tf_op jit(solution)/shard_map/ppermute | solution.py:286
  6.3 6.7 %collective-permute-start = (bf16[512,128]{1,0:T(8,128)(2,1)}, bf16[512,128]{1,0:T(8,128)(2,1)S(1)}, u32[]{:S(2)}, u32[]{:S(2)}) collective-permute-start(bf16[512,128]{1,0:T(8,128)(2,1)} %points_ref.1), channel_id=1, source_target_pairs={{0,1},{1,0},{2,3},{3,2},{4,5},{5,4},{6,7},{7,6},{8,9},{9,8},{10,11... | collective-permute-start | bytes 393224 | tf_op jit(solution)/shard_map/ppermute | solution.py:286
  7.8 5.2 %collective-permute-start.2 = (bf16[512,128]{1,0:T(8,128)(2,1)}, bf16[512,128]{1,0:T(8,128)(2,1)S(1)}, u32[]{:S(2)}, u32[]{:S(2)}) collective-permute-start(bf16[512,128]{1,0:T(8,128)(2,1)} %points_ref.1), channel_id=1, source_target_pairs={{0,8},{8,0},{1,9},{9,1},{2,10},{10,2},{3,11},{11,3},{4,12},{12,4},... | collective-permute-start | bytes 393224 | tf_op jit(solution)/shard_map/ppermute | solution.py:289
  7.8 0.9 %copy-start = (bf16[512,128]{1,0:T(8,128)(2,1)S(1)}, bf16[512,128]{1,0:T(8,128)(2,1)}, u32[]{:S(2)}) copy-start(bf16[512,128]{1,0:T(8,128)(2,1)} %points_ref.1) | copy-start | bytes 393220
  10.0 5.9 %collective-permute-start.4 = (bf16[512,128]{1,0:T(8,128)(2,1)S(1)}, bf16[512,128]{1,0:T(8,128)(2,1)S(1)}, u32[]{:S(2)}, u32[]{:S(2)}) collective-permute-start(bf16[512,128]{1,0:T(8,128)(2,1)S(1)} %collective-permute-done.1.refs_1_), channel_id=1, source_target_pairs={{0,1},{1,0},{2,3},{3,2},{4,5},{5,4},{6,7},{7,6},{8,9},{9,8},{10,11... | collective-permute-start | bytes 393224 | tf_op jit(solution)/shard_map/ppermute | solution.py:286
  12.7 4.0 %collective-permute-start.5 = (bf16[512,128]{1,0:T(8,128)(2,1)S(1)}, bf16[512,128]{1,0:T(8,128)(2,1)S(1)}, u32[]{:S(2)}, u32[]{:S(2)}) collective-permute-start(bf16[512,128]{1,0:T(8,128)(2,1)S(1)} %collective-permute-done.3.refs_4_), channel_id=1, source_target_pairs={{0,8},{8,0},{1,9},{9,1},{2,10},{10,2},{3,11},{11,3},{4,12},{12,4},... | collective-permute-start | bytes 393224 | tf_op jit(solution)/shard_map/ppermute | solution.py:289
  12.7 6.9 %collective-permute-start.7 = (bf16[64,512]{1,0:T(8,128)(2,1)}, bf16[64,512]{1,0:T(8,128)(2,1)S(1)}, u32[]{:S(2)}, u32[]{:S(2)}) collective-permute-start(bf16[64,512]{1,0:T(8,128)(2,1)} %bitcast.vector_ref), channel_id=1, source_target_pairs={{0,4},{1,5},{2,6},{3,7},{4,0},{5,1},{6,2},{7,3},{8,12},{9,13},{10,... | collective-permute-start | bytes 196616 | tf_op jit(solution)/shard_map/ppermute | solution.py:286
  17.6 4.6 %collective-permute-start.8 = (f32[1,2048]{1,0:T(1,128)S(1)}, f32[1,2048]{1,0:T(1,128)S(1)}, u32[]{:S(2)}, u32[]{:S(2)}) collective-permute-start(f32[1,2048]{1,0:T(1,128)S(1)} %get-tuple-element.36.refs_0_), channel_id=1, source_target_pairs={{0,4},{1,5},{2,6},{3,7},{4,0},{5,1},{6,2},{7,3},{8,12},{9,13},{10,... | collective-permute-start | bytes 24584 | tf_op jit(solution)/shard_map/ppermute | solution.py:286
  19.4 3.4 %collective-permute-start.6 = (bf16[64,512]{1,0:T(8,128)(2,1)}, bf16[64,512]{1,0:T(8,128)(2,1)S(1)}, u32[]{:S(2)}, u32[]{:S(2)}) collective-permute-start(bf16[64,512]{1,0:T(8,128)(2,1)} %bitcast.vector_ref), channel_id=1, source_target_pairs={{0,8},{8,0},{1,9},{9,1},{2,10},{10,2},{3,11},{11,3},{4,12},{12,4},... | collective-permute-start | bytes 196616 | tf_op jit(solution)/shard_map/ppermute | solution.py:289
  22.2 1.3 %collective-permute-start.9 = (bf16[64,512]{1,0:T(8,128)(2,1)S(1)}, bf16[64,512]{1,0:T(8,128)(2,1)S(1)}, u32[]{:S(2)}, u32[]{:S(2)}) collective-permute-start(bf16[64,512]{1,0:T(8,128)(2,1)S(1)} %collective-permute-done.7.refs_2_), channel_id=1, source_target_pairs={{0,8},{8,0},{1,9},{9,1},{2,10},{10,2},{3,11},{11,3},{4,12},{12,4},... | collective-permute-start | bytes 196616 | tf_op jit(solution)/shard_map/ppermute | solution.py:289
  22.3 1.3 %collective-permute-start.10 = (f32[1,2048]{1,0:T(1,128)S(1)}, f32[1,2048]{1,0:T(1,128)S(1)}, u32[]{:S(2)}, u32[]{:S(2)}) collective-permute-start(f32[1,2048]{1,0:T(1,128)S(1)} %get-tuple-element.36.refs_0_), channel_id=1, source_target_pairs={{0,8},{8,0},{1,9},{9,1},{2,10},{10,2},{3,11},{11,3},{4,12},{12,4},... | collective-permute-start | bytes 24584 | tf_op jit(solution)/shard_map/ppermute | solution.py:289
  22.8 1.2 %collective-permute-start.11 = (f32[1,2048]{1,0:T(1,128)S(1)}, f32[1,2048]{1,0:T(1,128)S(1)}, u32[]{:S(2)}, u32[]{:S(2)}) collective-permute-start(f32[1,2048]{1,0:T(1,128)S(1)} %collective-permute-done.8.refs_2_), channel_id=1, source_target_pairs={{0,8},{8,0},{1,9},{9,1},{2,10},{10,2},{3,11},{11,3},{4,12},{12,4},... | collective-permute-start | bytes 24584 | tf_op jit(solution)/shard_map/ppermute | solution.py:289
  25.8 6.0 %collective-permute-start.12 = (bf16[80,512]{1,0:T(8,128)(2,1)S(1)}, bf16[80,512]{1,0:T(8,128)(2,1)S(1)}, u32[]{:S(2)}, u32[]{:S(2)}) collective-permute-start(bf16[80,512]{1,0:T(8,128)(2,1)S(1)} %get-tuple-element.42), channel_id=1, source_target_pairs={{0,3},{1,2},{2,1},{3,0},{4,7},{5,6},{6,5},{7,4},{8,11},{9,10},{10,... | collective-permute-start | bytes 245768 | tf_op jit(solution)/shard_map/ppermute | solution.py:286
  28.6 4.4 %collective-permute-start.13 = (bf16[80,512]{1,0:T(8,128)(2,1)S(1)}, bf16[80,512]{1,0:T(8,128)(2,1)S(1)}, u32[]{:S(2)}, u32[]{:S(2)}) collective-permute-start(bf16[80,512]{1,0:T(8,128)(2,1)S(1)} %get-tuple-element.43), channel_id=1, source_target_pairs={{0,2},{1,3},{2,0},{3,1},{4,6},{5,7},{6,4},{7,5},{8,10},{9,11},{10,... | collective-permute-start | bytes 245768 | tf_op jit(solution)/shard_map/ppermute | solution.py:286
  28.6 4.6 %collective-permute-start.14 = (bf16[80,512]{1,0:T(8,128)(2,1)S(1)}, bf16[80,512]{1,0:T(8,128)(2,1)S(1)}, u32[]{:S(2)}, u32[]{:S(2)}) collective-permute-start(bf16[80,512]{1,0:T(8,128)(2,1)S(1)} %get-tuple-element.44), channel_id=1, source_target_pairs={{0,1},{1,0},{2,3},{3,2},{4,5},{5,4},{6,7},{7,6},{8,9},{9,8},{10,11... | collective-permute-start | bytes 245768 | tf_op jit(solution)/shard_map/ppermute | solution.py:286

commit v7 on v6

--- a/solution.py
+++ b/solution.py
@@ -144,6 +144,15 @@
             c_at += bn
 
 
+def last_body(unit, scale, *refs):
+    row_ref, col_own, cols_near, before, row_own, rows_near, col_ref = refs[:7]
+    k_last, k_side, sum_ref, early, row_made, col_made = refs[7:]
+    first = (row_ref, col_own, cols_near, before, k_last, early, row_made)
+    kernel_body([1, 0, 0, 2, 1, 0], unit, scale, False, 512, 256, *first)
+    second = (row_own, rows_near, row_made, col_ref, early, k_side, sum_ref, col_made)
+    kernel_body([0, 3, 1, 0, 0, 1], unit, scale, False, 512, 256, *second)
+
+
 def on_chip(body, shapes, name, limit, *args, scratch=()):
     return pl.pallas_call(
         body,
@@ -314,11 +323,25 @@
     k_near, sums_near, rows_near, cols_near = kernel_tile(
         "near", rows[:-1], [row_own], [beside, far], [col_own], diagonal=True
     )
-    k_last, sums_last, row_last = kernel_tile(
-        "last", rows[-1:], [], [], [col_own, cols_near], [sums_near]
-    )
-    k_side, sums = kernel_tile(
-        "side", [], [row_own, rows_near, row_last], [far_beside], [], [], [sums_last]
+    scale = 2.0 * math.log2(math.e) / (1.05 * math.sqrt(feats))
+    n_rows = n_units * unit
+    k_last, k_side, sums = on_chip(
+        functools.partial(last_body, unit, scale),
+        (
+            pltpu.VMEM((unit, 3 * unit), jnp.float32),
+            pltpu.VMEM((n_rows, unit), jnp.float32),
+            pltpu.VMEM((1, n_wide), jnp.float32),
+        ),
+        "last",
+        12,
+        rows[-1],
+        col_own,
+        cols_near,
+        sums_near,
+        row_own,
+        rows_near,
+        far_beside,
+        scratch=(pltpu.VMEM((1, 3 * unit), jnp.float32), augmented, augmented),
     )
     sums_far = across(sums, n_units)
     all_sums = [sums, sibling(sums), sums_far, sibling(sums_far)]

time: 34.1 us -> 34.8 us (1.021)
  starting transfers between devices: 14.4 us -> 16.1 us
  waiting for transfers between devices: 9.1 us -> 8.13 us
  Pallas kernels: 8.77 us -> 7.9 us
  local copies, waits for them, and re-layouts: 0.93 us -> 1.77 us
    ppermute x9, starting transfers between devices: 13.9 us -> 15.6 us  [across(): return lax.ppermute(x, 'col', [(i, i ^ mask) for i in range(n_col)])]
    ppermute x9, waiting for transfers between devices: 7.97 us -> 6.99 us  [across(): return lax.ppermute(x, 'col', [(i, i ^ mask) for i in range(n_col)])]
    pallas_call x8 -> x7, Pallas kernels: 8.77 us -> 7.9 us  [on_chip(): pl.pallas_call(body, out_shape=tuple(shapes), in_specs=[VMEM_SPEC] * len(...]
    unnamed x2 -> x4, local copies, waits for them, and re-layouts: 0.93 us -> 1.77 us
  transfers between devices with their start and end apart: 15 -> 15, of which waited for: 9 -> 10; matrix products, arithmetic and copies ran while one was open for 0% -> 0% of each run, Pallas kernels for 18% -> 15%
where the time goes in v7:
time: 34.8 us; the launch traced here: 34.6 us
  starting transfers between devices  16.1 us (46%)
  waiting for transfers between devices  8.13 us (23%)
  Pallas kernels  7.9 us (23%)
  local copies, waits for them, and re-layouts  1.77 us (5%)
  between operations  0.67 us (2%)
    ppermute x9, starting transfers between devices, across(): return lax.ppermute(x, 'col', [(i, i ^ mask) for i in range(n_col)])  15.6 us
    pallas_call x7, Pallas kernels, on_chip(): pl.pallas_call(body, out_shape=tuple(shapes), in_specs=[VMEM_SPEC] * len(...  7.9 us
    ppermute x9, waiting for transfers between devices, across(): return lax.ppermute(x, 'col', [(i, i ^ mask) for i in range(n_col)])  6.99 us
    unnamed x4, local copies, waits for them, and re-layouts  1.77 us
    ppermute x6, waiting for transfers between devices, sibling(): return lax.ppermute(x, 'row', [(0, 1), (1, 0)])  1.13 us
  transfers between devices with their start and end apart: 15, of which 10 were waited for; matrix products, arithmetic and copies ran while one was open for 0% of the time, Pallas kernels for 15%

profile of v7, /device:TPU:0, one launch (start us, length us, event | category | flops | bytes accessed | tf_op | source)
XLA Modules:
  0.0 34.6 jit_solution(18391530840374715808)
XLA Ops:
  0.6 4.1 %collective-permute-start.3 = (bf16[512,128]{1,0:T(8,128)(2,1)}, bf16[512,128]{1,0:T(8,128)(2,1)S(1)}, u32[]{:S(2)}, u32[]{:S(2)}) collective-permute-start(bf16[512,128]{1,0:T(8,128)(2,1)} %points_ref.1), channel_id=1, source_target_pairs={{0,4},{1,5},{2,6},{3,7},{4,0},{5,1},{6,2},{7,3},{8,12},{9,13},{10,... | collective-permute-start | bytes 393224 | tf_op jit(solution)/shard_map/ppermute | solution.py:295
  4.7 1.6 %collective-permute-start.1 = (bf16[512,128]{1,0:T(8,128)(2,1)}, bf16[512,128]{1,0:T(8,128)(2,1)S(1)}, u32[]{:S(2)}, u32[]{:S(2)}) collective-permute-start(bf16[512,128]{1,0:T(8,128)(2,1)} %points_ref.1), channel_id=1, source_target_pairs={{0,2},{1,3},{2,0},{3,1},{4,6},{5,7},{6,4},{7,5},{8,10},{9,11},{10,... | collective-permute-start | bytes 393224 | tf_op jit(solution)/shard_map/ppermute | solution.py:295
  6.3 1.5 %collective-permute-start = (bf16[512,128]{1,0:T(8,128)(2,1)}, bf16[512,128]{1,0:T(8,128)(2,1)S(1)}, u32[]{:S(2)}, u32[]{:S(2)}) collective-permute-start(bf16[512,128]{1,0:T(8,128)(2,1)} %points_ref.1), channel_id=1, source_target_pairs={{0,1},{1,0},{2,3},{3,2},{4,5},{5,4},{6,7},{7,6},{8,9},{9,8},{10,11... | collective-permute-start | bytes 393224 | tf_op jit(solution)/shard_map/ppermute | solution.py:295
  7.8 0.9 %copy-done = bf16[512,128]{1,0:T(8,128)(2,1)S(1)} copy-done((bf16[512,128]{1,0:T(8,128)(2,1)S(1)}, bf16[512,128]{1,0:T(8,128)(2,1)}, u32[]{:S(2)}) %copy-start) | copy-done | bytes 131096
  8.8 0.8 %copy-done.1 = bf16[512,64]{0,1:T(8,128)(2,1)S(1)} copy-done((bf16[512,64]{0,1:T(8,128)(2,1)S(1)}, bf16[512,64]{0,1:T(8,128)(2,1)}, u32[]{:S(2)}) %copy-start.1) | copy-done | bytes 65560
  9.6 0.4 %own.1 = (bf16[512,256]{1,0:T(8,128)(2,1)S(1)}, bf16[512,256]{1,0:T(8,128)(2,1)S(1)}, bf16[64,512]{1,0:T(8,128)(2,1)S(1)}) custom-call(bf16[512,128]{1,0:T(8,128)(2,1)S(1)} %copy-done, bf16[64,512]{1,0:T(8,128)(2,1)S(1)} %bitcast.3), custom_call_target="tpu_custom_call" | custom-call | tf_op jit(solution)/shard_map/own/pallas_call | solution.py:157
  10.0 1.4 %collective-permute-done.3.refs_4_ = bf16[512,128]{1,0:T(8,128)(2,1)S(1)} collective-permute-done((bf16[512,128]{1,0:T(8,128)(2,1)}, bf16[512,128]{1,0:T(8,128)(2,1)S(1)}, u32[]{:S(2)}, u32[]{:S(2)}) %collective-permute-start.3) | collective-permute-done | bytes 131104 | tf_op jit(solution)/shard_map/ppermute | solution.py:295
  11.4 0.2 collective-permute-done.1.refs_1_
  11.6 1.6 %collective-permute-start.4 = (bf16[512,128]{1,0:T(8,128)(2,1)S(1)}, bf16[512,128]{1,0:T(8,128)(2,1)S(1)}, u32[]{:S(2)}, u32[]{:S(2)}) collective-permute-start(bf16[512,128]{1,0:T(8,128)(2,1)S(1)} %collective-permute-done.1.refs_1_), channel_id=1, source_target_pairs={{0,1},{1,0},{2,3},{3,2},{4,5},{5,4},{6,7},{7,6},{8,9},{9,8},{10,11... | collective-permute-start | bytes 393224 | tf_op jit(solution)/shard_map/ppermute | solution.py:295
  13.1 0.0 collective-permute-start.5
  13.1 1.3 %collective-permute-start.7 = (bf16[64,512]{1,0:T(8,128)(2,1)S(1)}, bf16[64,512]{1,0:T(8,128)(2,1)S(1)}, u32[]{:S(2)}, u32[]{:S(2)}) collective-permute-start(bf16[64,512]{1,0:T(8,128)(2,1)S(1)} %bitcast.4), channel_id=1, source_target_pairs={{0,4},{1,5},{2,6},{3,7},{4,0},{5,1},{6,2},{7,3},{8,12},{9,13},{10,... | collective-permute-start | bytes 196616 | tf_op jit(solution)/shard_map/ppermute | solution.py:295
  14.4 2.0 %near.1 = (f32[1536,1536]{1,0:T(8,128)S(1)}, f32[1,1536]{1,0:T(1,128)S(1)}, bf16[1024,256]{1,0:T(8,128)(2,1)S(1)}, bf16[1024,256]{1,0:T(8,128)(2,1)S(1)}) custom-call(bf16[512,128]{1,0:T(8,128)(2,1)S(1)} %collective-permute-done.refs_0_, bf16[512,128]{1,0:T(8,128)(2,1)S(1)} %collective-permute-done.1.refs_1_, ...), custom_call_target="tpu_custom_call" | custom-call | tf_op jit(solution)/shard_map/near/pallas_call | solution.py:157
  16.4 0.1 collective-permute-done.4.refs_0_
  16.5 1.5 %last.1 = (f32[512,1536]{1,0:T(8,128)S(1)}, f32[2048,512]{1,0:T(8,128)S(1)}, f32[1,2048]{1,0:T(1,128)S(1)}) custom-call(bf16[512,128]{1,0:T(8,128)(2,1)S(1)} %collective-permute-done.4.refs_0_, bf16[512,256]{1,0:T(8,128)(2,1)S(1)} %get-tuple-element.23.refs_5_.refs_1_, bf16[1024,256]{1,0:T(8,128)(2,1)S(1)} %get-tuple-element.25.refs_2_, ...), custom_call_target="tpu_custom_call" | custom-call | tf_op jit(solution)/shard_map/last/pallas_call | solution.py:157
  18.1 1.6 %collective-permute-start.8 = (f32[1,2048]{1,0:T(1,128)S(1)}, f32[1,2048]{1,0:T(1,128)S(1)}, u32[]{:S(2)}, u32[]{:S(2)}) collective-permute-start(f32[1,2048]{1,0:T(1,128)S(1)} %get-tuple-element.32.refs_0_), channel_id=1, source_target_pairs={{0,4},{1,5},{2,6},{3,7},{4,0},{5,1},{6,2},{7,3},{8,12},{9,13},{10,... | collective-permute-start | bytes 24584 | tf_op jit(solution)/shard_map/ppermute | solution.py:295
  19.7 0.0 collective-permute-start.6
  19.7 0.2 collective-permute-done.7.refs_2_
  19.9 2.8 %collective-permute-done.8.refs_2_ = f32[1,2048]{1,0:T(1,128)S(1)} collective-permute-done((f32[1,2048]{1,0:T(1,128)S(1)}, f32[1,2048]{1,0:T(1,128)S(1)}, u32[]{:S(2)}, u32[]{:S(2)}) %collective-permute-start.8) | collective-permute-done | bytes 8224 | tf_op jit(solution)/shard_map/ppermute | solution.py:295
  22.7 0.5 %collective-permute-start.10 = (f32[1,2048]{1,0:T(1,128)S(1)}, f32[1,2048]{1,0:T(1,128)S(1)}, u32[]{:S(2)}, u32[]{:S(2)}) collective-permute-start(f32[1,2048]{1,0:T(1,128)S(1)} %get-tuple-element.32.refs_0_), channel_id=1, source_target_pairs={{0,8},{8,0},{1,9},{9,1},{2,10},{10,2},{3,11},{11,3},{4,12},{12,4},... | collective-permute-start | bytes 24584 | tf_op jit(solution)/shard_map/ppermute | solution.py:298
  23.2 0.0 collective-permute-start.11
  23.2 0.7 %collective-permute-done.9.refs_3_ = bf16[64,512]{1,0:T(8,128)(2,1)S(1)} collective-permute-done((bf16[64,512]{1,0:T(8,128)(2,1)S(1)}, bf16[64,512]{1,0:T(8,128)(2,1)S(1)}, u32[]{:S(2)}, u32[]{:S(2)}) %collective-permute-start.9) | collective-permute-done | bytes 65568 | tf_op jit(solution)/shard_map/ppermute | solution.py:298
  24.0 0.0 collective-permute-done.10.refs_1_
  24.0 0.3 collective-permute-done.11.refs_3_
  24.4 2.0 %give.1 = (bf16[80,512]{1,0:T(8,128)(2,1)S(1)}, bf16[80,512]{1,0:T(8,128)(2,1)S(1)}, bf16[80,512]{1,0:T(8,128)(2,1)S(1)}, f32[1,2048]{1,0:T(1,128)S(1)}, f32[1,512]{1,0:T(1,128)S(1)}) custom-call(f32[1536,1536]{1,0:T(8,128)S(1)} %get-tuple-element.24.k_near.refs_0_, f32[512,1536]{1,0:T(8,128)S(1)} %get-tuple-element.34.k_last, ...), custom_call_target="tpu_custom_call" | custom-call | tf_op jit(solution)/shard_map/give/pallas_call | solution.py:157
  26.3 2.4 %collective-permute-start.12 = (bf16[80,512]{1,0:T(8,128)(2,1)S(1)}, bf16[80,512]{1,0:T(8,128)(2,1)S(1)}, u32[]{:S(2)}, u32[]{:S(2)}) collective-permute-start(bf16[80,512]{1,0:T(8,128)(2,1)S(1)} %get-tuple-element.38), channel_id=1, source_target_pairs={{0,3},{1,2},{2,1},{3,0},{4,7},{5,6},{6,5},{7,4},{8,11},{9,10},{10,... | collective-permute-start | bytes 245768 | tf_op jit(solution)/shard_map/ppermute | solution.py:295
  28.8 0.7 %collective-permute-start.13 = (bf16[80,512]{1,0:T(8,128)(2,1)S(1)}, bf16[80,512]{1,0:T(8,128)(2,1)S(1)}, u32[]{:S(2)}, u32[]{:S(2)}) collective-permute-start(bf16[80,512]{1,0:T(8,128)(2,1)S(1)} %get-tuple-element.39), channel_id=1, source_target_pairs={{0,2},{1,3},{2,0},{3,1},{4,6},{5,7},{6,4},{7,5},{8,10},{9,11},{10,... | collective-permute-start | bytes 245768 | tf_op jit(solution)/shard_map/ppermute | solution.py:295
  29.5 0.8 %collective-permute-start.14 = (bf16[80,512]{1,0:T(8,128)(2,1)S(1)}, bf16[80,512]{1,0:T(8,128)(2,1)S(1)}, u32[]{:S(2)}, u32[]{:S(2)}) collective-permute-start(bf16[80,512]{1,0:T(8,128)(2,1)S(1)} %get-tuple-element.40), channel_id=1, source_target_pairs={{0,1},{1,0},{2,3},{3,2},{4,5},{5,4},{6,7},{7,6},{8,9},{9,8},{10,11... | collective-permute-start | bytes 245768 | tf_op jit(solution)/shard_map/ppermute | solution.py:295
  30.3 1.3 %keep.1 = (f32[72,512]{1,0:T(8,128)S(1)}, f32[1,512]{1,0:T(1,128)}) custom-call(f32[1536,1536]{1,0:T(8,128)S(1)} %get-tuple-element.24.k_near.refs_0_, f32[2048,512]{1,0:T(8,128)S(1)} %get-tuple-element.29.k_side.refs_1_, bf16[128,2048]{1,0:T(8,128)(2,1)S(1)} %vectors.1.vec_all.refs_2_, f32[1,2048]{1,0:T(1,128)S(1)} %get-tuple-element.35.refs_3_, ...), custom_call_target="tpu_custom_call" | custom-call | tf_op jit(solution)/shard_map/keep/pallas_call | solution.py:157
  31.5 0.3 collective-permute-done.12.refs_0_
  31.8 1.9 %collective-permute-done.13.refs_1_ = bf16[80,512]{1,0:T(8,128)(2,1)S(1)} collective-permute-done((bf16[80,512]{1,0:T(8,128)(2,1)S(1)}, bf16[80,512]{1,0:T(8,128)(2,1)S(1)}, u32[]{:S(2)}, u32[]{:S(2)}) %collective-permute-start.13) | collective-permute-done | bytes 81952 | tf_op jit(solution)/shard_map/ppermute | solution.py:295
  33.7 0.2 collective-permute-done.14.refs_2_
  33.9 0.7 %finish.1 = f32[64,512]{1,0:T(8,128)} custom-call(f32[72,512]{1,0:T(8,128)S(1)} %get-tuple-element.37.near_ref, bf16[80,512]{1,0:T(8,128)(2,1)S(1)} %collective-permute-done.12.refs_0_, bf16[80,512]{1,0:T(8,128)(2,1)S(1)} %collective-permute-done.13.refs_1_, bf16[80,512]{1,0:T(8,128)(2,1)S(1)} %collective-permute-done.14.refs_2_), custom_call_target="tpu_custom_call" | custom-call | tf_op jit(solution)/shard_map/finish/pallas_call | solution.py:157
  (9 shorter events, 0.1 us)
Async XLA Ops:
  0.6 10.7 %collective-permute-start.3 = (bf16[512,128]{1,0:T(8,128)(2,1)}, bf16[512,128]{1,0:T(8,128)(2,1)S(1)}, u32[]{:S(2)}, u32[]{:S(2)}) collective-permute-start(bf16[512,128]{1,0:T(8,128)(2,1)} %points_ref.1), channel_id=1, source_target_pairs={{0,4},{1,5},{2,6},{3,7},{4,0},{5,1},{6,2},{7,3},{8,12},{9,13},{10,... | collective-permute-start | bytes 393224 | tf_op jit(solution)/shard_map/ppermute | solution.py:295
  4.7 6.8 %collective-permute-start.1 = (bf16[512,128]{1,0:T(8,128)(2,1)}, bf16[512,128]{1,0:T(8,128)(2,1)S(1)}, u32[]{:S(2)}, u32[]{:S(2)}) collective-permute-start(bf16[512,128]{1,0:T(8,128)(2,1)} %points_ref.1), channel_id=1, source_target_pairs={{0,2},{1,3},{2,0},{3,1},{4,6},{5,7},{6,4},{7,5},{8,10},{9,11},{10,... | collective-permute-start | bytes 393224 | tf_op jit(solution)/shard_map/ppermute | solution.py:295
  6.3 8.1 %collective-permute-start = (bf16[512,128]{1,0:T(8,128)(2,1)}, bf16[512,128]{1,0:T(8,128)(2,1)S(1)}, u32[]{:S(2)}, u32[]{:S(2)}) collective-permute-start(bf16[512,128]{1,0:T(8,128)(2,1)} %points_ref.1), channel_id=1, source_target_pairs={{0,1},{1,0},{2,3},{3,2},{4,5},{5,4},{6,7},{7,6},{8,9},{9,8},{10,11... | collective-permute-start | bytes 393224 | tf_op jit(solution)/shard_map/ppermute | solution.py:295
  7.8 6.6 %collective-permute-start.2 = (bf16[512,128]{1,0:T(8,128)(2,1)}, bf16[512,128]{1,0:T(8,128)(2,1)S(1)}, u32[]{:S(2)}, u32[]{:S(2)}) collective-permute-start(bf16[512,128]{1,0:T(8,128)(2,1)} %points_ref.1), channel_id=1, source_target_pairs={{0,8},{8,0},{1,9},{9,1},{2,10},{10,2},{3,11},{11,3},{4,12},{12,4},... | collective-permute-start | bytes 393224 | tf_op jit(solution)/shard_map/ppermute | solution.py:298
  7.8 0.9 %copy-start = (bf16[512,128]{1,0:T(8,128)(2,1)S(1)}, bf16[512,128]{1,0:T(8,128)(2,1)}, u32[]{:S(2)}) copy-start(bf16[512,128]{1,0:T(8,128)(2,1)} %points_ref.1) | copy-start | bytes 393220
  8.8 0.8 %copy-start.1 = (bf16[512,64]{0,1:T(8,128)(2,1)S(1)}, bf16[512,64]{0,1:T(8,128)(2,1)}, u32[]{:S(2)}) copy-start(bf16[512,64]{0,1:T(8,128)(2,1)} %param.3) | copy-start | bytes 196612
  11.6 5.0 %collective-permute-start.4 = (bf16[512,128]{1,0:T(8,128)(2,1)S(1)}, bf16[512,128]{1,0:T(8,128)(2,1)S(1)}, u32[]{:S(2)}, u32[]{:S(2)}) collective-permute-start(bf16[512,128]{1,0:T(8,128)(2,1)S(1)} %collective-permute-done.1.refs_1_), channel_id=1, source_target_pairs={{0,1},{1,0},{2,3},{3,2},{4,5},{5,4},{6,7},{7,6},{8,9},{9,8},{10,11... | collective-permute-start | bytes 393224 | tf_op jit(solution)/shard_map/ppermute | solution.py:295
  13.1 3.4 %collective-permute-start.5 = (bf16[512,128]{1,0:T(8,128)(2,1)S(1)}, bf16[512,128]{1,0:T(8,128)(2,1)S(1)}, u32[]{:S(2)}, u32[]{:S(2)}) collective-permute-start(bf16[512,128]{1,0:T(8,128)(2,1)S(1)} %collective-permute-done.3.refs_4_), channel_id=1, source_target_pairs={{0,8},{8,0},{1,9},{9,1},{2,10},{10,2},{3,11},{11,3},{4,12},{12,4},... | collective-permute-start | bytes 393224 | tf_op jit(solution)/shard_map/ppermute | solution.py:298
  13.1 6.8 %collective-permute-start.7 = (bf16[64,512]{1,0:T(8,128)(2,1)S(1)}, bf16[64,512]{1,0:T(8,128)(2,1)S(1)}, u32[]{:S(2)}, u32[]{:S(2)}) collective-permute-start(bf16[64,512]{1,0:T(8,128)(2,1)S(1)} %bitcast.4), channel_id=1, source_target_pairs={{0,4},{1,5},{2,6},{3,7},{4,0},{5,1},{6,2},{7,3},{8,12},{9,13},{10,... | collective-permute-start | bytes 196616 | tf_op jit(solution)/shard_map/ppermute | solution.py:295
  18.1 4.6 %collective-permute-start.8 = (f32[1,2048]{1,0:T(1,128)S(1)}, f32[1,2048]{1,0:T(1,128)S(1)}, u32[]{:S(2)}, u32[]{:S(2)}) collective-permute-start(f32[1,2048]{1,0:T(1,128)S(1)} %get-tuple-element.32.refs_0_), channel_id=1, source_target_pairs={{0,4},{1,5},{2,6},{3,7},{4,0},{5,1},{6,2},{7,3},{8,12},{9,13},{10,... | collective-permute-start | bytes 24584 | tf_op jit(solution)/shard_map/ppermute | solution.py:295
  19.7 3.5 %collective-permute-start.6 = (bf16[64,512]{1,0:T(8,128)(2,1)S(1)}, bf16[64,512]{1,0:T(8,128)(2,1)S(1)}, u32[]{:S(2)}, u32[]{:S(2)}) collective-permute-start(bf16[64,512]{1,0:T(8,128)(2,1)S(1)} %bitcast.5), channel_id=1, source_target_pairs={{0,8},{8,0},{1,9},{9,1},{2,10},{10,2},{3,11},{11,3},{4,12},{12,4},... | collective-permute-start | bytes 196616 | tf_op jit(solution)/shard_map/ppermute | solution.py:298
  22.7 1.3 %collective-permute-start.9 = (bf16[64,512]{1,0:T(8,128)(2,1)S(1)}, bf16[64,512]{1,0:T(8,128)(2,1)S(1)}, u32[]{:S(2)}, u32[]{:S(2)}) collective-permute-start(bf16[64,512]{1,0:T(8,128)(2,1)S(1)} %collective-permute-done.7.refs_2_), channel_id=1, source_target_pairs={{0,8},{8,0},{1,9},{9,1},{2,10},{10,2},{3,11},{11,3},{4,12},{12,4},... | collective-permute-start | bytes 196616 | tf_op jit(solution)/shard_map/ppermute | solution.py:298
  22.7 1.3 %collective-permute-start.10 = (f32[1,2048]{1,0:T(1,128)S(1)}, f32[1,2048]{1,0:T(1,128)S(1)}, u32[]{:S(2)}, u32[]{:S(2)}) collective-permute-start(f32[1,2048]{1,0:T(1,128)S(1)} %get-tuple-element.32.refs_0_), channel_id=1, source_target_pairs={{0,8},{8,0},{1,9},{9,1},{2,10},{10,2},{3,11},{11,3},{4,12},{12,4},... | collective-permute-start | bytes 24584 | tf_op jit(solution)/shard_map/ppermute | solution.py:298
  23.2 1.2 %collective-permute-start.11 = (f32[1,2048]{1,0:T(1,128)S(1)}, f32[1,2048]{1,0:T(1,128)S(1)}, u32[]{:S(2)}, u32[]{:S(2)}) collective-permute-start(f32[1,2048]{1,0:T(1,128)S(1)} %collective-permute-done.8.refs_2_), channel_id=1, source_target_pairs={{0,8},{8,0},{1,9},{9,1},{2,10},{10,2},{3,11},{11,3},{4,12},{12,4},... | collective-permute-start | bytes 24584 | tf_op jit(solution)/shard_map/ppermute | solution.py:298
  26.3 5.5 %collective-permute-start.12 = (bf16[80,512]{1,0:T(8,128)(2,1)S(1)}, bf16[80,512]{1,0:T(8,128)(2,1)S(1)}, u32[]{:S(2)}, u32[]{:S(2)}) collective-permute-start(bf16[80,512]{1,0:T(8,128)(2,1)S(1)} %get-tuple-element.38), channel_id=1, source_target_pairs={{0,3},{1,2},{2,1},{3,0},{4,7},{5,6},{6,5},{7,4},{8,11},{9,10},{10,... | collective-permute-start | bytes 245768 | tf_op jit(solution)/shard_map/ppermute | solution.py:295
  28.8 4.9 %collective-permute-start.13 = (bf16[80,512]{1,0:T(8,128)(2,1)S(1)}, bf16[80,512]{1,0:T(8,128)(2,1)S(1)}, u32[]{:S(2)}, u32[]{:S(2)}) collective-permute-start(bf16[80,512]{1,0:T(8,128)(2,1)S(1)} %get-tuple-element.39), channel_id=1, source_target_pairs={{0,2},{1,3},{2,0},{3,1},{4,6},{5,7},{6,4},{7,5},{8,10},{9,11},{10,... | collective-permute-start | bytes 245768 | tf_op jit(solution)/shard_map/ppermute | solution.py:295
  29.5 4.4 %collective-permute-start.14 = (bf16[80,512]{1,0:T(8,128)(2,1)S(1)}, bf16[80,512]{1,0:T(8,128)(2,1)S(1)}, u32[]{:S(2)}, u32[]{:S(2)}) collective-permute-start(bf16[80,512]{1,0:T(8,128)(2,1)S(1)} %get-tuple-element.40), channel_id=1, source_target_pairs={{0,1},{1,0},{2,3},{3,2},{4,5},{5,4},{6,7},{7,6},{8,9},{9,8},{10,11... | collective-permute-start | bytes 245768 | tf_op jit(solution)/shard_map/ppermute | solution.py:295
